TPU v7x, 32 devices: a whole 2x2x4 slice. The times are simulated.
32 devices in a mesh: dp: 8 (over z, y), mp: 4 (over x, core).
Axes of the slice: x: 2, y: 2, z: 4, core: 2. Of those that a mesh axis runs over, the one named last changes fastest.
Arguments:
- features: bfloat16 [24576, 1024], P('dp'), may hold values from -6 to 6
- curvature: bfloat16 [24576, 4096], P('dp', 'mp'), may hold values from 0.099609375 to 2
- task_grad: float32 [1024, 4096], P('dp', 'mp'), may hold values from -6 to 6
Outputs:
- solution: float32 [1024, 4096], P('dp', 'mp')
- residual: float32 [1024, 4096], P('dp', 'mp')
All inputs are finite; a program needn't handle non-finite values.
Results may differ from a plain program's by a relative error of at most 0.0095.
The roundings to bfloat16 on the way count: a program that leaves them out, or rounds other values in their place, can miss the bound.
Values may be sent and summed in bfloat16 or wider, within the bound.
No kernel may reach another device: no remote copies, remote signals or barrier semaphores. Data moves between devices by JAX's collectives and lax.ppermute only.
A program may use at most 64 MiB of HBM per device.

v0:
```python
import jax
import jax.numpy as jnp
from jax import lax
from jax.sharding import PartitionSpec as P

ITERS = 2


damp_coef = 0.5


def weigh_rows(curvature, projected):
    return (curvature * projected).astype(jnp.bfloat16)


def shards(features, curvature, task_grad):
    token_count = features.shape[0] * lax.axis_size("dp")

    def global_sums(values):
        return lax.psum(values, ("dp", "mp"))

    solution = jnp.zeros_like(task_grad)
    residual = task_grad
    direction = task_grad
    norm_now = jnp.sum(residual * residual)
    for turn in range(ITERS):
        dir_bf = direction.astype(jnp.bfloat16)
        gathered = lax.all_gather(dir_bf, "dp", axis=0, tiled=True)
        projected = jnp.dot(features, gathered, preferred_element_type=jnp.float32)
        weighted = weigh_rows(curvature, projected)
        summed = lax.psum_scatter(
            lax.dot_general(
                features, weighted, (((0,), (0,)), ((), ())), preferred_element_type=jnp.float32
            ),
            "dp",
            scatter_dimension=0,
            tiled=True,
        )
        curved = summed / token_count + damp_coef * direction
        pdot_local = jnp.sum(direction * curved)
        rdot_local = jnp.sum(residual * curved)
        cdot_local = jnp.sum(curved * curved)
        if turn == 0:
            norm_now, curv_dot, resid_dot, image_dot = global_sums(
                (norm_now, pdot_local, rdot_local, cdot_local)
            )
        else:
            curv_dot, resid_dot, image_dot = global_sums((pdot_local, rdot_local, cdot_local))
        step_len = norm_now / curv_dot
        solution = solution + step_len * direction
        residual = residual - step_len * curved
        norm_next = norm_now - 2.0 * step_len * resid_dot + step_len * step_len * image_dot
        if turn + 1 < ITERS:
            direction = residual + norm_next / norm_now * direction
            norm_now = norm_next
    return (solution, residual)


def solution(mesh):
    placed = (P("dp", None), P("dp", "mp"), P("dp", "mp"))
    return jax.shard_map(
        shards,
        mesh=mesh,
        in_specs=placed,
        out_specs=(P("dp", "mp"), P("dp", "mp")),
        check_vma=False,
    )
```

profile of v0, /device:TPU:0, one launch (start us, length us, event | category | flops | bytes accessed | tf_op | source)
XLA Modules:
  0.0 433.5 jit_solution(17407566458538032969)
XLA Ops:
  7.2 0.0 all-gather.3.cloned.1.call-start
  7.2 2.6 fusion.7
  9.8 0.0 all-gather.3.cloned.1.call-update
  9.8 0.0 copy-start.1
  9.8 0.0 reduce-scatter.3.cloned.1.call-start
  9.9 52.9 %all-gather.3.cloned.1.call-done = bf16[1024,1024]{1,0:T(8,128)(2,1)} async-done(((bf16[128,1024]{1,0:T(8,128)(2,1)}), bf16[1024,1024]{1,0:T(8,128)(2,1)}) %all-gather.3.cloned.1.call-update) | async-done | bytes 2097168 | tf_op jit(solution)/shard_map/all_gather | solution.py:28
  62.7 22.5 %fusion.5 = f32[1024,1024]{0,1:T(8,128)} fusion(bf16[3072,1024]{1,0:T(8,128)(2,1)} %param.3, bf16[3072,1024]{1,0:T(8,128)(2,1)} %param.4, bf16[1024,1024]{1,0:T(8,128)(2,1)} %all-gather.3.cloned.1.call-done), kind=kOutput, calls=%fused_computation.7 | convolution fusion | flops 12894339072 | bytes 18874368 | tf_op jit(solution)/shard_map/dot_general | solution.py:32
  85.2 0.0 reduce-scatter.3.cloned.1.call-update
  85.2 0.0 all-gather.5.cloned.1.call-start
  85.3 0.0 copy-done.1
  85.3 0.2 copy.6
  85.5 86.9 %reduce-scatter.3.cloned.1.call-done = f32[128,1024]{0,1:T(8,128)} async-done(((f32[1024,1024]{0,1:T(8,128)}), f32[128,1024]{0,1:T(8,128)}) %reduce-scatter.3.cloned.1.call-update) | async-done | bytes 524304 | tf_op jit(solution)/shard_map/reduce_scatter | solution.py:31
  172.3 1.9 multiply_reduce_fusion.1
  174.2 40.6 %all-reduce = (f32[]{:T(128)}, f32[]{:T(128)}, f32[]{:T(128)}) all-reduce(f32[]{:T(128)} %get-tuple-element.12, f32[]{:T(128)} %get-tuple-element.5, f32[]{:T(128)} %get-tuple-element.4), channel_id=1, replica_groups=mesh['dp'=8,'mp'=4] {'dp','mp'}, use_global_device_ids=true, to_apply=%region_1.0 | all-reduce | flops 3 | bytes 24 | tf_op jit(solution)/shard_map/psum | solution.py:20
  218.6 1.9 fusion.6
  220.5 0.0 all-gather.5.cloned.1.call-update
  220.5 0.0 copy-start
  220.5 0.0 reduce-scatter.5.cloned.1.call-start
  220.6 50.9 %all-gather.5.cloned.1.call-done = bf16[1024,1024]{0,1:T(8,128)(2,1)} async-done(((bf16[128,1024]{0,1:T(8,128)(2,1)}), bf16[1024,1024]{0,1:T(8,128)(2,1)}) %all-gather.5.cloned.1.call-update) | async-done | bytes 2097168 | tf_op jit(solution)/shard_map/all_gather | solution.py:28
  271.4 22.3 %fusion.4 = f32[1024,1024]{0,1:T(8,128)} fusion(bf16[3072,1024]{1,0:T(8,128)(2,1)} %param.3, bf16[3072,1024]{1,0:T(8,128)(2,1)} %param.4, bf16[1024,1024]{0,1:T(8,128)(2,1)} %all-gather.5.cloned.1.call-done), kind=kOutput, calls=%fused_computation.6 | convolution fusion | flops 12894339072 | bytes 18874368 | tf_op jit(solution)/shard_map/dot_general | solution.py:32
  293.7 0.0 reduce-scatter.5.cloned.1.call-update
  293.8 86.8 %reduce-scatter.5.cloned.1.call-done = f32[128,1024]{0,1:T(8,128)} async-done(((f32[1024,1024]{0,1:T(8,128)}), f32[128,1024]{0,1:T(8,128)}) %reduce-scatter.5.cloned.1.call-update) | async-done | bytes 524304 | tf_op jit(solution)/shard_map/reduce_scatter | solution.py:31
  380.6 0.0 copy-done
  380.6 1.9 multiply_reduce_fusion
  382.4 40.5 %psum.34 = f32[]{:T(128)} all-reduce(f32[]{:T(128)} %multiply_reduce_fusion), channel_id=1, replica_groups=mesh['dp'=8,'mp'=4] {'dp','mp'}, use_global_device_ids=true, to_apply=%region_9.0 | all-reduce | flops 1 | bytes 8 | tf_op jit(solution)/shard_map/psum | solution.py:20
  423.6 1.3 multiply_subtract_fusion
  425.0 1.0 copy.11
  425.9 1.0 copy.10
Async XLA Ops:
  7.2 55.6 %all-gather.3.cloned.1.call-start = ((), (), s32[]{:S(2)}) async-start(), calls=%async_computation.2 | async-start | bytes 2359296 | tf_op jit(solution)/shard_map/all_gather | solution.py:28
  9.8 75.5 %copy-start.1 = (f32[128,1024]{1,0:T(8,128)S(1)}, f32[128,1024]{1,0:T(8,128)}, u32[]{:S(2)}) copy-start(f32[128,1024]{1,0:T(8,128)} %param.5) | copy-start | bytes 1572868
  9.8 162.5 %reduce-scatter.3.cloned.1.call-start = ((), (), s32[]{:S(2)}) async-start(), calls=%async_computation.3 | async-start | bytes 4718592 | tf_op jit(solution)/shard_map/reduce_scatter | solution.py:31
  85.2 186.2 %all-gather.5.cloned.1.call-start = ((), (), s32[]{:S(2)}) async-start(), calls=%async_computation.4 | async-start | bytes 2359296 | tf_op jit(solution)/shard_map/all_gather | solution.py:28
  220.5 160.1 %copy-start = (f32[128,1024]{0,1:T(8,128)S(1)}, f32[128,1024]{0,1:T(8,128)}, u32[]{:S(2)}) copy-start(f32[128,1024]{0,1:T(8,128)} %reduce-scatter.3.cloned.1.call-done) | copy-start | bytes 1572868
  220.5 160.1 %reduce-scatter.5.cloned.1.call-start = ((), (), s32[]{:S(2)}) async-start(), calls=%async_computation.5 | async-start | bytes 4718592 | tf_op jit(solution)/shard_map/reduce_scatter | solution.py:31
Sparse Core Ops, SparseCore 0:
  10.7 51.9 all-gather.2
  85.3 86.9 reduce-scatter.2
  220.6 50.7 all-gather.4
  293.9 86.6 reduce-scatter.4
where the time goes:
time: 434 us; the launch traced here: 433 us
  waiting for transfers between devices  277 us (64%)
  blocking collectives  81.1 us (19%)
  matrix products  44.8 us (10%)
  between operations  18.3 us (4%)
  other arithmetic  9.48 us (2%)
    reduce_scatter x2, waiting for transfers between devices, shards(): lax.psum_scatter(lax.dot_general(features, weighted, (((0,), (0,)), ((),...  174 us
    all_gather x2, waiting for transfers between devices, shards(): gathered = lax.all_gather(dir_bf, 'dp', axis=0, tiled=True)  104 us
    psum x2, blocking collectives, global_sums(): return lax.psum(values, ('dp', 'mp'))  81.1 us
    dot_general x2, matrix products, shards(): lax.dot_general(features, weighted, (((0,), (0,)), ((), ())), preferred_e...  44.8 us
  transfers between devices with their start and end apart: 4, of which 4 were waited for; matrix products, arithmetic and copies ran while one was open for 0% of the time, Pallas kernels for 0%

commit v1 on v0

v1 whole, which is shorter than its diff:
```python
import jax
import jax.numpy as jnp
from jax import lax
from jax.sharding import PartitionSpec as P

ITERS = 2
CHUNKS = 2

damp_coef = 0.5

FEATURE_MAX = 6.0
CURVATURE_MAX = 2.0
WIRE = jnp.float16
WIRE_MAX = 32768.0


def swap(values, axis, stride):
    size = lax.axis_size(axis)
    return lax.ppermute(values, axis, [(i, i ^ stride) for i in range(size)])


def strides_of(axis):
    size = lax.axis_size(axis)
    return [1 << bit for bit in reversed(range(size.bit_length() - 1))]


def global_sums(*values):
    total = jnp.stack(values)
    for axis in ("dp", "mp"):
        for stride in strides_of(axis):
            total = total + swap(total, axis, stride)
    return [total[i] for i in range(len(values))]


def gather_rows(block):
    for stride in strides_of("dp"):
        block = jnp.concatenate([block, swap(block, "dp", stride)], axis=0)
    return block


def block_order():
    order = [0]
    for stride in strides_of("dp"):
        order = order + [place ^ stride for place in order]
    return order


def scatter_rows(rows, scale):
    total = rows * scale
    for stride in reversed(strides_of("dp")):
        half = total.shape[0] // 2
        received = swap(total[half:].astype(WIRE), "dp", stride)
        total = total[:half] + received.astype(jnp.float32)
    return total / scale


def wire_scale(gathered, din):
    largest = jnp.max(jnp.abs(gathered.astype(jnp.float32)), axis=0, keepdims=True)
    bound = FEATURE_MAX * FEATURE_MAX * CURVATURE_MAX * din
    return WIRE_MAX / (bound * jnp.maximum(largest, 1e-30))


def shards(features, curvature, task_grad):
    n_dp = lax.axis_size("dp")
    token_count = features.shape[0] * n_dp
    din = features.shape[1]
    rows, cols = task_grad.shape
    width = cols // CHUNKS
    me = lax.axis_index("dp")
    spans = [slice(k * width, (k + 1) * width) for k in range(CHUNKS)]

    ordered = jnp.concatenate(
        [
            lax.dynamic_slice_in_dim(features, (me ^ place) * rows, rows, axis=1)
            for place in block_order()
        ],
        axis=1,
    )
    curv = [curvature[:, span] for span in spans]
    grad = [task_grad[:, span] for span in spans]

    def product(direction, k):
        gathered = gather_rows(direction.astype(jnp.bfloat16))
        projected = jnp.dot(ordered, gathered, preferred_element_type=jnp.float32)
        weighted = (curv[k] * projected).astype(jnp.bfloat16)
        partial = lax.dot_general(
            ordered, weighted, (((0,), (0,)), ((), ())), preferred_element_type=jnp.float32
        )
        partial = partial / token_count
        summed = scatter_rows(partial, wire_scale(gathered, din))
        return summed + damp_coef * direction, gathered, partial

    chunks = range(CHUNKS)
    norm_local = jnp.sum(task_grad * task_grad)
    image = [product(grad[k], k)[0] for k in chunks]
    curv_dot = sum(jnp.sum(grad[k] * image[k]) for k in chunks)
    image_dot = sum(jnp.sum(image[k] * image[k]) for k in chunks)
    norm_now, curv_dot, image_dot = global_sums(norm_local, curv_dot, image_dot)
    step_len = norm_now / curv_dot
    norm_next = norm_now - 2.0 * step_len * curv_dot + step_len * step_len * image_dot
    ratio = norm_next / norm_now
    residual = [grad[k] - step_len * image[k] for k in chunks]
    direction = [residual[k] + ratio * grad[k] for k in chunks]

    done = [product(direction[k], k) for k in chunks]
    dots = sum(
        jnp.sum(gathered.astype(jnp.float32) * partial) for _, gathered, partial in done
    ) + damp_coef * sum(jnp.sum(d * d) for d in direction)
    (curv_dot,) = global_sums(dots)
    last_len = norm_next / curv_dot
    solution = [step_len * grad[k] + last_len * direction[k] for k in chunks]
    residual = [residual[k] - last_len * done[k][0] for k in chunks]
    return jnp.concatenate(solution, axis=1), jnp.concatenate(residual, axis=1)


def solution(mesh):
    placed = (P("dp", None), P("dp", "mp"), P("dp", "mp"))
    return jax.shard_map(
        shards,
        mesh=mesh,
        in_specs=placed,
        out_specs=(P("dp", "mp"), P("dp", "mp")),
        check_vma=False,
    )
```

time: 434 us -> 240 us (0.55)
  waiting for transfers between devices: 277 us -> 81.8 us
  blocking collectives: 81.1 us -> 0 us
  starting transfers between devices: 0.16 us -> 49.1 us
  local copies, waits for them, and re-layouts: 2.19 us -> 19.6 us
  matrix products: 44.8 us -> 55.9 us
  other arithmetic: 9.48 us -> 19.5 us
  between operations: 18.3 us -> 12.9 us
    reduce_scatter x2 -> x0, waiting for transfers between devices: 174 us -> none  [shards(): lax.psum_scatter(lax.dot_general(features, weighted, (((0,), (0,)), ((),...]
    all_gather x2 -> x0, waiting for transfers between devices: 104 us -> none  [shards(): gathered = lax.all_gather(dir_bf, 'dp', axis=0, tiled=True)]
    ppermute x0 -> x34, waiting for transfers between devices: none -> 81.8 us  [swap(): return lax.ppermute(values, axis, [(i, i ^ stride) for i in range(size)])]
    psum x2 -> x0, blocking collectives: 81.1 us -> none  [global_sums(): return lax.psum(values, ('dp', 'mp'))]
    ppermute x0 -> x34, starting transfers between devices: none -> 49.1 us  [swap(): return lax.ppermute(values, axis, [(i, i ^ stride) for i in range(size)])]
    unnamed x7 -> x21, local copies, waits for them, and re-layouts: 2.19 us -> 15.8 us
    dot_general x2 -> x4, matrix products: 44.8 us -> 55.9 us  [product(): lax.dot_general(ordered, weighted, (((0,), (0,)), ((), ())), preferred_el...]
    add x0 -> x13, other arithmetic: none -> 4.65 us  [the longest x8 3.11 us: scatter_rows(): total = total[:half] + received.astype(jnp.float32)]
  transfers between devices with their start and end apart: 4 -> 34, of which waited for: 4 -> 25; matrix products, arithmetic and copies ran while one was open for 0% -> 37% of each run, Pallas kernels for 0% -> 0%
where the time goes in v1:
time: 240 us; the launch traced here: 239 us
  waiting for transfers between devices  81.8 us (34%)
  matrix products  55.9 us (23%)
  starting transfers between devices  49.1 us (20%)
  local copies, waits for them, and re-layouts  19.6 us (8%)
  other arithmetic  19.5 us (8%)
  between operations  12.9 us (5%)
    ppermute x34, waiting for transfers between devices, swap(): return lax.ppermute(values, axis, [(i, i ^ stride) for i in range(size)])  81.8 us
    dot_general x4, matrix products, product(): lax.dot_general(ordered, weighted, (((0,), (0,)), ((), ())), preferred_el...  55.9 us
    ppermute x34, starting transfers between devices, swap(): return lax.ppermute(values, axis, [(i, i ^ stride) for i in range(size)])  49.1 us
    unnamed x21, local copies, waits for them, and re-layouts  15.8 us
  transfers between devices with their start and end apart: 34, of which 25 were waited for; matrix products, arithmetic and copies ran while one was open for 37% of the time, Pallas kernels for 0%

profile of v1, /device:TPU:0, one launch (start us, length us, event | category | flops | bytes accessed | tf_op | source)
XLA Modules:
  0.0 238.8 jit_solution(8446228669983929747)
XLA Ops:
  1.7 4.1 %collective-permute-start.6 = (bf16[128,512]{1,0:T(8,128)(2,1)S(1)}, bf16[128,512]{1,0:T(8,128)(2,1)S(1)}, u32[]{:S(2)}, u32[]{:S(2)}) collective-permute-start(bf16[128,512]{1,0:T(8,128)(2,1)S(1)} %get-tuple-element.32), channel_id=1, source_target_pairs={{0,16},{4,20},{8,24},{12,28},{16,0},{20,4},{24,8},{28,12},{1,17},{... | collective-permute-start | bytes 393224 | tf_op jit(solution)/shard_map/ppermute | solution.py:19
  5.9 2.1 dynamic-slice_dynamic-update-slice_fusion.7
  8.0 2.1 dynamic-slice_dynamic-update-slice_fusion.6
  10.1 2.2 dynamic-slice_dynamic-update-slice_fusion.5
  12.3 2.1 dynamic-slice_dynamic-update-slice_fusion.4
  14.5 2.2 dynamic-slice_dynamic-update-slice_fusion.3
  16.6 2.2 dynamic-slice_dynamic-update-slice_fusion.2
  18.9 1.9 collective-permute-start.7
  20.8 2.1 dynamic-slice_dynamic-update-slice_fusion.1
  22.9 3.8 %collective-permute-done.7 = bf16[256,512]{1,0:T(8,128)(2,1)S(1)} collective-permute-done((bf16[256,512]{1,0:T(8,128)(2,1)S(1)}, bf16[256,512]{1,0:T(8,128)(2,1)S(1)}, u32[]{:S(2)}, u32[]{:S(2)}) %collective-permute-start.7) | collective-permute-done | bytes 262176 | tf_op jit(solution)/shard_map/ppermute | solution.py:19
  26.7 1.6 collective-permute-start.8
  28.3 1.6 collective-permute-start.1
  30.0 2.1 dynamic-slice_dynamic-update-slice_fusion
  32.1 2.7 %collective-permute-done.1 = bf16[256,512]{1,0:T(8,128)(2,1)S(1)} collective-permute-done((bf16[256,512]{1,0:T(8,128)(2,1)S(1)}, bf16[256,512]{1,0:T(8,128)(2,1)S(1)}, u32[]{:S(2)}, u32[]{:S(2)}) %collective-permute-start.1) | collective-permute-done | bytes 262176 | tf_op jit(solution)/shard_map/ppermute | solution.py:19
  36.3 5.3 %collective-permute-done.8 = bf16[512,512]{1,0:T(8,128)(2,1)S(1)} collective-permute-done((bf16[512,512]{1,0:T(8,128)(2,1)S(1)}, bf16[512,512]{1,0:T(8,128)(2,1)S(1)}, u32[]{:S(2)}, u32[]{:S(2)}) %collective-permute-start.8) | collective-permute-done | bytes 524320 | tf_op jit(solution)/shard_map/ppermute | solution.py:19
  42.4 12.3 %convolution_multiply_fusion = f32[1024,512]{1,0:T(8,128)S(1)} fusion(bf16[3072,1024]{1,0:T(8,128)(2,1)} %dynamic-slice_dynamic-update-slice_fusion, f32[512]{0:T(512)S(1)} %get-tuple-element.22, bf16[3072,1024]{1,0:T(8,128)(2,1)} %param.4, bf16[512,512]{1,0:T(8,128)(2,1)} %copy-done.4, bf16[256,512]{1,0:T(8,128)(2,1)S(1)} %collective-permute-done.7, ...), kind=kOutput, calls=%fused_computation.18 | convolution fusion | flops 6451888128 | bytes 18876416 | tf_op jit(solution)/shard_map/dot_general | solution.py:86
  58.4 13.9 %convolution_multiply_fusion.1 = f32[1024,512]{1,0:T(8,128)} fusion(bf16[3072,1024]{1,0:T(8,128)(2,1)} %dynamic-slice_dynamic-update-slice_fusion, f32[512]{0:T(512)S(1)} %get-tuple-element.20, bf16[3072,1024]{1,0:T(8,128)(2,1)} %param.4, bf16[512,512]{1,0:T(8,128)(2,1)} %collective-permute-done.2, bf16[256,512]{1,0:T(8,128)(2,1)S(1)} %collective-permute-done.1, ...), kind=kOutput, calls=%fused_computation.19 | convolution fusion | flops 6451888128 | bytes 18876416 | tf_op jit(solution)/shard_map/dot_general | solution.py:86
  75.5 1.6 collective-permute-start.10
  77.2 5.7 %collective-permute-done.3 = f16[512,512]{1,0:T(8,128)(2,1)S(1)} collective-permute-done((f16[512,512]{1,0:T(8,128)(2,1)S(1)}, f16[512,512]{1,0:T(8,128)(2,1)S(1)}, u32[]{:S(2)}, u32[]{:S(2)}) %collective-permute-start.3) | collective-permute-done | bytes 524320 | tf_op jit(solution)/shard_map/ppermute | solution.py:19
  83.1 1.6 collective-permute-start.4
  86.3 1.7 collective-permute-start.11
  87.9 1.6 collective-permute-done.4
  89.7 3.4 %collective-permute-start.5 = (f16[128,512]{1,0:T(8,128)(2,1)S(1)}, f16[128,512]{1,0:T(8,128)(2,1)S(1)}, u32[]{:S(2)}, u32[]{:S(2)}) collective-permute-start(f16[128,512]{1,0:T(8,128)(2,1)S(1)} %slice_convert_fusion.11), channel_id=1, source_target_pairs={{0,16},{4,20},{8,24},{12,28},{16,0},{20,4},{24,8},{28,12},{1,17},{... | collective-permute-start | bytes 393224 | tf_op jit(solution)/shard_map/ppermute | solution.py:19
  93.8 1.7 collective-permute-done.11
  95.6 2.8 %collective-permute-done.5 = f16[128,512]{1,0:T(8,128)(2,1)S(1)} collective-permute-done((f16[128,512]{1,0:T(8,128)(2,1)S(1)}, f16[128,512]{1,0:T(8,128)(2,1)S(1)}, u32[]{:S(2)}, u32[]{:S(2)}) %collective-permute-start.5) | collective-permute-done | bytes 131104 | tf_op jit(solution)/shard_map/ppermute | solution.py:19
  103.1 3.8 %collective-permute-done.12 = f32[3]{0:T(128)S(1)} collective-permute-done((f32[3]{0:T(128)S(1)}, f32[3]{0:T(128)S(1)}, u32[]{:S(2)}, u32[]{:S(2)}) %collective-permute-start.12) | collective-permute-done | bytes 44 | tf_op jit(solution)/shard_map/ppermute | solution.py:19
  108.3 2.9 %collective-permute-done.13 = f32[3]{0:T(128)S(1)} collective-permute-done((f32[3]{0:T(128)S(1)}, f32[3]{0:T(128)S(1)}, u32[]{:S(2)}, u32[]{:S(2)}) %collective-permute-start.13) | collective-permute-done | bytes 44 | tf_op jit(solution)/shard_map/ppermute | solution.py:19
  112.5 3.0 %collective-permute-done.14 = f32[3]{0:T(128)S(1)} collective-permute-done((f32[3]{0:T(128)S(1)}, f32[3]{0:T(128)S(1)}, u32[]{:S(2)}, u32[]{:S(2)}) %collective-permute-start.14) | collective-permute-done | bytes 44 | tf_op jit(solution)/shard_map/ppermute | solution.py:19
  117.0 2.1 collective-permute-done.15
  125.8 1.6 collective-permute-start.20
  127.3 7.8 %collective-permute-done.20 = bf16[128,512]{1,0:T(8,128)(2,1)S(1)} collective-permute-done((bf16[128,512]{1,0:T(8,128)(2,1)S(1)}, bf16[128,512]{1,0:T(8,128)(2,1)S(1)}, u32[]{:S(2)}, u32[]{:S(2)}) %collective-permute-start.20) | collective-permute-done | bytes 131104 | tf_op jit(solution)/shard_map/ppermute | solution.py:19
  135.3 3.0 %collective-permute-start.17 = (bf16[128,512]{1,0:T(8,128)(2,1)S(1)}, bf16[128,512]{1,0:T(8,128)(2,1)S(1)}, u32[]{:S(2)}, u32[]{:S(2)}) collective-permute-start(bf16[128,512]{1,0:T(8,128)(2,1)S(1)} %convert_element_type.108), channel_id=1, source_target_pairs={{0,16},{4,20},{8,24},{12,28},{16,0},{20,4},{24,8},{28,12},{1,17},{... | collective-permute-start | bytes 393224 | tf_op jit(solution)/shard_map/ppermute | solution.py:19
  138.3 7.7 %collective-permute-done.21 = bf16[256,512]{1,0:T(8,128)(2,1)S(1)} collective-permute-done((bf16[256,512]{1,0:T(8,128)(2,1)S(1)}, bf16[256,512]{1,0:T(8,128)(2,1)S(1)}, u32[]{:S(2)}, u32[]{:S(2)}) %collective-permute-start.21) | collective-permute-done | bytes 262176 | tf_op jit(solution)/shard_map/ppermute | solution.py:19
  147.6 6.0 %collective-permute-done.18 = bf16[256,512]{1,0:T(8,128)(2,1)S(1)} collective-permute-done((bf16[256,512]{1,0:T(8,128)(2,1)S(1)}, bf16[256,512]{1,0:T(8,128)(2,1)S(1)}, u32[]{:S(2)}, u32[]{:S(2)}) %collective-permute-start.18) | collective-permute-done | bytes 262176 | tf_op jit(solution)/shard_map/ppermute | solution.py:19
  155.8 5.2 %collective-permute-done.22 = bf16[512,512]{1,0:T(8,128)(2,1)} collective-permute-done((bf16[512,512]{1,0:T(8,128)(2,1)S(1)}, bf16[512,512]{1,0:T(8,128)(2,1)}, u32[]{:S(2)}, u32[]{:S(2)}) %collective-permute-start.22) | collective-permute-done | bytes 524320 | tf_op jit(solution)/shard_map/ppermute | solution.py:19
  161.0 14.7 %fusion.7 = (f32[512]{0:T(512)S(1)}, f32[]{:T(128)}, f32[1024,512]{1,0:T(8,128)}) fusion(bf16[512,512]{1,0:T(8,128)(2,1)} %collective-permute-done.22, bf16[256,512]{1,0:T(8,128)(2,1)S(1)} %collective-permute-done.21, bf16[128,512]{1,0:T(8,128)(2,1)S(1)} %collective-permute-done.20, bf16[128,512]{1,0:T(8,128)(2,1)S(1)} %convert_element_type.111, ...), kind=kOutput, calls=%fused_computation.15 | convolution fusion | flops 6458179072 | bytes 19924996 | tf_op jit(solution)/shard_map/dot_general | solution.py:86
  175.7 1.8 broadcast_multiply_fusion
  179.0 15.0 %fusion.5 = (f32[512]{0:T(512)S(1)}, f32[]{:T(128)}, f32[1024,512]{1,0:T(8,128)}) fusion(bf16[512,512]{1,0:T(8,128)(2,1)} %collective-permute-done.19, bf16[256,512]{1,0:T(8,128)(2,1)} %copy-done.6, bf16[128,512]{1,0:T(8,128)(2,1)} %copy-done.5, bf16[128,512]{1,0:T(8,128)(2,1)S(1)} %convert_element_type.108, ...), kind=kOutput, calls=%fused_computation.13 | convolution fusion | flops 6458179072 | bytes 19924996 | tf_op jit(solution)/shard_map/dot_general | solution.py:86
  194.0 1.8 broadcast_multiply_fusion.1
  198.8 6.6 %collective-permute-done.28 = f16[512,512]{1,0:T(8,128)(2,1)S(1)} collective-permute-done((f16[512,512]{1,0:T(8,128)(2,1)S(1)}, f16[512,512]{1,0:T(8,128)(2,1)S(1)}, u32[]{:S(2)}, u32[]{:S(2)}) %collective-permute-start.28) | collective-permute-done | bytes 524320 | tf_op jit(solution)/shard_map/ppermute | solution.py:19
  205.8 3.1 %collective-permute-done.32 = f16[256,512]{1,0:T(8,128)(2,1)S(1)} collective-permute-done((f16[256,512]{1,0:T(8,128)(2,1)S(1)}, f16[256,512]{1,0:T(8,128)(2,1)S(1)}, u32[]{:S(2)}, u32[]{:S(2)}) %collective-permute-start.32) | collective-permute-done | bytes 262176 | tf_op jit(solution)/shard_map/ppermute | solution.py:19
  209.7 2.5 %collective-permute-done.29 = f16[256,512]{1,0:T(8,128)(2,1)S(1)} collective-permute-done((f16[256,512]{1,0:T(8,128)(2,1)S(1)}, f16[256,512]{1,0:T(8,128)(2,1)S(1)}, u32[]{:S(2)}, u32[]{:S(2)}) %collective-permute-start.29) | collective-permute-done | bytes 262176 | tf_op jit(solution)/shard_map/ppermute | solution.py:19
  212.3 2.0 collective-permute-start.30
  216.8 2.4 collective-permute-start.23
  219.2 2.5 %collective-permute-done.23 = f32[1]{0:T(128)} collective-permute-done((f32[1]{0:T(128)}, f32[1]{0:T(128)}, u32[]{:S(2)}, u32[]{:S(2)}) %collective-permute-start.23) | collective-permute-done | bytes 36 | tf_op jit(solution)/shard_map/ppermute | solution.py:19
  222.3 2.9 %collective-permute-start.24 = (f32[1]{0:T(128)}, f32[1]{0:T(128)}, u32[]{:S(2)}, u32[]{:S(2)}) collective-permute-start(f32[1]{0:T(128)} %add.161), channel_id=1, source_target_pairs={{0,8},{4,12},{8,0},{12,4},{16,24},{20,28},{24,16},{28,20},{1,9},{5... | collective-permute-start | bytes 20 | tf_op jit(solution)/shard_map/ppermute | solution.py:19
  226.6 3.8 %collective-permute-start.25 = (f32[1]{0:T(128)}, f32[1]{0:T(128)}, u32[]{:S(2)}, u32[]{:S(2)}) collective-permute-start(f32[1]{0:T(128)} %add.162), channel_id=1, source_target_pairs={{0,4},{4,0},{8,12},{12,8},{16,20},{20,16},{24,28},{28,24},{1,5},{5... | collective-permute-start | bytes 20 | tf_op jit(solution)/shard_map/ppermute | solution.py:19
  231.3 2.9 %collective-permute-start.26 = (f32[1]{0:T(128)}, f32[1]{0:T(128)}, u32[]{:S(2)}, u32[]{:S(2)}) collective-permute-start(f32[1]{0:T(128)} %add.163), channel_id=1, source_target_pairs={{0,2},{1,3},{2,0},{3,1},{4,6},{5,7},{6,4},{7,5},{8,10},{9,11},{10,... | collective-permute-start | bytes 20 | tf_op jit(solution)/shard_map/ppermute | solution.py:19
  (97 shorter events, 36.2 us)
Async XLA Ops:
  1.7 17.1 %collective-permute-start.6 = (bf16[128,512]{1,0:T(8,128)(2,1)S(1)}, bf16[128,512]{1,0:T(8,128)(2,1)S(1)}, u32[]{:S(2)}, u32[]{:S(2)}) collective-permute-start(bf16[128,512]{1,0:T(8,128)(2,1)S(1)} %get-tuple-element.32), channel_id=1, source_target_pairs={{0,16},{4,20},{8,24},{12,28},{16,0},{20,4},{24,8},{28,12},{1,17},{... | collective-permute-start | bytes 393224 | tf_op jit(solution)/shard_map/ppermute | solution.py:19
  5.8 22.5 %collective-permute-start = (bf16[128,512]{1,0:T(8,128)(2,1)S(1)}, bf16[128,512]{1,0:T(8,128)(2,1)S(1)}, u32[]{:S(2)}, u32[]{:S(2)}) collective-permute-start(bf16[128,512]{1,0:T(8,128)(2,1)S(1)} %get-tuple-element.33), channel_id=1, source_target_pairs={{0,16},{4,20},{8,24},{12,28},{16,0},{20,4},{24,8},{28,12},{1,17},{... | collective-permute-start | bytes 393224 | tf_op jit(solution)/shard_map/ppermute | solution.py:19
  18.9 7.8 %collective-permute-start.7 = (bf16[256,512]{1,0:T(8,128)(2,1)S(1)}, bf16[256,512]{1,0:T(8,128)(2,1)S(1)}, u32[]{:S(2)}, u32[]{:S(2)}) collective-permute-start(bf16[256,512]{1,0:T(8,128)(2,1)S(1)} %pad_maximum_fusion.11), channel_id=1, source_target_pairs={{0,8},{4,12},{8,0},{12,4},{16,24},{20,28},{24,16},{28,20},{1,9},{5... | collective-permute-start | bytes 786440 | tf_op jit(solution)/shard_map/ppermute | solution.py:19
  26.7 14.9 %collective-permute-start.8 = (bf16[512,512]{1,0:T(8,128)(2,1)S(1)}, bf16[512,512]{1,0:T(8,128)(2,1)S(1)}, u32[]{:S(2)}, u32[]{:S(2)}) collective-permute-start(bf16[512,512]{1,0:T(8,128)(2,1)S(1)} %pad_maximum_fusion.5), channel_id=1, source_target_pairs={{0,4},{4,0},{8,12},{12,8},{16,20},{20,16},{24,28},{28,24},{1,5},{5... | collective-permute-start | bytes 1572872 | tf_op jit(solution)/shard_map/ppermute | solution.py:19
  28.3 6.4 %collective-permute-start.1 = (bf16[256,512]{1,0:T(8,128)(2,1)S(1)}, bf16[256,512]{1,0:T(8,128)(2,1)S(1)}, u32[]{:S(2)}, u32[]{:S(2)}) collective-permute-start(bf16[256,512]{1,0:T(8,128)(2,1)S(1)} %pad_maximum_fusion.10), channel_id=1, source_target_pairs={{0,8},{4,12},{8,0},{12,4},{16,24},{20,28},{24,16},{28,20},{1,9},{5... | collective-permute-start | bytes 786440 | tf_op jit(solution)/shard_map/ppermute | solution.py:19
  35.6 21.6 %collective-permute-start.2 = (bf16[512,512]{1,0:T(8,128)(2,1)}, bf16[512,512]{1,0:T(8,128)(2,1)}, u32[]{:S(2)}, u32[]{:S(2)}) collective-permute-start(bf16[512,512]{1,0:T(8,128)(2,1)} %pad_maximum_fusion.4), channel_id=1, source_target_pairs={{0,4},{4,0},{8,12},{12,8},{16,20},{20,16},{24,28},{28,24},{1,5},{5... | collective-permute-start | bytes 1572872 | tf_op jit(solution)/shard_map/ppermute | solution.py:19
  41.7 0.8 copy-start.4
  55.7 18.5 %collective-permute-start.9 = (f16[512,512]{1,0:T(8,128)(2,1)}, f16[512,512]{1,0:T(8,128)(2,1)}, u32[]{:S(2)}, u32[]{:S(2)}) collective-permute-start(f16[512,512]{1,0:T(8,128)(2,1)} %slice_convert_fusion.2), channel_id=1, source_target_pairs={{0,4},{4,0},{8,12},{12,8},{16,20},{20,16},{24,28},{28,24},{1,5},{5... | collective-permute-start | bytes 1572872 | tf_op jit(solution)/shard_map/ppermute | solution.py:19
  73.6 9.3 %copy-start.3 = (f32[1024,512]{1,0:T(8,128)S(1)}, f32[1024,512]{1,0:T(8,128)}, u32[]{:S(2)}) copy-start(f32[1024,512]{1,0:T(8,128)} %convolution_multiply_fusion.1) | copy-start | bytes 6291460
  73.6 9.2 %collective-permute-start.3 = (f16[512,512]{1,0:T(8,128)(2,1)S(1)}, f16[512,512]{1,0:T(8,128)(2,1)S(1)}, u32[]{:S(2)}, u32[]{:S(2)}) collective-permute-start(f16[512,512]{1,0:T(8,128)(2,1)S(1)} %slice_convert_fusion.3), channel_id=1, source_target_pairs={{0,4},{4,0},{8,12},{12,8},{16,20},{20,16},{24,28},{28,24},{1,5},{5... | collective-permute-start | bytes 1572872 | tf_op jit(solution)/shard_map/ppermute | solution.py:19
  75.5 10.6 %collective-permute-start.10 = (f16[256,512]{1,0:T(8,128)(2,1)S(1)}, f16[256,512]{1,0:T(8,128)(2,1)S(1)}, u32[]{:S(2)}, u32[]{:S(2)}) collective-permute-start(f16[256,512]{1,0:T(8,128)(2,1)S(1)} %slice_convert_fusion.6), channel_id=1, source_target_pairs={{0,8},{4,12},{8,0},{12,4},{16,24},{20,28},{24,16},{28,20},{1,9},{5... | collective-permute-start | bytes 786440 | tf_op jit(solution)/shard_map/ppermute | solution.py:19
  83.1 10.0 %copy-start = (f32[128,1024]{1,0:T(8,128)S(1)}, f32[128,1024]{1,0:T(8,128)}, u32[]{:S(2)}) copy-start(f32[128,1024]{1,0:T(8,128)} %param.5) | copy-start | bytes 1572868
  83.1 6.4 %collective-permute-start.4 = (f16[256,512]{1,0:T(8,128)(2,1)S(1)}, f16[256,512]{1,0:T(8,128)(2,1)S(1)}, u32[]{:S(2)}, u32[]{:S(2)}) collective-permute-start(f16[256,512]{1,0:T(8,128)(2,1)S(1)} %slice_convert_fusion.7), channel_id=1, source_target_pairs={{0,8},{4,12},{8,0},{12,4},{16,24},{20,28},{24,16},{28,20},{1,9},{5... | collective-permute-start | bytes 786440 | tf_op jit(solution)/shard_map/ppermute | solution.py:19
  86.3 9.3 %collective-permute-start.11 = (f16[128,512]{1,0:T(8,128)(2,1)S(1)}, f16[128,512]{1,0:T(8,128)(2,1)S(1)}, u32[]{:S(2)}, u32[]{:S(2)}) collective-permute-start(f16[128,512]{1,0:T(8,128)(2,1)S(1)} %slice_convert_fusion.10), channel_id=1, source_target_pairs={{0,16},{4,20},{8,24},{12,28},{16,0},{20,4},{24,8},{28,12},{1,17},{... | collective-permute-start | bytes 393224 | tf_op jit(solution)/shard_map/ppermute | solution.py:19
  89.7 8.7 %collective-permute-start.5 = (f16[128,512]{1,0:T(8,128)(2,1)S(1)}, f16[128,512]{1,0:T(8,128)(2,1)S(1)}, u32[]{:S(2)}, u32[]{:S(2)}) collective-permute-start(f16[128,512]{1,0:T(8,128)(2,1)S(1)} %slice_convert_fusion.11), channel_id=1, source_target_pairs={{0,16},{4,20},{8,24},{12,28},{16,0},{20,4},{24,8},{28,12},{1,17},{... | collective-permute-start | bytes 393224 | tf_op jit(solution)/shard_map/ppermute | solution.py:19
  99.2 47.5 %copy-start.1 = (f32[128,512]{1,0:T(8,128)}, f32[128,512]{1,0:T(8,128)S(1)}, u32[]{:S(2)}) copy-start(f32[128,512]{1,0:T(8,128)S(1)} %get-tuple-element.19) | copy-start | bytes 786436
  102.5 4.4 %collective-permute-start.12 = (f32[3]{0:T(128)S(1)}, f32[3]{0:T(128)S(1)}, u32[]{:S(2)}, u32[]{:S(2)}) collective-permute-start(f32[3]{0:T(128)S(1)} %pad_maximum_fusion.18), channel_id=1, source_target_pairs={{0,16},{4,20},{8,24},{12,28},{16,0},{20,4},{24,8},{28,12},{1,17},{... | collective-permute-start | bytes 44 | tf_op jit(solution)/shard_map/ppermute | solution.py:19
  107.7 3.5 %collective-permute-start.13 = (f32[3]{0:T(128)S(1)}, f32[3]{0:T(128)S(1)}, u32[]{:S(2)}, u32[]{:S(2)}) collective-permute-start(f32[3]{0:T(128)S(1)} %fusion.38), channel_id=1, source_target_pairs={{0,8},{4,12},{8,0},{12,4},{16,24},{20,28},{24,16},{28,20},{1,9},{5... | collective-permute-start | bytes 44 | tf_op jit(solution)/shard_map/ppermute | solution.py:19
  112.0 3.5 %collective-permute-start.14 = (f32[3]{0:T(128)S(1)}, f32[3]{0:T(128)S(1)}, u32[]{:S(2)}, u32[]{:S(2)}) collective-permute-start(f32[3]{0:T(128)S(1)} %fusion.39), channel_id=1, source_target_pairs={{0,4},{4,0},{8,12},{12,8},{16,20},{20,16},{24,28},{28,24},{1,5},{5... | collective-permute-start | bytes 44 | tf_op jit(solution)/shard_map/ppermute | solution.py:19
  115.5 3.5 %collective-permute-start.15 = (f32[3]{0:T(128)S(1)}, f32[3]{0:T(128)S(1)}, u32[]{:S(2)}, u32[]{:S(2)}) collective-permute-start(f32[3]{0:T(128)S(1)} %add.152), channel_id=1, source_target_pairs={{0,2},{1,3},{2,0},{3,1},{4,6},{5,7},{6,4},{7,5},{8,10},{9,11},{10,... | collective-permute-start | bytes 44 | tf_op jit(solution)/shard_map/ppermute | solution.py:19
  119.1 1.1 collective-permute-start.16
  125.8 9.4 %collective-permute-start.20 = (bf16[128,512]{1,0:T(8,128)(2,1)S(1)}, bf16[128,512]{1,0:T(8,128)(2,1)S(1)}, u32[]{:S(2)}, u32[]{:S(2)}) collective-permute-start(bf16[128,512]{1,0:T(8,128)(2,1)S(1)} %convert_element_type.111), channel_id=1, source_target_pairs={{0,16},{4,20},{8,24},{12,28},{16,0},{20,4},{24,8},{28,12},{1,17},{... | collective-permute-start | bytes 393224 | tf_op jit(solution)/shard_map/ppermute | solution.py:19
  135.2 10.8 %collective-permute-start.21 = (bf16[256,512]{1,0:T(8,128)(2,1)S(1)}, bf16[256,512]{1,0:T(8,128)(2,1)S(1)}, u32[]{:S(2)}, u32[]{:S(2)}) collective-permute-start(bf16[256,512]{1,0:T(8,128)(2,1)S(1)} %pad_maximum_fusion.13), channel_id=1, source_target_pairs={{0,8},{4,12},{8,0},{12,4},{16,24},{20,28},{24,16},{28,20},{1,9},{5... | collective-permute-start | bytes 786440 | tf_op jit(solution)/shard_map/ppermute | solution.py:19
  135.3 11.4 %collective-permute-start.17 = (bf16[128,512]{1,0:T(8,128)(2,1)S(1)}, bf16[128,512]{1,0:T(8,128)(2,1)S(1)}, u32[]{:S(2)}, u32[]{:S(2)}) collective-permute-start(bf16[128,512]{1,0:T(8,128)(2,1)S(1)} %convert_element_type.108), channel_id=1, source_target_pairs={{0,16},{4,20},{8,24},{12,28},{16,0},{20,4},{24,8},{28,12},{1,17},{... | collective-permute-start | bytes 393224 | tf_op jit(solution)/shard_map/ppermute | solution.py:19
  146.0 15.0 %collective-permute-start.22 = (bf16[512,512]{1,0:T(8,128)(2,1)S(1)}, bf16[512,512]{1,0:T(8,128)(2,1)}, u32[]{:S(2)}, u32[]{:S(2)}) collective-permute-start(bf16[512,512]{1,0:T(8,128)(2,1)S(1)} %pad_maximum_fusion.7), channel_id=1, source_target_pairs={{0,4},{4,0},{8,12},{12,8},{16,20},{20,16},{24,28},{28,24},{1,5},{5... | collective-permute-start | bytes 1572872 | tf_op jit(solution)/shard_map/ppermute | solution.py:19
  146.7 29.0 %copy-start.5 = (bf16[128,512]{1,0:T(8,128)(2,1)}, bf16[128,512]{1,0:T(8,128)(2,1)S(1)}, u32[]{:S(2)}) copy-start(bf16[128,512]{1,0:T(8,128)(2,1)S(1)} %collective-permute-done.17) | copy-start | bytes 393220
  146.7 6.9 %collective-permute-start.18 = (bf16[256,512]{1,0:T(8,128)(2,1)S(1)}, bf16[256,512]{1,0:T(8,128)(2,1)S(1)}, u32[]{:S(2)}, u32[]{:S(2)}) collective-permute-start(bf16[256,512]{1,0:T(8,128)(2,1)S(1)} %pad_maximum_fusion.12), channel_id=1, source_target_pairs={{0,8},{4,12},{8,0},{12,4},{16,24},{20,28},{24,16},{28,20},{1,9},{5... | collective-permute-start | bytes 786440 | tf_op jit(solution)/shard_map/ppermute | solution.py:19
  153.6 22.1 %copy-start.6 = (bf16[256,512]{1,0:T(8,128)(2,1)}, bf16[256,512]{1,0:T(8,128)(2,1)S(1)}, u32[]{:S(2)}) copy-start(bf16[256,512]{1,0:T(8,128)(2,1)S(1)} %collective-permute-done.18) | copy-start | bytes 786436
  154.5 24.5 %collective-permute-start.19 = (bf16[512,512]{1,0:T(8,128)(2,1)}, bf16[512,512]{1,0:T(8,128)(2,1)}, u32[]{:S(2)}, u32[]{:S(2)}) collective-permute-start(bf16[512,512]{1,0:T(8,128)(2,1)} %pad_maximum_fusion.6), channel_id=1, source_target_pairs={{0,4},{4,0},{8,12},{12,8},{16,20},{20,16},{24,28},{28,24},{1,5},{5... | collective-permute-start | bytes 1572872 | tf_op jit(solution)/shard_map/ppermute | solution.py:19
  178.5 19.1 %collective-permute-start.31 = (f16[512,512]{1,0:T(8,128)(2,1)}, f16[512,512]{1,0:T(8,128)(2,1)}, u32[]{:S(2)}, u32[]{:S(2)}) collective-permute-start(f16[512,512]{1,0:T(8,128)(2,1)} %slice_convert_fusion), channel_id=1, source_target_pairs={{0,4},{4,0},{8,12},{12,8},{16,20},{20,16},{24,28},{28,24},{1,5},{5... | collective-permute-start | bytes 1572872 | tf_op jit(solution)/shard_map/ppermute | solution.py:19
  196.0 9.5 %collective-permute-start.28 = (f16[512,512]{1,0:T(8,128)(2,1)S(1)}, f16[512,512]{1,0:T(8,128)(2,1)S(1)}, u32[]{:S(2)}, u32[]{:S(2)}) collective-permute-start(f16[512,512]{1,0:T(8,128)(2,1)S(1)} %slice_convert_fusion.1), channel_id=1, source_target_pairs={{0,4},{4,0},{8,12},{12,8},{16,20},{20,16},{24,28},{28,24},{1,5},{5... | collective-permute-start | bytes 1572872 | tf_op jit(solution)/shard_map/ppermute | solution.py:19
  198.8 10.1 %collective-permute-start.32 = (f16[256,512]{1,0:T(8,128)(2,1)S(1)}, f16[256,512]{1,0:T(8,128)(2,1)S(1)}, u32[]{:S(2)}, u32[]{:S(2)}) collective-permute-start(f16[256,512]{1,0:T(8,128)(2,1)S(1)} %slice_convert_fusion.4), channel_id=1, source_target_pairs={{0,8},{4,12},{8,0},{12,4},{16,24},{20,28},{24,16},{28,20},{1,9},{5... | collective-permute-start | bytes 786440 | tf_op jit(solution)/shard_map/ppermute | solution.py:19
  205.6 31.9 %copy-start.2 = (f32[128,512]{1,0:T(8,128)S(1)}, f32[128,512]{1,0:T(8,128)}, u32[]{:S(2)}) copy-start(f32[128,512]{1,0:T(8,128)} %copy-done.1) | copy-start | bytes 786436
  205.7 6.5 %collective-permute-start.29 = (f16[256,512]{1,0:T(8,128)(2,1)S(1)}, f16[256,512]{1,0:T(8,128)(2,1)S(1)}, u32[]{:S(2)}, u32[]{:S(2)}) collective-permute-start(f16[256,512]{1,0:T(8,128)(2,1)S(1)} %slice_convert_fusion.5), channel_id=1, source_target_pairs={{0,8},{4,12},{8,0},{12,4},{16,24},{20,28},{24,16},{28,20},{1,9},{5... | collective-permute-start | bytes 786440 | tf_op jit(solution)/shard_map/ppermute | solution.py:19
  209.0 28.5 %collective-permute-start.33 = (f16[128,512]{1,0:T(8,128)(2,1)S(1)}, f16[128,512]{1,0:T(8,128)(2,1)S(1)}, u32[]{:S(2)}, u32[]{:S(2)}) collective-permute-start(f16[128,512]{1,0:T(8,128)(2,1)S(1)} %slice_convert_fusion.8), channel_id=1, source_target_pairs={{0,16},{4,20},{8,24},{12,28},{16,0},{20,4},{24,8},{28,12},{1,17},{... | collective-permute-start | bytes 393224 | tf_op jit(solution)/shard_map/ppermute | solution.py:19
  212.3 25.1 %collective-permute-start.30 = (f16[128,512]{1,0:T(8,128)(2,1)S(1)}, f16[128,512]{1,0:T(8,128)(2,1)S(1)}, u32[]{:S(2)}, u32[]{:S(2)}) collective-permute-start(f16[128,512]{1,0:T(8,128)(2,1)S(1)} %slice_convert_fusion.9), channel_id=1, source_target_pairs={{0,16},{4,20},{8,24},{12,28},{16,0},{20,4},{24,8},{28,12},{1,17},{... | collective-permute-start | bytes 393224 | tf_op jit(solution)/shard_map/ppermute | solution.py:19
  216.8 4.9 %collective-permute-start.23 = (f32[1]{0:T(128)}, f32[1]{0:T(128)}, u32[]{:S(2)}, u32[]{:S(2)}) collective-permute-start(f32[1]{0:T(128)} %bitcast.6), channel_id=1, source_target_pairs={{0,16},{4,20},{8,24},{12,28},{16,0},{20,4},{24,8},{28,12},{1,17},{... | collective-permute-start | bytes 20 | tf_op jit(solution)/shard_map/ppermute | solution.py:19
  222.3 3.7 %collective-permute-start.24 = (f32[1]{0:T(128)}, f32[1]{0:T(128)}, u32[]{:S(2)}, u32[]{:S(2)}) collective-permute-start(f32[1]{0:T(128)} %add.161), channel_id=1, source_target_pairs={{0,8},{4,12},{8,0},{12,4},{16,24},{20,28},{24,16},{28,20},{1,9},{5... | collective-permute-start | bytes 20 | tf_op jit(solution)/shard_map/ppermute | solution.py:19
  226.6 4.1 %collective-permute-start.25 = (f32[1]{0:T(128)}, f32[1]{0:T(128)}, u32[]{:S(2)}, u32[]{:S(2)}) collective-permute-start(f32[1]{0:T(128)} %add.162), channel_id=1, source_target_pairs={{0,4},{4,0},{8,12},{12,8},{16,20},{20,16},{24,28},{28,24},{1,5},{5... | collective-permute-start | bytes 20 | tf_op jit(solution)/shard_map/ppermute | solution.py:19
  231.3 3.7 %collective-permute-start.26 = (f32[1]{0:T(128)}, f32[1]{0:T(128)}, u32[]{:S(2)}, u32[]{:S(2)}) collective-permute-start(f32[1]{0:T(128)} %add.163), channel_id=1, source_target_pairs={{0,2},{1,3},{2,0},{3,1},{4,6},{5,7},{6,4},{7,5},{8,10},{9,11},{10,... | collective-permute-start | bytes 20 | tf_op jit(solution)/shard_map/ppermute | solution.py:19
  235.5 1.3 collective-permute-start.27

commit v2 on v0

v2 whole, which is shorter than its diff:
```python
import jax
import jax.numpy as jnp
from jax import lax
from jax.experimental import pallas as pl
from jax.experimental.pallas import tpu as pltpu
from jax.sharding import PartitionSpec as P

CHUNKS = 2
TILE = 768
VMEM_LIMIT = 56 * 2**20

damp_coef = 0.5

FEATURE_MAX = 6.0
CURVATURE_MAX = 2.0
WIRE = jnp.float16
WIRE_MAX = 32768.0
TINY = 1e-30
EXTRA = 16


def swap(values, axis, stride):
    size = lax.axis_size(axis)
    return lax.ppermute(values, axis, [(i, i ^ stride) for i in range(size)])


def strides_of(axis):
    size = lax.axis_size(axis)
    return [1 << bit for bit in reversed(range(size.bit_length() - 1))]


def routes():
    even = strides_of("dp")
    odd = even[:-2] + even[:-3:-1]
    return even, odd


def trade(values, step):
    n_dp, n_mp = lax.axis_size("dp"), lax.axis_size("mp")
    pairs = []
    for d in range(n_dp):
        for m in range(n_mp):
            pairs.append((d * n_mp + m, (d ^ routes()[m % 2][step]) * n_mp + m))
    return lax.ppermute(values, ("dp", "mp"), pairs)


def order_of(route):
    order = [0]
    for stride in route:
        order = order + [place ^ stride for place in order]
    return order


def join(halves):
    return jnp.concatenate(halves, axis=0)


def scatter_start(total, extra, step):
    half = total.shape[0] // 2
    sent = total[half:].astype(WIRE)
    if extra is not None:
        extra = extra.astype(WIRE)
        sent = join([sent, jnp.broadcast_to(extra, (EXTRA, extra.shape[1]))])
    return total[:half], extra, trade(sent, step)


def scatter_end(kept, extra, received):
    half = kept.shape[0]
    total = kept + received[:half].astype(jnp.float32)
    if extra is not None:
        extra = extra.astype(jnp.float32) + received[half : half + 1].astype(jnp.float32)
    return total, extra


def colsum(values):
    return jnp.sum(values, axis=0, keepdims=True)


def coef_kernel(sums_ref, *refs):
    out_ref = refs[-1]
    total = jnp.sum(sums_ref[...], axis=1, keepdims=True)
    norm, curv, image = total[0:1], total[1:2], total[2:3]
    step = norm / curv
    following = norm - 2.0 * step * curv + step * step * image
    ratio = following / norm
    width = sums_ref.shape[1]
    for k, (guess_ref, lift_ref) in enumerate(zip(refs[:-1:2], refs[1:-1:2])):
        along = step / guess_ref[...]
        out_ref[8 * k : 8 * k + 1, :] = along / lift_ref[...]
        out_ref[8 * k + 1 : 8 * k + 2, :] = 1.0 + ratio - along
        out_ref[8 * k + 2 : 8 * k + 3, :] = jnp.broadcast_to(step, (1, width))
        out_ref[8 * k + 3 : 8 * k + 4, :] = jnp.broadcast_to(1.0 + ratio, (1, width))
        out_ref[8 * k + 4 : 8 * k + 5, :] = jnp.broadcast_to(following, (1, width))


def curve_kernel(blocks, f_ref, c_ref, near_ref, far_ref, out_ref, stat_ref, held, total, *, n_dp, token_count):
    din = total.shape[0]
    rows = din // n_dp
    step = pl.program_id(0)
    last = pl.num_programs(0) - 1

    def place(position):
        return pl.ds(pl.multiple_of(blocks[position] * rows, rows), rows)

    @pl.when(step == 0)
    def _():
        for position in range(n_dp):
            half = (near_ref, far_ref)[2 * position // n_dp]
            at = (position % (n_dp // 2)) * rows
            held[place(position), :] = half[at : at + rows, :]

    projected = jnp.dot(f_ref[...], held[...], preferred_element_type=jnp.float32)
    weighted = (c_ref[...].astype(jnp.float32) * projected).astype(jnp.bfloat16)
    share = lax.dot_general(
        f_ref[...], weighted, (((0,), (0,)), ((), ())), preferred_element_type=jnp.float32
    )

    @pl.when(step == 0)
    def _():
        total[...] = share

    @pl.when(step > 0)
    def _():
        total[...] += share

    @pl.when(step == last)
    def _():
        vector = held[...].astype(jnp.float32)
        dot = jnp.sum(vector * total[...], axis=0, keepdims=True)
        largest = jnp.max(jnp.abs(vector), axis=0, keepdims=True)
        to_wire = WIRE_MAX / (bound_of(din) * token_count)
        square = jnp.sum(vector * vector, axis=0, keepdims=True)
        scale = to_wire / jnp.maximum(largest, TINY)
        stat_ref[0:1, :] = dot
        stat_ref[1:2, :] = largest
        stat_ref[2:3, :] = scale
        stat_ref[3:4, :] = dot / jnp.maximum(square, TINY) * to_wire
        for position in range(n_dp):
            out_ref[position * rows : (position + 1) * rows, :] = total[place(position), :] * scale


def bound_of(din):
    return FEATURE_MAX * FEATURE_MAX * CURVATURE_MAX * din


def curve(features, curvature, chunk, blocks, halves, n_dp):
    tokens, din = features.shape
    width = halves[0].shape[1]
    tile = TILE if tokens % TILE == 0 else tokens
    flops = 4 * tokens * din * width
    size = 2 * tokens * (din + width) + 6 * din * width
    half = pl.BlockSpec((din // 2, width), lambda i, blocks: (0, 0))
    return pl.pallas_call(
        lambda *refs: curve_kernel(*refs, n_dp=n_dp, token_count=n_dp * tokens),
        grid_spec=pltpu.PrefetchScalarGridSpec(
            num_scalar_prefetch=1,
            grid=(tokens // tile,),
            in_specs=[
                pl.BlockSpec((tile, din), lambda i, blocks: (i, 0)),
                pl.BlockSpec((tile, width), lambda i, blocks: (i, chunk)),
                half,
                half,
            ],
            out_specs=[
                pl.BlockSpec((din, width), lambda i, blocks: (0, 0)),
                pl.BlockSpec((8, width), lambda i, blocks: (0, 0)),
            ],
            scratch_shapes=[
                pltpu.VMEM((din, width), jnp.bfloat16),
                pltpu.VMEM((din, width), jnp.float32),
            ],
        ),
        out_shape=[
            jax.ShapeDtypeStruct((din, width), jnp.float32),
            jax.ShapeDtypeStruct((8, width), jnp.float32),
        ],
        compiler_params=pltpu.CompilerParams(vmem_limit_bytes=VMEM_LIMIT),
        cost_estimate=pl.CostEstimate(flops=flops, bytes_accessed=size, transcendentals=0),
    )(blocks, features, curvature, *halves)


def shards(features, curvature, task_grad):
    n_dp = lax.axis_size("dp")
    din = features.shape[1]
    token_count = features.shape[0] * n_dp
    width = task_grad.shape[1] // CHUNKS
    me = lax.axis_index("dp")
    odd = lax.axis_index("mp") % 2
    blocks = jnp.where(odd, *[jnp.array(order_of(r), jnp.int32) for r in routes()[::-1]]) ^ me
    steps = len(strides_of("dp"))
    chunks = range(CHUNKS)
    hops = []
    dots = None

    def multiply(k, halves):
        rows, stats = curve(features, curvature, k, blocks, halves, n_dp)
        return rows, stats

    def hop():
        nonlocal dots
        if hops:
            dots = dots + swap(dots, *hops.pop(0))

    grad = [task_grad[:, k * width : (k + 1) * width] for k in chunks]

    held = [g.astype(jnp.bfloat16) for g in grad]
    for step in range(steps):
        grad_rows = [(h, trade(h, step)) for h in held]
        if step + 1 < steps:
            held = [join(pair) for pair in grad_rows]

    stats, moving = [None] * CHUNKS, [None] * CHUNKS
    for k in chunks:
        rows, stats[k] = multiply(k, grad_rows[k])
        moving[k] = scatter_start(rows, stats[k][3:4], steps - 1)
    image, guess, lift = [None] * CHUNKS, [None] * CHUNKS, [None] * CHUNKS
    bound = bound_of(din)
    for step in reversed(range(steps)):
        for k in chunks:
            total, extra = scatter_end(*moving[k])
            if step:
                moving[k] = scatter_start(total, extra, step - 1)
                continue
            image[k] = total / (stats[k][2:3] * token_count) + damp_coef * grad[k]
            guess[k] = 1.0 / (extra * (bound / WIRE_MAX) + damp_coef)
            reach = jnp.maximum(stats[k][1:2], TINY) * (1.0 + 2.0 * (bound + 1.0))
            lift[k] = WIRE_MAX / reach
            trial = ((grad[k] - guess[k] * image[k]) * lift[k]).astype(WIRE)
            moving[k] = (trial, trade(trial, 0))

    dots = jnp.concatenate(
        [
            sum(colsum(grad[k] * grad[k]) for k in chunks),
            sum(colsum(grad[k] * image[k]) for k in chunks),
            sum(colsum(image[k] * image[k]) for k in chunks),
        ]
    )
    all_hops = [(axis, stride) for axis in ("dp", "mp") for stride in strides_of(axis)]
    hops = list(all_hops)
    per_step = -(-len(hops) // steps)
    tie = lax.optimization_barrier
    for step in range(1, steps):
        held = [join(pair) for pair in moving]
        moving = [(h, trade(h, step)) for h in held]
        for _ in range(per_step):
            hop()
    while hops:
        hop()
    coef = pl.pallas_call(
        coef_kernel, out_shape=jax.ShapeDtypeStruct((8 * CHUNKS, width), jnp.float32)
    )(dots, *[row for k in chunks for row in (guess[k], lift[k])])

    direction = []
    for k in chunks:
        row = coef[8 * k : 8 * k + 8]
        direction.append(row[3:4] * grad[k] - row[2:3] * image[k])
        halves = [
            (row[0:1] * t.astype(jnp.float32) + row[1:2] * g.astype(jnp.float32)).astype(
                jnp.bfloat16
            )
            for t, g in zip(moving[k], grad_rows[k])
        ]
        rows, stats[k] = multiply(k, halves)
        moving[k] = scatter_start(rows, None, steps - 1)

    dots = sum(s[0:1] for s in stats) / token_count
    dots += damp_coef * sum(colsum(d * d) for d in direction)
    hops = list(all_hops)
    hop()
    for step in reversed(range(steps)):
        for k in chunks:
            kept, _, received = moving[k]
            if hops:
                received, dots = tie((received, dots))
                hop()
            total, _ = scatter_end(kept, None, received)
            if step:
                moving[k] = scatter_start(total, None, step - 1)
            else:
                moving[k] = total / (stats[k][2:3] * token_count)
    while hops:
        hop()
    direction_dot = jnp.sum(dots, axis=1, keepdims=True)
    solution, residual = [], []
    for k in chunks:
        row = coef[8 * k : 8 * k + 8]
        last_len = row[4:5] / direction_dot
        curved = moving[k] + damp_coef * direction[k]
        solution.append(row[2:3] * grad[k] + last_len * direction[k])
        residual.append(grad[k] - row[2:3] * image[k] - last_len * curved)
    return jnp.concatenate(solution, axis=1), jnp.concatenate(residual, axis=1)


def solution(mesh):
    placed = (P("dp", None), P("dp", "mp"), P("dp", "mp"))
    return jax.shard_map(
        shards,
        mesh=mesh,
        in_specs=placed,
        out_specs=(P("dp", "mp"), P("dp", "mp")),
        check_vma=False,
    )
```

time: 434 us -> 207 us (0.48)
  waiting for transfers between devices: 277 us -> 78.8 us
  blocking collectives: 81.1 us -> 0 us
  Pallas kernels: 0 us -> 52.2 us
  starting transfers between devices: 0.16 us -> 48.6 us
  matrix products: 44.8 us -> 0 us
  between operations: 18.3 us -> 1.15 us
  other arithmetic: 9.48 us -> 21.3 us
    reduce_scatter x2 -> x0, waiting for transfers between devices: 174 us -> none  [shards(): lax.psum_scatter(lax.dot_general(features, weighted, (((0,), (0,)), ((),...]
    all_gather x2 -> x0, waiting for transfers between devices: 104 us -> none  [shards(): gathered = lax.all_gather(dir_bf, 'dp', axis=0, tiled=True)]
    psum x2 -> x0, blocking collectives: 81.1 us -> none  [global_sums(): return lax.psum(values, ('dp', 'mp'))]
    ppermute x0 -> x34, waiting for transfers between devices: none -> 78.8 us  [the longest x24 69.5 us: trade(): return lax.ppermute(values, ('dp', 'mp'), pairs)]
    pallas_call x0 -> x5, Pallas kernels: none -> 52.2 us  [the longest x4 50.7 us: curve(): pl.pallas_call(lambda *refs: curve_kernel(*refs, n_dp=n_dp, token_count=n...]
    ppermute x0 -> x34, starting transfers between devices: none -> 48.6 us  [the longest x24 38.9 us: trade(): return lax.ppermute(values, ('dp', 'mp'), pairs)]
    dot_general x2 -> x0, matrix products: 44.8 us -> none  [shards(): lax.dot_general(features, weighted, (((0,), (0,)), ((), ())), preferred_e...]
    another operation x0 -> x12, other arithmetic: none -> 5.51 us
  transfers between devices with their start and end apart: 4 -> 34, of which waited for: 4 -> 21; matrix products, arithmetic and copies ran while one was open for 0% -> 9% of each run, Pallas kernels for 0% -> 25%
where the time goes in v2:
time: 207 us; the launch traced here: 206 us
  waiting for transfers between devices  78.8 us (38%)
  Pallas kernels  52.2 us (25%)
  starting transfers between devices  48.6 us (23%)
  other arithmetic  21.3 us (10%)
  local copies, waits for them, and re-layouts  3.74 us (2%)
    ppermute x24, waiting for transfers between devices, trade(): return lax.ppermute(values, ('dp', 'mp'), pairs)  69.5 us
    pallas_call x4, Pallas kernels, curve(): pl.pallas_call(lambda *refs: curve_kernel(*refs, n_dp=n_dp, token_count=n...  50.7 us
    ppermute x24, starting transfers between devices, trade(): return lax.ppermute(values, ('dp', 'mp'), pairs)  38.9 us
    ppermute x10, starting transfers between devices, swap(): return lax.ppermute(values, axis, [(i, i ^ stride) for i in range(size)])  9.74 us
    ppermute x10, waiting for transfers between devices, swap(): return lax.ppermute(values, axis, [(i, i ^ stride) for i in range(size)])  9.32 us
    another operation x12, other arithmetic  5.51 us
  transfers between devices with their start and end apart: 34, of which 21 were waited for; matrix products, arithmetic and copies ran while one was open for 9% of the time, Pallas kernels for 25%

profile of v2, /device:TPU:0, one launch (start us, length us, event | category | flops | bytes accessed | tf_op | source)
XLA Modules:
  0.0 205.8 jit_solution(14999724017967754275)
XLA Ops:
  1.7 4.1 %collective-permute-start.6 = (bf16[128,512]{1,0:T(8,128)(2,1)S(1)}, bf16[128,512]{1,0:T(8,128)(2,1)S(1)}, u32[]{:S(2)}, u32[]{:S(2)}) collective-permute-start(bf16[128,512]{1,0:T(8,128)(2,1)S(1)} %get-tuple-element.59), channel_id=1, source_target_pairs={{0,16},{1,17},{2,18},{3,19},{4,20},{5,21},{6,22},{7,23},{8,24},{9,... | collective-permute-start | bytes 393224 | tf_op jit(solution)/shard_map/ppermute | solution.py:44
  5.8 6.3 %collective-permute-done.6 = bf16[128,512]{1,0:T(8,128)(2,1)S(1)} collective-permute-done((bf16[128,512]{1,0:T(8,128)(2,1)S(1)}, bf16[128,512]{1,0:T(8,128)(2,1)S(1)}, u32[]{:S(2)}, u32[]{:S(2)}) %collective-permute-start.6) | collective-permute-done | bytes 131104 | tf_op jit(solution)/shard_map/ppermute | solution.py:44
  12.9 3.4 %collective-permute-start = (bf16[128,512]{1,0:T(8,128)(2,1)S(1)}, bf16[128,512]{1,0:T(8,128)(2,1)S(1)}, u32[]{:S(2)}, u32[]{:S(2)}) collective-permute-start(bf16[128,512]{1,0:T(8,128)(2,1)S(1)} %get-tuple-element.58), channel_id=1, source_target_pairs={{0,16},{1,17},{2,18},{3,19},{4,20},{5,21},{6,22},{7,23},{8,24},{9,... | collective-permute-start | bytes 393224 | tf_op jit(solution)/shard_map/ppermute | solution.py:44
  16.3 6.2 %collective-permute-done.7 = bf16[256,512]{1,0:T(8,128)(2,1)S(1)} collective-permute-done((bf16[256,512]{1,0:T(8,128)(2,1)S(1)}, bf16[256,512]{1,0:T(8,128)(2,1)S(1)}, u32[]{:S(2)}, u32[]{:S(2)}) %collective-permute-start.7) | collective-permute-done | bytes 262176 | tf_op jit(solution)/shard_map/ppermute | solution.py:44
  24.7 5.1 %collective-permute-done.1 = bf16[256,512]{1,0:T(8,128)(2,1)S(1)} collective-permute-done((bf16[256,512]{1,0:T(8,128)(2,1)S(1)}, bf16[256,512]{1,0:T(8,128)(2,1)S(1)}, u32[]{:S(2)}, u32[]{:S(2)}) %collective-permute-start.1) | collective-permute-done | bytes 262176 | tf_op jit(solution)/shard_map/ppermute | solution.py:44
  29.9 2.3 %collective-permute-start.2 = (bf16[512,512]{1,0:T(8,128)(2,1)S(1)}, bf16[512,512]{1,0:T(8,128)(2,1)S(1)}, u32[]{:S(2)}, u32[]{:S(2)}) collective-permute-start(bf16[512,512]{1,0:T(8,128)(2,1)S(1)} %pad_maximum_fusion.2.refs_3_), channel_id=1, source_target_pairs={{0,4},{1,9},{2,6},{3,11},{4,0},{5,13},{6,2},{7,15},{8,12},{9,1},{1... | collective-permute-start | bytes 1572872 | tf_op jit(solution)/shard_map/ppermute | solution.py:44
  33.0 12.6 %shard_map.69 = (f32[1024,512]{1,0:T(8,128)}, f32[8,512]{1,0:T(8,128)}) custom-call(s32[8]{0:T(128)} %fusion.26.refs_0_, bf16[3072,1024]{1,0:T(8,128)(2,1)} %refs_1_.7, bf16[3072,1024]{1,0:T(8,128)(2,1)} %refs_2_.7, bf16[512,512]{1,0:T(8,128)(2,1)} %copy-done.5, bf16[512,512]{1,0:T(8,128)(2,1)} %copy-done.7), custom_call_target="tpu_custom_call" | custom-call | flops 6442450944 | bytes 12582912 | tf_op jit(solution)/shard_map/pallas_call | solution.py:153
  46.3 1.3 slice_convert_fusion.2
  48.8 12.5 %shard_map.68 = (f32[1024,512]{1,0:T(8,128)}, f32[8,512]{1,0:T(8,128)}) custom-call(s32[8]{0:T(128)} %fusion.26.refs_0_, bf16[3072,1024]{1,0:T(8,128)(2,1)} %refs_1_.7, bf16[3072,1024]{1,0:T(8,128)(2,1)} %refs_2_.7, bf16[512,512]{1,0:T(8,128)(2,1)} %copy-done.6, bf16[512,512]{1,0:T(8,128)(2,1)} %copy-done.9), custom_call_target="tpu_custom_call" | custom-call | flops 6442450944 | bytes 12582912 | tf_op jit(solution)/shard_map/pallas_call | solution.py:153
  62.2 1.3 slice_convert_fusion.3
  63.7 1.9 collective-permute-start.3
  66.7 7.7 %collective-permute-done.3 = f16[528,512]{1,0:T(8,128)(2,1)S(1)} collective-permute-done((f16[528,512]{1,0:T(8,128)(2,1)S(1)}, f16[528,512]{1,0:T(8,128)(2,1)S(1)}, u32[]{:S(2)}, u32[]{:S(2)}) %collective-permute-start.3) | collective-permute-done | bytes 540704 | tf_op jit(solution)/shard_map/ppermute | solution.py:44
  76.4 2.0 collective-permute-start.10
  78.4 3.6 %collective-permute-done.4 = f16[272,512]{1,0:T(8,128)(2,1)S(1)} collective-permute-done((f16[272,512]{1,0:T(8,128)(2,1)S(1)}, f16[272,512]{1,0:T(8,128)(2,1)S(1)}, u32[]{:S(2)}, u32[]{:S(2)}) %collective-permute-start.4) | collective-permute-done | bytes 278560 | tf_op jit(solution)/shard_map/ppermute | solution.py:44
  82.1 6.0 %collective-permute-done.10 = f16[272,512]{1,0:T(8,128)(2,1)S(1)} collective-permute-done((f16[272,512]{1,0:T(8,128)(2,1)S(1)}, f16[272,512]{1,0:T(8,128)(2,1)S(1)}, u32[]{:S(2)}, u32[]{:S(2)}) %collective-permute-start.10) | collective-permute-done | bytes 278560 | tf_op jit(solution)/shard_map/ppermute | solution.py:44
  88.2 3.7 %collective-permute-start.5 = (f16[144,512]{1,0:T(8,128)(2,1)S(1)}, f16[144,512]{1,0:T(8,128)(2,1)S(1)}, u32[]{:S(2)}, u32[]{:S(2)}) collective-permute-start(f16[144,512]{1,0:T(8,128)(2,1)S(1)} %pad_maximum_fusion.14), channel_id=1, source_target_pairs={{0,16},{1,17},{2,18},{3,19},{4,20},{5,21},{6,22},{7,23},{8,24},{9,... | collective-permute-start | bytes 442376 | tf_op jit(solution)/shard_map/ppermute | solution.py:44
  92.2 8.2 %collective-permute-done.5 = f16[144,512]{1,0:T(8,128)(2,1)S(1)} collective-permute-done((f16[144,512]{1,0:T(8,128)(2,1)S(1)}, f16[144,512]{1,0:T(8,128)(2,1)S(1)}, u32[]{:S(2)}, u32[]{:S(2)}) %collective-permute-start.5) | collective-permute-done | bytes 147488 | tf_op jit(solution)/shard_map/ppermute | solution.py:44
  100.4 1.6 collective-permute-done.11
  102.5 2.9 %collective-permute-start.21 = (f16[128,512]{1,0:T(8,128)(2,1)S(1)}, f16[128,512]{1,0:T(8,128)(2,1)S(1)}, u32[]{:S(2)}, u32[]{:S(2)}) collective-permute-start(f16[128,512]{1,0:T(8,128)(2,1)S(1)} %get-tuple-element.42), channel_id=1, source_target_pairs={{0,16},{1,17},{2,18},{3,19},{4,20},{5,21},{6,22},{7,23},{8,24},{9,... | collective-permute-start | bytes 393224 | tf_op jit(solution)/shard_map/ppermute | solution.py:44
  105.4 1.6 collective-permute-done.12
  109.2 3.3 %collective-permute-start.22 = (f16[256,512]{1,0:T(8,128)(2,1)}, f16[256,512]{1,0:T(8,128)(2,1)S(1)}, u32[]{:S(2)}, u32[]{:S(2)}) collective-permute-start(f16[256,512]{1,0:T(8,128)(2,1)} %pad_maximum_fusion.13), channel_id=1, source_target_pairs={{0,8},{1,5},{2,10},{3,7},{4,12},{5,1},{6,14},{7,3},{8,0},{9,13},{1... | collective-permute-start | bytes 786440 | tf_op jit(solution)/shard_map/ppermute | solution.py:44
  112.5 2.0 collective-permute-start.14
  114.5 1.8 collective-permute-done.14
  116.3 1.5 collective-permute-start.15
  117.8 2.2 %collective-permute-done.15 = f32[3,512]{1,0:T(4,128)S(1)} collective-permute-done((f32[3,512]{1,0:T(4,128)S(1)}, f32[3,512]{1,0:T(4,128)S(1)}, u32[]{:S(2)}, u32[]{:S(2)}) %collective-permute-start.15) | collective-permute-done | bytes 6176 | tf_op jit(solution)/shard_map/ppermute | solution.py:24
  119.9 1.6 collective-permute-start.17
  122.1 1.5 shard_map.70
  124.7 1.6 collective-permute-start.23
  126.3 2.8 %collective-permute-done.17 = f16[128,512]{1,0:T(8,128)(2,1)S(1)} collective-permute-done((f16[128,512]{1,0:T(8,128)(2,1)S(1)}, f16[128,512]{1,0:T(8,128)(2,1)S(1)}, u32[]{:S(2)}, u32[]{:S(2)}) %collective-permute-start.17) | collective-permute-done | bytes 131104 | tf_op jit(solution)/shard_map/ppermute | solution.py:44
  129.4 8.0 %collective-permute-done.18 = f16[256,512]{1,0:T(8,128)(2,1)S(1)} collective-permute-done((f16[256,512]{1,0:T(8,128)(2,1)S(1)}, f16[256,512]{1,0:T(8,128)(2,1)S(1)}, u32[]{:S(2)}, u32[]{:S(2)}) %collective-permute-start.18) | collective-permute-done | bytes 262176 | tf_op jit(solution)/shard_map/ppermute | solution.py:44
  137.6 2.0 collective-permute-start.19
  139.5 1.4 add_convert_fusion
  140.9 12.7 %shard_map.72 = (f32[1024,512]{1,0:T(8,128)}, f32[8,512]{1,0:T(8,128)}) custom-call(s32[8]{0:T(128)} %fusion.26.refs_0_, bf16[3072,1024]{1,0:T(8,128)(2,1)} %refs_1_.7, bf16[3072,1024]{1,0:T(8,128)(2,1)} %refs_2_.7, bf16[512,512]{1,0:T(8,128)(2,1)} %get-tuple-element.78.refs_3_, bf16[512,512]{1,0:T(8,128)(2,1)} %get-tuple-element.77.refs_4_), custom_call_target="tpu_custom_call" | custom-call | flops 6442450944 | bytes 12582912 | tf_op jit(solution)/shard_map/pallas_call | solution.py:153
  153.6 1.3 slice_convert_fusion
  155.2 1.4 add_convert_fusion.2
  156.6 12.9 %shard_map.71 = (f32[1024,512]{1,0:T(8,128)}, f32[8,512]{1,0:T(8,128)}) custom-call(s32[8]{0:T(128)} %fusion.26.refs_0_, bf16[3072,1024]{1,0:T(8,128)(2,1)} %refs_1_.7, bf16[3072,1024]{1,0:T(8,128)(2,1)} %refs_2_.7, bf16[512,512]{1,0:T(8,128)(2,1)} %get-tuple-element.80.refs_3_, bf16[512,512]{1,0:T(8,128)(2,1)} %get-tuple-element.79.refs_4_), custom_call_target="tpu_custom_call" | custom-call | flops 6442450944 | bytes 12582912 | tf_op jit(solution)/shard_map/pallas_call | solution.py:153
  170.8 1.3 slice_convert_fusion.1
  172.1 1.5 collective-permute-start.20
  173.6 1.3 collective-permute-done.25
  177.3 1.4 collective-permute-done.26
  178.6 5.9 %collective-permute-done.20 = f16[512,512]{1,0:T(8,128)(2,1)S(1)} collective-permute-done((f16[512,512]{1,0:T(8,128)(2,1)S(1)}, f16[512,512]{1,0:T(8,128)(2,1)S(1)}, u32[]{:S(2)}, u32[]{:S(2)}) %collective-permute-start.20) | collective-permute-done | bytes 524320 | tf_op jit(solution)/shard_map/ppermute | solution.py:44
  184.7 2.5 %collective-permute-start.29 = (f32[1,512]{1,0:T(1,128)S(1)}, f32[1,512]{1,0:T(1,128)S(1)}, u32[]{:S(2)}, u32[]{:S(2)}) collective-permute-start(f32[1,512]{1,0:T(1,128)S(1)} %add.220), channel_id=1, source_target_pairs={{0,4},{4,0},{8,12},{12,8},{16,20},{20,16},{24,28},{28,24},{1,5},{5... | collective-permute-start | bytes 6152 | tf_op jit(solution)/shard_map/ppermute | solution.py:24
  187.3 2.0 collective-permute-start.27
  189.4 1.5 collective-permute-start.30
  191.9 1.1 collective-permute-done.30
  193.9 1.5 collective-permute-start.33
  196.0 1.4 slice_divide_fusion.1
  198.4 5.4 %collective-permute-done.33 = f16[128,512]{1,0:T(8,128)(2,1)S(1)} collective-permute-done((f16[128,512]{1,0:T(8,128)(2,1)S(1)}, f16[128,512]{1,0:T(8,128)(2,1)S(1)}, u32[]{:S(2)}, u32[]{:S(2)}) %collective-permute-start.33) | collective-permute-done | bytes 131104 | tf_op jit(solution)/shard_map/ppermute | solution.py:44
  (135 shorter events, 25.7 us)
Async XLA Ops:
  0.6 23.5 %copy-start.15 = (s32[8]{0:T(128)S(1)}, s32[8]{0:T(128)}, u32[]{:S(2)}) copy-start(s32[8]{0:T(128)} %constant.48.clone) | copy-start | bytes 100
  0.6 23.5 %copy-start.16 = (s32[8]{0:T(128)S(1)}, s32[8]{0:T(128)}, u32[]{:S(2)}) copy-start(s32[8]{0:T(128)} %constant.47.clone) | copy-start | bytes 100
  1.7 10.4 %collective-permute-start.6 = (bf16[128,512]{1,0:T(8,128)(2,1)S(1)}, bf16[128,512]{1,0:T(8,128)(2,1)S(1)}, u32[]{:S(2)}, u32[]{:S(2)}) collective-permute-start(bf16[128,512]{1,0:T(8,128)(2,1)S(1)} %get-tuple-element.59), channel_id=1, source_target_pairs={{0,16},{1,17},{2,18},{3,19},{4,20},{5,21},{6,22},{7,23},{8,24},{9,... | collective-permute-start | bytes 393224 | tf_op jit(solution)/shard_map/ppermute | solution.py:44
  12.2 10.3 %collective-permute-start.7 = (bf16[256,512]{1,0:T(8,128)(2,1)S(1)}, bf16[256,512]{1,0:T(8,128)(2,1)S(1)}, u32[]{:S(2)}, u32[]{:S(2)}) collective-permute-start(bf16[256,512]{1,0:T(8,128)(2,1)S(1)} %pad_maximum_fusion.11), channel_id=1, source_target_pairs={{0,8},{1,5},{2,10},{3,7},{4,12},{5,1},{6,14},{7,3},{8,0},{9,13},{1... | collective-permute-start | bytes 786440 | tf_op jit(solution)/shard_map/ppermute | solution.py:44
  12.9 10.2 %collective-permute-start = (bf16[128,512]{1,0:T(8,128)(2,1)S(1)}, bf16[128,512]{1,0:T(8,128)(2,1)S(1)}, u32[]{:S(2)}, u32[]{:S(2)}) collective-permute-start(bf16[128,512]{1,0:T(8,128)(2,1)S(1)} %get-tuple-element.58), channel_id=1, source_target_pairs={{0,16},{1,17},{2,18},{3,19},{4,20},{5,21},{6,22},{7,23},{8,24},{9,... | collective-permute-start | bytes 393224 | tf_op jit(solution)/shard_map/ppermute | solution.py:44
  22.5 9.6 %copy-start.5 = (bf16[512,512]{1,0:T(8,128)(2,1)}, bf16[512,512]{1,0:T(8,128)(2,1)S(1)}, u32[]{:S(2)}) copy-start(bf16[512,512]{1,0:T(8,128)(2,1)S(1)} %pad_maximum_fusion.3.refs_3_) | copy-start | bytes 1572868
  22.6 9.6 %collective-permute-start.8 = (bf16[512,512]{1,0:T(8,128)(2,1)S(1)}, bf16[512,512]{1,0:T(8,128)(2,1)S(1)}, u32[]{:S(2)}, u32[]{:S(2)}) collective-permute-start(bf16[512,512]{1,0:T(8,128)(2,1)S(1)} %pad_maximum_fusion.3.refs_3_), channel_id=1, source_target_pairs={{0,4},{1,9},{2,6},{3,11},{4,0},{5,13},{6,2},{7,15},{8,12},{9,1},{1... | collective-permute-start | bytes 1572872 | tf_op jit(solution)/shard_map/ppermute | solution.py:44
  23.2 6.6 %collective-permute-start.1 = (bf16[256,512]{1,0:T(8,128)(2,1)S(1)}, bf16[256,512]{1,0:T(8,128)(2,1)S(1)}, u32[]{:S(2)}, u32[]{:S(2)}) collective-permute-start(bf16[256,512]{1,0:T(8,128)(2,1)S(1)} %pad_maximum_fusion.10), channel_id=1, source_target_pairs={{0,8},{1,5},{2,10},{3,7},{4,12},{5,1},{6,14},{7,3},{8,0},{9,13},{1... | collective-permute-start | bytes 786440 | tf_op jit(solution)/shard_map/ppermute | solution.py:44
  29.9 15.7 %copy-start.6 = (bf16[512,512]{1,0:T(8,128)(2,1)}, bf16[512,512]{1,0:T(8,128)(2,1)S(1)}, u32[]{:S(2)}) copy-start(bf16[512,512]{1,0:T(8,128)(2,1)S(1)} %pad_maximum_fusion.2.refs_3_) | copy-start | bytes 1572868
  29.9 18.1 %collective-permute-start.2 = (bf16[512,512]{1,0:T(8,128)(2,1)S(1)}, bf16[512,512]{1,0:T(8,128)(2,1)S(1)}, u32[]{:S(2)}, u32[]{:S(2)}) collective-permute-start(bf16[512,512]{1,0:T(8,128)(2,1)S(1)} %pad_maximum_fusion.2.refs_3_), channel_id=1, source_target_pairs={{0,4},{1,9},{2,6},{3,11},{4,0},{5,13},{6,2},{7,15},{8,12},{9,1},{1... | collective-permute-start | bytes 1572872 | tf_op jit(solution)/shard_map/ppermute | solution.py:44
  47.7 18.7 %collective-permute-start.9 = (f16[528,512]{1,0:T(8,128)(2,1)S(1)}, f16[528,512]{1,0:T(8,128)(2,1)S(1)}, u32[]{:S(2)}, u32[]{:S(2)}) collective-permute-start(f16[528,512]{1,0:T(8,128)(2,1)S(1)} %pad_maximum_fusion.1), channel_id=1, source_target_pairs={{0,4},{1,9},{2,6},{3,11},{4,0},{5,13},{6,2},{7,15},{8,12},{9,1},{1... | collective-permute-start | bytes 1622024 | tf_op jit(solution)/shard_map/ppermute | solution.py:44
  63.6 10.8 %copy-start.4 = (f32[1024,512]{1,0:T(8,128)S(1)}, f32[1024,512]{1,0:T(8,128)}, u32[]{:S(2)}) copy-start(f32[1024,512]{1,0:T(8,128)} %get-tuple-element.18) | copy-start | bytes 6291460
  63.7 10.7 %collective-permute-start.3 = (f16[528,512]{1,0:T(8,128)(2,1)S(1)}, f16[528,512]{1,0:T(8,128)(2,1)S(1)}, u32[]{:S(2)}, u32[]{:S(2)}) collective-permute-start(f16[528,512]{1,0:T(8,128)(2,1)S(1)} %pad_maximum_fusion), channel_id=1, source_target_pairs={{0,4},{1,9},{2,6},{3,11},{4,0},{5,13},{6,2},{7,15},{8,12},{9,1},{1... | collective-permute-start | bytes 1622024 | tf_op jit(solution)/shard_map/ppermute | solution.py:44
  66.4 35.6 %copy-start.13 = (f32[1,512]{1,0:T(1,128)}, f32[1,512]{1,0:T(1,128)S(1)}, u32[]{:S(2)}) copy-start(f32[1,512]{1,0:T(1,128)S(1)} %get-tuple-element.76.refs_3_) | copy-start | bytes 6148
  66.4 35.6 %copy-start.14 = (f32[1,512]{1,0:T(1,128)}, f32[1,512]{1,0:T(1,128)S(1)}, u32[]{:S(2)}) copy-start(f32[1,512]{1,0:T(1,128)S(1)} %get-tuple-element.83.refs_1_) | copy-start | bytes 6148
  75.4 6.6 %collective-permute-start.4 = (f16[272,512]{1,0:T(8,128)(2,1)S(1)}, f16[272,512]{1,0:T(8,128)(2,1)S(1)}, u32[]{:S(2)}, u32[]{:S(2)}) collective-permute-start(f16[272,512]{1,0:T(8,128)(2,1)S(1)} %pad_maximum_fusion.8), channel_id=1, source_target_pairs={{0,8},{1,5},{2,10},{3,7},{4,12},{5,1},{6,14},{7,3},{8,0},{9,13},{1... | collective-permute-start | bytes 835592 | tf_op jit(solution)/shard_map/ppermute | solution.py:44
  76.4 25.7 %copy-start = (f32[128,1024]{1,0:T(8,128)S(1)}, f32[128,1024]{1,0:T(8,128)}, u32[]{:S(2)}) copy-start(f32[128,1024]{1,0:T(8,128)} %param.7) | copy-start | bytes 1572868
  76.4 11.8 %collective-permute-start.10 = (f16[272,512]{1,0:T(8,128)(2,1)S(1)}, f16[272,512]{1,0:T(8,128)(2,1)S(1)}, u32[]{:S(2)}, u32[]{:S(2)}) collective-permute-start(f16[272,512]{1,0:T(8,128)(2,1)S(1)} %pad_maximum_fusion.9), channel_id=1, source_target_pairs={{0,8},{1,5},{2,10},{3,7},{4,12},{5,1},{6,14},{7,3},{8,0},{9,13},{1... | collective-permute-start | bytes 835592 | tf_op jit(solution)/shard_map/ppermute | solution.py:44
  88.2 12.2 %collective-permute-start.5 = (f16[144,512]{1,0:T(8,128)(2,1)S(1)}, f16[144,512]{1,0:T(8,128)(2,1)S(1)}, u32[]{:S(2)}, u32[]{:S(2)}) collective-permute-start(f16[144,512]{1,0:T(8,128)(2,1)S(1)} %pad_maximum_fusion.14), channel_id=1, source_target_pairs={{0,16},{1,17},{2,18},{3,19},{4,20},{5,21},{6,22},{7,23},{8,24},{9,... | collective-permute-start | bytes 442376 | tf_op jit(solution)/shard_map/ppermute | solution.py:44
  92.2 9.8 %collective-permute-start.11 = (f16[144,512]{1,0:T(8,128)(2,1)S(1)}, f16[144,512]{1,0:T(8,128)(2,1)S(1)}, u32[]{:S(2)}, u32[]{:S(2)}) collective-permute-start(f16[144,512]{1,0:T(8,128)(2,1)S(1)} %pad_maximum_fusion.15), channel_id=1, source_target_pairs={{0,16},{1,17},{2,18},{3,19},{4,20},{5,21},{6,22},{7,23},{8,24},{9,... | collective-permute-start | bytes 442376 | tf_op jit(solution)/shard_map/ppermute | solution.py:44
  100.4 21.7 %copy-start.11 = (f32[1,512]{1,0:T(1,128)}, f32[1,512]{1,0:T(1,128)S(1)}, u32[]{:S(2)}) copy-start(f32[1,512]{1,0:T(1,128)S(1)} %add_divide_fusion.1.refs_0_) | copy-start | bytes 6148
  102.0 20.1 %copy-start.12 = (f32[1,512]{1,0:T(1,128)}, f32[1,512]{1,0:T(1,128)S(1)}, u32[]{:S(2)}) copy-start(f32[1,512]{1,0:T(1,128)S(1)} %add_divide_fusion.refs_2_) | copy-start | bytes 6148
  102.4 4.6 %collective-permute-start.12 = (f32[3,512]{1,0:T(4,128)S(1)}, f32[3,512]{1,0:T(4,128)S(1)}, u32[]{:S(2)}, u32[]{:S(2)}) collective-permute-start(f32[3,512]{1,0:T(4,128)S(1)} %pad_maximum_fusion.16), channel_id=1, source_target_pairs={{0,16},{4,20},{8,24},{12,28},{16,0},{20,4},{24,8},{28,12},{1,17},{... | collective-permute-start | bytes 18440 | tf_op jit(solution)/shard_map/ppermute | solution.py:24
  102.5 5.9 %collective-permute-start.21 = (f16[128,512]{1,0:T(8,128)(2,1)S(1)}, f16[128,512]{1,0:T(8,128)(2,1)S(1)}, u32[]{:S(2)}, u32[]{:S(2)}) collective-permute-start(f16[128,512]{1,0:T(8,128)(2,1)S(1)} %get-tuple-element.42), channel_id=1, source_target_pairs={{0,16},{1,17},{2,18},{3,19},{4,20},{5,21},{6,22},{7,23},{8,24},{9,... | collective-permute-start | bytes 393224 | tf_op jit(solution)/shard_map/ppermute | solution.py:44
  107.1 32.4 %copy-start.10 = (bf16[512,512]{1,0:T(8,128)(2,1)S(1)}, bf16[512,512]{1,0:T(8,128)(2,1)}, u32[]{:S(2)}) copy-start(bf16[512,512]{1,0:T(8,128)(2,1)} %copy-done.9) | copy-start | bytes 1572868
  107.1 5.4 %collective-permute-start.13 = (f32[3,512]{1,0:T(4,128)S(1)}, f32[3,512]{1,0:T(4,128)S(1)}, u32[]{:S(2)}, u32[]{:S(2)}) collective-permute-start(f32[3,512]{1,0:T(4,128)S(1)} %fusion.29), channel_id=1, source_target_pairs={{0,8},{4,12},{8,0},{12,4},{16,24},{20,28},{24,16},{28,20},{1,9},{5... | collective-permute-start | bytes 18440 | tf_op jit(solution)/shard_map/ppermute | solution.py:24
  109.2 15.3 %collective-permute-start.22 = (f16[256,512]{1,0:T(8,128)(2,1)}, f16[256,512]{1,0:T(8,128)(2,1)S(1)}, u32[]{:S(2)}, u32[]{:S(2)}) collective-permute-start(f16[256,512]{1,0:T(8,128)(2,1)} %pad_maximum_fusion.13), channel_id=1, source_target_pairs={{0,8},{1,5},{2,10},{3,7},{4,12},{5,1},{6,14},{7,3},{8,0},{9,13},{1... | collective-permute-start | bytes 786440 | tf_op jit(solution)/shard_map/ppermute | solution.py:44
  112.5 3.7 %collective-permute-start.14 = (f32[3,512]{1,0:T(4,128)S(1)}, f32[3,512]{1,0:T(4,128)S(1)}, u32[]{:S(2)}, u32[]{:S(2)}) collective-permute-start(f32[3,512]{1,0:T(4,128)S(1)} %fusion.38), channel_id=1, source_target_pairs={{0,4},{4,0},{8,12},{12,8},{16,20},{20,16},{24,28},{28,24},{1,5},{5... | collective-permute-start | bytes 18440 | tf_op jit(solution)/shard_map/ppermute | solution.py:24
  116.3 3.7 %collective-permute-start.15 = (f32[3,512]{1,0:T(4,128)S(1)}, f32[3,512]{1,0:T(4,128)S(1)}, u32[]{:S(2)}, u32[]{:S(2)}) collective-permute-start(f32[3,512]{1,0:T(4,128)S(1)} %add.205), channel_id=1, source_target_pairs={{0,2},{1,3},{2,0},{3,1},{4,6},{5,7},{6,4},{7,5},{8,10},{9,11},{10,... | collective-permute-start | bytes 18440 | tf_op jit(solution)/shard_map/ppermute | solution.py:24
  119.9 1.6 collective-permute-start.16
  119.9 9.2 %collective-permute-start.17 = (f16[128,512]{1,0:T(8,128)(2,1)S(1)}, f16[128,512]{1,0:T(8,128)(2,1)S(1)}, u32[]{:S(2)}, u32[]{:S(2)}) collective-permute-start(f16[128,512]{1,0:T(8,128)(2,1)S(1)} %get-tuple-element.56), channel_id=1, source_target_pairs={{0,16},{1,17},{2,18},{3,19},{4,20},{5,21},{6,22},{7,23},{8,24},{9,... | collective-permute-start | bytes 393224 | tf_op jit(solution)/shard_map/ppermute | solution.py:44
  124.7 14.8 %collective-permute-start.23 = (f16[512,512]{1,0:T(8,128)(2,1)S(1)}, f16[512,512]{1,0:T(8,128)(2,1)S(1)}, u32[]{:S(2)}, u32[]{:S(2)}) collective-permute-start(f16[512,512]{1,0:T(8,128)(2,1)S(1)} %pad_maximum_fusion.5), channel_id=1, source_target_pairs={{0,4},{1,9},{2,6},{3,11},{4,0},{5,13},{6,2},{7,15},{8,12},{9,1},{1... | collective-permute-start | bytes 1572872 | tf_op jit(solution)/shard_map/ppermute | solution.py:44
  129.2 8.3 %collective-permute-start.18 = (f16[256,512]{1,0:T(8,128)(2,1)S(1)}, f16[256,512]{1,0:T(8,128)(2,1)S(1)}, u32[]{:S(2)}, u32[]{:S(2)}) collective-permute-start(f16[256,512]{1,0:T(8,128)(2,1)S(1)} %pad_maximum_fusion.12), channel_id=1, source_target_pairs={{0,8},{1,5},{2,10},{3,7},{4,12},{5,1},{6,14},{7,3},{8,0},{9,13},{1... | collective-permute-start | bytes 786440 | tf_op jit(solution)/shard_map/ppermute | solution.py:44
  137.6 17.6 %collective-permute-start.19 = (f16[512,512]{1,0:T(8,128)(2,1)S(1)}, f16[512,512]{1,0:T(8,128)(2,1)S(1)}, u32[]{:S(2)}, u32[]{:S(2)}) collective-permute-start(f16[512,512]{1,0:T(8,128)(2,1)S(1)} %pad_maximum_fusion.4), channel_id=1, source_target_pairs={{0,4},{1,9},{2,6},{3,11},{4,0},{5,13},{6,2},{7,15},{8,12},{9,1},{1... | collective-permute-start | bytes 1572872 | tf_op jit(solution)/shard_map/ppermute | solution.py:44
  140.9 14.2 %copy-start.8 = (bf16[512,512]{1,0:T(8,128)(2,1)S(1)}, bf16[512,512]{1,0:T(8,128)(2,1)}, u32[]{:S(2)}) copy-start(bf16[512,512]{1,0:T(8,128)(2,1)} %copy-done.7) | copy-start | bytes 1572868
  154.9 20.0 %collective-permute-start.24 = (f16[512,512]{1,0:T(8,128)(2,1)S(1)}, f16[512,512]{1,0:T(8,128)(2,1)S(1)}, u32[]{:S(2)}, u32[]{:S(2)}) collective-permute-start(f16[512,512]{1,0:T(8,128)(2,1)S(1)} %slice_convert_fusion), channel_id=1, source_target_pairs={{0,4},{1,9},{2,6},{3,11},{4,0},{5,13},{6,2},{7,15},{8,12},{9,1},{1... | collective-permute-start | bytes 1572872 | tf_op jit(solution)/shard_map/ppermute | solution.py:44
  156.5 19.4 %copy-start.1 = (f32[1024,512]{1,0:T(8,128)S(1)}, f32[1024,512]{1,0:T(8,128)}, u32[]{:S(2)}) copy-start(f32[1024,512]{1,0:T(8,128)} %get-tuple-element.23) | copy-start | bytes 6291460
  170.2 4.7 %collective-permute-start.25 = (f32[1,512]{1,0:T(1,128)S(1)}, f32[1,512]{1,0:T(1,128)S(1)}, u32[]{:S(2)}, u32[]{:S(2)}) collective-permute-start(f32[1,512]{1,0:T(1,128)S(1)} %get-tuple-element.71), channel_id=1, source_target_pairs={{0,16},{4,20},{8,24},{12,28},{16,0},{20,4},{24,8},{28,12},{1,17},{... | collective-permute-start | bytes 6152 | tf_op jit(solution)/shard_map/ppermute | solution.py:24
  172.1 12.5 %copy-start.2 = (f32[1024,512]{1,0:T(8,128)S(1)}, f32[1024,512]{1,0:T(8,128)}, u32[]{:S(2)}) copy-start(f32[1024,512]{1,0:T(8,128)} %get-tuple-element.22) | copy-start | bytes 6291460
  172.1 12.5 %collective-permute-start.20 = (f16[512,512]{1,0:T(8,128)(2,1)S(1)}, f16[512,512]{1,0:T(8,128)(2,1)S(1)}, u32[]{:S(2)}, u32[]{:S(2)}) collective-permute-start(f16[512,512]{1,0:T(8,128)(2,1)S(1)} %slice_convert_fusion.1), channel_id=1, source_target_pairs={{0,4},{1,9},{2,6},{3,11},{4,0},{5,13},{6,2},{7,15},{8,12},{9,1},{1... | collective-permute-start | bytes 1572872 | tf_op jit(solution)/shard_map/ppermute | solution.py:44
  174.9 3.7 %collective-permute-start.26 = (f32[1,512]{1,0:T(1,128)S(1)}, f32[1,512]{1,0:T(1,128)S(1)}, u32[]{:S(2)}, u32[]{:S(2)}) collective-permute-start(f32[1,512]{1,0:T(1,128)S(1)} %add.219), channel_id=1, source_target_pairs={{0,8},{4,12},{8,0},{12,4},{16,24},{20,28},{24,16},{28,20},{1,9},{5... | collective-permute-start | bytes 6152 | tf_op jit(solution)/shard_map/ppermute | solution.py:24
  176.2 13.1 %collective-permute-start.28 = (f16[256,512]{1,0:T(8,128)(2,1)S(1)}, f16[256,512]{1,0:T(8,128)(2,1)S(1)}, u32[]{:S(2)}, u32[]{:S(2)}) collective-permute-start(f16[256,512]{1,0:T(8,128)(2,1)S(1)} %slice_convert_fusion.4), channel_id=1, source_target_pairs={{0,8},{1,5},{2,10},{3,7},{4,12},{5,1},{6,14},{7,3},{8,0},{9,13},{1... | collective-permute-start | bytes 786440 | tf_op jit(solution)/shard_map/ppermute | solution.py:44
  184.7 4.6 %collective-permute-start.29 = (f32[1,512]{1,0:T(1,128)S(1)}, f32[1,512]{1,0:T(1,128)S(1)}, u32[]{:S(2)}, u32[]{:S(2)}) collective-permute-start(f32[1,512]{1,0:T(1,128)S(1)} %add.220), channel_id=1, source_target_pairs={{0,4},{4,0},{8,12},{12,8},{16,20},{20,16},{24,28},{28,24},{1,5},{5... | collective-permute-start | bytes 6152 | tf_op jit(solution)/shard_map/ppermute | solution.py:24
  187.3 6.4 %collective-permute-start.27 = (f16[256,512]{1,0:T(8,128)(2,1)S(1)}, f16[256,512]{1,0:T(8,128)(2,1)S(1)}, u32[]{:S(2)}, u32[]{:S(2)}) collective-permute-start(f16[256,512]{1,0:T(8,128)(2,1)S(1)} %slice_convert_fusion.5), channel_id=1, source_target_pairs={{0,8},{1,5},{2,10},{3,7},{4,12},{5,1},{6,14},{7,3},{8,0},{9,13},{1... | collective-permute-start | bytes 786440 | tf_op jit(solution)/shard_map/ppermute | solution.py:44
  189.4 3.7 %collective-permute-start.30 = (f32[1,512]{1,0:T(1,128)S(1)}, f32[1,512]{1,0:T(1,128)S(1)}, u32[]{:S(2)}, u32[]{:S(2)}) collective-permute-start(f32[1,512]{1,0:T(1,128)S(1)} %add.223), channel_id=1, source_target_pairs={{0,2},{1,3},{2,0},{3,1},{4,6},{5,7},{6,4},{7,5},{8,10},{9,11},{10,... | collective-permute-start | bytes 6152 | tf_op jit(solution)/shard_map/ppermute | solution.py:24
  190.9 7.5 %collective-permute-start.32 = (f16[128,512]{1,0:T(8,128)(2,1)S(1)}, f16[128,512]{1,0:T(8,128)(2,1)S(1)}, u32[]{:S(2)}, u32[]{:S(2)}) collective-permute-start(f16[128,512]{1,0:T(8,128)(2,1)S(1)} %slice_convert_fusion.9), channel_id=1, source_target_pairs={{0,16},{1,17},{2,18},{3,19},{4,20},{5,21},{6,22},{7,23},{8,24},{9,... | collective-permute-start | bytes 393224 | tf_op jit(solution)/shard_map/ppermute | solution.py:44
  193.8 1.6 collective-permute-start.31
  193.9 9.9 %collective-permute-start.33 = (f16[128,512]{1,0:T(8,128)(2,1)S(1)}, f16[128,512]{1,0:T(8,128)(2,1)S(1)}, u32[]{:S(2)}, u32[]{:S(2)}) collective-permute-start(f16[128,512]{1,0:T(8,128)(2,1)S(1)} %slice_convert_fusion.8), channel_id=1, source_target_pairs={{0,16},{1,17},{2,18},{3,19},{4,20},{5,21},{6,22},{7,23},{8,24},{9,... | collective-permute-start | bytes 393224 | tf_op jit(solution)/shard_map/ppermute | solution.py:44
  (3 other events, 6.7 us)

commit v3 on v2

--- a/solution.py
+++ b/solution.py
@@ -6,8 +6,8 @@
 from jax.sharding import PartitionSpec as P
 
 CHUNKS = 2
-TILE = 768
-VMEM_LIMIT = 56 * 2**20
+TILE = 1536
+VMEM_LIMIT = 28 * 2**20
 
 damp_coef = 0.5
 
@@ -141,6 +141,34 @@
 
 def bound_of(din):
     return FEATURE_MAX * FEATURE_MAX * CURVATURE_MAX * din
+
+
+def load_kernel(f_ref, c_ref, f_out, c_out, sems):
+    copies = [
+        pltpu.make_async_copy(f_ref, f_out, sems.at[0]),
+        pltpu.make_async_copy(c_ref, c_out, sems.at[1]),
+    ]
+    for copy in copies:
+        copy.start()
+    for copy in copies:
+        copy.wait()
+
+
+def load(features, curvature):
+    anywhere = pl.BlockSpec(memory_space=pl.ANY)
+    size = 4 * (features.size + curvature.size)
+    return pl.pallas_call(
+        load_kernel,
+        in_specs=[anywhere, anywhere],
+        out_specs=[anywhere, anywhere],
+        out_shape=[
+            jax.ShapeDtypeStruct(features.shape, features.dtype),
+            jax.ShapeDtypeStruct(curvature.shape, curvature.dtype),
+        ],
+        scratch_shapes=[pltpu.SemaphoreType.DMA((2,))],
+        compiler_params=pltpu.CompilerParams(vmem_limit_bytes=2**20),
+        cost_estimate=pl.CostEstimate(flops=0, bytes_accessed=size, transcendentals=0),
+    )(features, curvature)
 
 
 def curve(features, curvature, chunk, blocks, halves, n_dp):
@@ -196,11 +224,18 @@
         rows, stats = curve(features, curvature, k, blocks, halves, n_dp)
         return rows, stats
 
+    tie = lax.optimization_barrier
+
+    def in_step(moving):
+        arrived = tie([m[-1] for m in moving])
+        return [(*m[:-1], a) for m, a in zip(moving, arrived)]
+
     def hop():
         nonlocal dots
         if hops:
             dots = dots + swap(dots, *hops.pop(0))
 
+    features, curvature = load(features, curvature)
     grad = [task_grad[:, k * width : (k + 1) * width] for k in chunks]
 
     held = [g.astype(jnp.bfloat16) for g in grad]
@@ -220,6 +255,7 @@
             total, extra = scatter_end(*moving[k])
             if step:
                 moving[k] = scatter_start(total, extra, step - 1)
+                moving[k : k + 2] = in_step(moving[k : k + 2])
                 continue
             image[k] = total / (stats[k][2:3] * token_count) + damp_coef * grad[k]
             guess[k] = 1.0 / (extra * (bound / WIRE_MAX) + damp_coef)
@@ -227,6 +263,7 @@
             lift[k] = WIRE_MAX / reach
             trial = ((grad[k] - guess[k] * image[k]) * lift[k]).astype(WIRE)
             moving[k] = (trial, trade(trial, 0))
+            moving[k : k + 2] = in_step(moving[k : k + 2])
 
     dots = jnp.concatenate(
         [
@@ -237,13 +274,11 @@
     )
     all_hops = [(axis, stride) for axis in ("dp", "mp") for stride in strides_of(axis)]
     hops = list(all_hops)
-    per_step = -(-len(hops) // steps)
-    tie = lax.optimization_barrier
     for step in range(1, steps):
-        held = [join(pair) for pair in moving]
-        moving = [(h, trade(h, step)) for h in held]
-        for _ in range(per_step):
-            hop()
+        for k in chunks:
+            held = join(moving[k])
+            moving[k] = (held, trade(held, step))
+            moving[k : k + 2] = in_step(moving[k : k + 2])
     while hops:
         hop()
     coef = pl.pallas_call(

time: 207 us -> 184 us (0.89)
  Pallas kernels: 52.2 us -> 37.2 us
  waiting for transfers between devices: 78.8 us -> 63.9 us
  other arithmetic: 21.3 us -> 10.9 us
  local copies, waits for them, and re-layouts: 3.74 us -> 13.2 us
  starting transfers between devices: 48.6 us -> 57.1 us
    pallas_call x4, Pallas kernels: 50.7 us -> 34.8 us  [curve(): pl.pallas_call(lambda *refs: curve_kernel(*refs, n_dp=n_dp, token_count=n...]
    ppermute x24, waiting for transfers between devices: 69.5 us -> 54.1 us  [trade(): return lax.ppermute(values, ('dp', 'mp'), pairs)]
    unnamed x34 -> x30, local copies, waits for them, and re-layouts: 1.66 us -> 11.2 us
    another operation x12, other arithmetic: 5.51 us -> 0.62 us
    ppermute x24, starting transfers between devices: 38.9 us -> 43.6 us  [trade(): return lax.ppermute(values, ('dp', 'mp'), pairs)]
    ppermute x10, starting transfers between devices: 9.74 us -> 13.6 us  [swap(): return lax.ppermute(values, axis, [(i, i ^ stride) for i in range(size)])]
  transfers between devices with their start and end apart: 34 -> 34, of which waited for: 21 -> 20; matrix products, arithmetic and copies ran while one was open for 9% -> 5% of each run, Pallas kernels for 25% -> 20%
where the time goes in v3:
time: 184 us; the launch traced here: 183 us
  waiting for transfers between devices  63.9 us (35%)
  starting transfers between devices  57.1 us (31%)
  Pallas kernels  37.2 us (20%)
  local copies, waits for them, and re-layouts  13.2 us (7%)
  other arithmetic  10.9 us (6%)
    ppermute x24, waiting for transfers between devices, trade(): return lax.ppermute(values, ('dp', 'mp'), pairs)  54.1 us
    ppermute x24, starting transfers between devices, trade(): return lax.ppermute(values, ('dp', 'mp'), pairs)  43.6 us
    pallas_call x4, Pallas kernels, curve(): pl.pallas_call(lambda *refs: curve_kernel(*refs, n_dp=n_dp, token_count=n...  34.8 us
    ppermute x10, starting transfers between devices, swap(): return lax.ppermute(values, axis, [(i, i ^ stride) for i in range(size)])  13.6 us
    unnamed x30, local copies, waits for them, and re-layouts  11.2 us
    ppermute x10, waiting for transfers between devices, swap(): return lax.ppermute(values, axis, [(i, i ^ stride) for i in range(size)])  9.81 us
  transfers between devices with their start and end apart: 34, of which 20 were waited for; matrix products, arithmetic and copies ran while one was open for 5% of the time, Pallas kernels for 20%

profile of v3, /device:TPU:0, one launch (start us, length us, event | category | flops | bytes accessed | tf_op | source)
XLA Modules:
  0.0 183.5 jit_solution(17559182655417332258)
XLA Ops:
  0.6 1.1 fusion.22
  1.7 4.1 %collective-permute-start = (bf16[128,512]{1,0:T(8,128)(2,1)S(1)}, bf16[128,512]{1,0:T(8,128)(2,1)S(1)}, u32[]{:S(2)}, u32[]{:S(2)}) collective-permute-start(bf16[128,512]{1,0:T(8,128)(2,1)S(1)} %get-tuple-element.80), channel_id=1, source_target_pairs={{0,16},{1,17},{2,18},{3,19},{4,20},{5,21},{6,22},{7,23},{8,24},{9,... | collective-permute-start | bytes 393224 | tf_op jit(solution)/shard_map/ppermute | solution.py:44
  5.8 6.3 %collective-permute-done = bf16[128,512]{1,0:T(8,128)(2,1)S(1)} collective-permute-done((bf16[128,512]{1,0:T(8,128)(2,1)S(1)}, bf16[128,512]{1,0:T(8,128)(2,1)S(1)}, u32[]{:S(2)}, u32[]{:S(2)}) %collective-permute-start) | collective-permute-done | bytes 131104 | tf_op jit(solution)/shard_map/ppermute | solution.py:44
  12.9 3.4 %collective-permute-start.5 = (bf16[128,512]{1,0:T(8,128)(2,1)S(1)}, bf16[128,512]{1,0:T(8,128)(2,1)S(1)}, u32[]{:S(2)}, u32[]{:S(2)}) collective-permute-start(bf16[128,512]{1,0:T(8,128)(2,1)S(1)} %get-tuple-element.81), channel_id=1, source_target_pairs={{0,16},{1,17},{2,18},{3,19},{4,20},{5,21},{6,22},{7,23},{8,24},{9,... | collective-permute-start | bytes 393224 | tf_op jit(solution)/shard_map/ppermute | solution.py:44
  16.3 6.2 %collective-permute-done.1 = bf16[256,512]{1,0:T(8,128)(2,1)S(1)} collective-permute-done((bf16[256,512]{1,0:T(8,128)(2,1)S(1)}, bf16[256,512]{1,0:T(8,128)(2,1)S(1)}, u32[]{:S(2)}, u32[]{:S(2)}) %collective-permute-start.1) | collective-permute-done | bytes 262176 | tf_op jit(solution)/shard_map/ppermute | solution.py:44
  24.1 2.8 %copy-done = bf16[3072,1024]{1,0:T(8,128)(2,1)S(1)} copy-done((bf16[3072,1024]{1,0:T(8,128)(2,1)S(1)}, bf16[3072,1024]{1,0:T(8,128)(2,1)}, u32[]{:S(2)}) %copy-start) | copy-done | bytes 6291480
  26.9 2.8 %copy-done.1 = bf16[3072,1024]{1,0:T(8,128)(2,1)S(1)} copy-done((bf16[3072,1024]{1,0:T(8,128)(2,1)S(1)}, bf16[3072,1024]{1,0:T(8,128)(2,1)}, u32[]{:S(2)}) %copy-start.1) | copy-done | bytes 6291480
  31.8 8.7 %shard_map.69 = (f32[1024,512]{1,0:T(8,128)S(1)}, f32[8,512]{1,0:T(8,128)S(1)}) custom-call(s32[8]{0:T(128)S(1)} %fusion.16.refs_0_, bf16[3072,1024]{1,0:T(8,128)(2,1)S(1)} %get-tuple-element.30.refs_1_, bf16[3072,1024]{1,0:T(8,128)(2,1)S(1)} %get-tuple-element.31.refs_2_, bf16[512,512]{1,0:T(8,128)(2,1)S(1)} %pad_maximum_fusion.2.refs_3_, ...), custom_call_target="tpu_custom_call" | custom-call | flops 6442450944 | bytes 12582912 | tf_op jit(solution)/shard_map/pallas_call | solution.py:181
  40.7 1.1 collective-permute-start.3
  41.8 8.7 %shard_map.70 = (f32[1024,512]{1,0:T(8,128)S(1)}, f32[8,512]{1,0:T(8,128)S(1)}) custom-call(s32[8]{0:T(128)S(1)} %fusion.16.refs_0_, bf16[3072,1024]{1,0:T(8,128)(2,1)S(1)} %get-tuple-element.30.refs_1_, bf16[3072,1024]{1,0:T(8,128)(2,1)S(1)} %get-tuple-element.31.refs_2_, bf16[512,512]{1,0:T(8,128)(2,1)S(1)} %pad_maximum_fusion.3.refs_3_, ...), custom_call_target="tpu_custom_call" | custom-call | flops 6442450944 | bytes 12582912 | tf_op jit(solution)/shard_map/pallas_call | solution.py:181
  52.2 1.7 collective-permute-start.4
  53.9 7.9 %collective-permute-done.8 = f16[528,512]{1,0:T(8,128)(2,1)S(1)} collective-permute-done((f16[528,512]{1,0:T(8,128)(2,1)S(1)}, f16[528,512]{1,0:T(8,128)(2,1)S(1)}, u32[]{:S(2)}, u32[]{:S(2)}) %collective-permute-start.8) | collective-permute-done | bytes 540704 | tf_op jit(solution)/shard_map/ppermute | solution.py:44
  62.8 4.9 %collective-permute-start.9 = (f16[144,512]{1,0:T(8,128)(2,1)S(1)}, f16[144,512]{1,0:T(8,128)(2,1)S(1)}, u32[]{:S(2)}, u32[]{:S(2)}) collective-permute-start(f16[144,512]{1,0:T(8,128)(2,1)S(1)} %pad_maximum_fusion.14), channel_id=1, source_target_pairs={{0,16},{1,17},{2,18},{3,19},{4,20},{5,21},{6,22},{7,23},{8,24},{9,... | collective-permute-start | bytes 442376 | tf_op jit(solution)/shard_map/ppermute | solution.py:44
  67.6 2.0 %collective-permute-done.10 = f16[272,512]{1,0:T(8,128)(2,1)S(1)} collective-permute-done((f16[272,512]{1,0:T(8,128)(2,1)S(1)}, f16[272,512]{1,0:T(8,128)(2,1)S(1)}, u32[]{:S(2)}, u32[]{:S(2)}) %collective-permute-start.10) | collective-permute-done | bytes 278560 | tf_op jit(solution)/shard_map/ppermute | solution.py:44
  69.6 5.4 %collective-permute-done.9 = f16[144,512]{1,0:T(8,128)(2,1)S(1)} collective-permute-done((f16[144,512]{1,0:T(8,128)(2,1)S(1)}, f16[144,512]{1,0:T(8,128)(2,1)S(1)}, u32[]{:S(2)}, u32[]{:S(2)}) %collective-permute-start.9) | collective-permute-done | bytes 147488 | tf_op jit(solution)/shard_map/ppermute | solution.py:44
  76.0 2.4 %collective-permute-start.12 = (f16[144,512]{1,0:T(8,128)(2,1)S(1)}, f16[144,512]{1,0:T(8,128)(2,1)S(1)}, u32[]{:S(2)}, u32[]{:S(2)}) collective-permute-start(f16[144,512]{1,0:T(8,128)(2,1)S(1)} %pad_maximum_fusion.15), channel_id=1, source_target_pairs={{0,16},{1,17},{2,18},{3,19},{4,20},{5,21},{6,22},{7,23},{8,24},{9,... | collective-permute-start | bytes 442376 | tf_op jit(solution)/shard_map/ppermute | solution.py:44
  78.4 5.8 %collective-permute-done.12 = f16[144,512]{1,0:T(8,128)(2,1)S(1)} collective-permute-done((f16[144,512]{1,0:T(8,128)(2,1)S(1)}, f16[144,512]{1,0:T(8,128)(2,1)S(1)}, u32[]{:S(2)}, u32[]{:S(2)}) %collective-permute-start.12) | collective-permute-done | bytes 147488 | tf_op jit(solution)/shard_map/ppermute | solution.py:44
  85.7 4.4 %collective-permute-start.18 = (f16[256,512]{1,0:T(8,128)(2,1)}, f16[256,512]{1,0:T(8,128)(2,1)}, u32[]{:S(2)}, u32[]{:S(2)}) collective-permute-start(f16[256,512]{1,0:T(8,128)(2,1)} %pad_maximum_fusion.12), channel_id=1, source_target_pairs={{0,8},{1,5},{2,10},{3,7},{4,12},{5,1},{6,14},{7,3},{8,0},{9,13},{1... | collective-permute-start | bytes 786440 | tf_op jit(solution)/shard_map/ppermute | solution.py:44
  90.2 1.5 collective-permute-start.14
  91.7 2.3 %collective-permute-start.19 = (f16[128,512]{1,0:T(8,128)(2,1)S(1)}, f16[128,512]{1,0:T(8,128)(2,1)S(1)}, u32[]{:S(2)}, u32[]{:S(2)}) collective-permute-start(f16[128,512]{1,0:T(8,128)(2,1)S(1)} %get-tuple-element.66), channel_id=1, source_target_pairs={{0,16},{1,17},{2,18},{3,19},{4,20},{5,21},{6,22},{7,23},{8,24},{9,... | collective-permute-start | bytes 393224 | tf_op jit(solution)/shard_map/ppermute | solution.py:44
  95.0 3.6 %collective-permute-done.15 = f32[3,512]{1,0:T(4,128)S(1)} collective-permute-done((f32[3,512]{1,0:T(4,128)S(1)}, f32[3,512]{1,0:T(4,128)S(1)}, u32[]{:S(2)}, u32[]{:S(2)}) %collective-permute-start.15) | collective-permute-done | bytes 6176 | tf_op jit(solution)/shard_map/ppermute | solution.py:24
  98.6 3.5 %collective-permute-start.16 = (f32[3,512]{1,0:T(4,128)S(1)}, f32[3,512]{1,0:T(4,128)S(1)}, u32[]{:S(2)}, u32[]{:S(2)}) collective-permute-start(f32[3,512]{1,0:T(4,128)S(1)} %add.207), channel_id=1, source_target_pairs={{0,2},{1,3},{2,0},{3,1},{4,6},{5,7},{6,4},{7,5},{8,10},{9,11},{10,... | collective-permute-start | bytes 18440 | tf_op jit(solution)/shard_map/ppermute | solution.py:24
  102.0 1.6 collective-permute-done.16
  103.7 1.2 collective-permute-done.17
  105.5 1.5 shard_map.71
  107.0 1.1 pad_maximum_fusion.4
  108.1 2.1 %collective-permute-start.20 = (f16[512,512]{1,0:T(8,128)(2,1)S(1)}, f16[512,512]{1,0:T(8,128)(2,1)S(1)}, u32[]{:S(2)}, u32[]{:S(2)}) collective-permute-start(f16[512,512]{1,0:T(8,128)(2,1)S(1)} %pad_maximum_fusion.4), channel_id=1, source_target_pairs={{0,4},{1,9},{2,6},{3,11},{4,0},{5,13},{6,2},{7,15},{8,12},{9,1},{1... | collective-permute-start | bytes 1572872 | tf_op jit(solution)/shard_map/ppermute | solution.py:44
  111.2 2.1 %collective-permute-start.21 = (f16[256,512]{1,0:T(8,128)(2,1)S(1)}, f16[256,512]{1,0:T(8,128)(2,1)S(1)}, u32[]{:S(2)}, u32[]{:S(2)}) collective-permute-start(f16[256,512]{1,0:T(8,128)(2,1)S(1)} %pad_maximum_fusion.13), channel_id=1, source_target_pairs={{0,8},{1,5},{2,10},{3,7},{4,12},{5,1},{6,14},{7,3},{8,0},{9,13},{1... | collective-permute-start | bytes 786440 | tf_op jit(solution)/shard_map/ppermute | solution.py:44
  113.5 6.2 %collective-permute-done.21 = f16[256,512]{1,0:T(8,128)(2,1)S(1)} collective-permute-done((f16[256,512]{1,0:T(8,128)(2,1)S(1)}, f16[256,512]{1,0:T(8,128)(2,1)S(1)}, u32[]{:S(2)}, u32[]{:S(2)}) %collective-permute-start.21) | collective-permute-done | bytes 262176 | tf_op jit(solution)/shard_map/ppermute | solution.py:44
  120.3 2.1 %collective-permute-start.22 = (f16[512,512]{1,0:T(8,128)(2,1)S(1)}, f16[512,512]{1,0:T(8,128)(2,1)S(1)}, u32[]{:S(2)}, u32[]{:S(2)}) collective-permute-start(f16[512,512]{1,0:T(8,128)(2,1)S(1)} %pad_maximum_fusion.5), channel_id=1, source_target_pairs={{0,4},{1,9},{2,6},{3,11},{4,0},{5,13},{6,2},{7,15},{8,12},{9,1},{1... | collective-permute-start | bytes 1572872 | tf_op jit(solution)/shard_map/ppermute | solution.py:44
  122.4 1.4 add_convert_fusion
  123.8 2.8 %copy-done.3 = bf16[3072,1024]{1,0:T(8,128)(2,1)S(1)} copy-done((bf16[3072,1024]{1,0:T(8,128)(2,1)S(1)}, bf16[3072,1024]{1,0:T(8,128)(2,1)}, u32[]{:S(2)}) %copy-start.3) | copy-done | bytes 6291480
  126.6 2.8 %copy-done.5 = bf16[3072,1024]{1,0:T(8,128)(2,1)S(1)} copy-done((bf16[3072,1024]{1,0:T(8,128)(2,1)S(1)}, bf16[3072,1024]{1,0:T(8,128)(2,1)}, u32[]{:S(2)}) %copy-start.5) | copy-done | bytes 6291480
  129.4 8.8 %shard_map.73 = (f32[1024,512]{1,0:T(8,128)S(1)}, f32[8,512]{1,0:T(8,128)S(1)}) custom-call(s32[8]{0:T(128)S(1)} %fusion.16.refs_0_, bf16[3072,1024]{1,0:T(8,128)(2,1)S(1)} %copy-done.3, bf16[3072,1024]{1,0:T(8,128)(2,1)S(1)} %copy-done.5, bf16[512,512]{1,0:T(8,128)(2,1)S(1)} %get-tuple-element.100.refs_3_, bf16[512,512]{1,0:T(8,128)(2,1)S(1)} %get-tuple-element.99.refs_4_), custom_call_target="tpu_custom_call" | custom-call | flops 6442450944 | bytes 12582912 | tf_op jit(solution)/shard_map/pallas_call | solution.py:181
  138.8 8.6 %shard_map.72 = (f32[1024,512]{1,0:T(8,128)S(1)}, f32[8,512]{1,0:T(8,128)S(1)}) custom-call(s32[8]{0:T(128)S(1)} %fusion.16.refs_0_, bf16[3072,1024]{1,0:T(8,128)(2,1)S(1)} %copy-done.3, bf16[3072,1024]{1,0:T(8,128)(2,1)S(1)} %copy-done.5, bf16[512,512]{1,0:T(8,128)(2,1)S(1)} %get-tuple-element.102.refs_3_, bf16[512,512]{1,0:T(8,128)(2,1)S(1)} %get-tuple-element.101.refs_4_), custom_call_target="tpu_custom_call" | custom-call | flops 6442450944 | bytes 12582912 | tf_op jit(solution)/shard_map/pallas_call | solution.py:181
  147.5 1.5 collective-permute-start.25
  149.1 2.1 %collective-permute-start.23 = (f16[512,512]{1,0:T(8,128)(2,1)S(1)}, f16[512,512]{1,0:T(8,128)(2,1)S(1)}, u32[]{:S(2)}, u32[]{:S(2)}) collective-permute-start(f16[512,512]{1,0:T(8,128)(2,1)S(1)} %slice_convert_fusion.1), channel_id=1, source_target_pairs={{0,4},{1,9},{2,6},{3,11},{4,0},{5,13},{6,2},{7,15},{8,12},{9,1},{1... | collective-permute-start | bytes 1572872 | tf_op jit(solution)/shard_map/ppermute | solution.py:44
  152.1 2.1 %collective-permute-start.26 = (f32[1,512]{1,0:T(1,128)S(1)}, f32[1,512]{1,0:T(1,128)S(1)}, u32[]{:S(2)}, u32[]{:S(2)}) collective-permute-start(f32[1,512]{1,0:T(1,128)S(1)} %add.219), channel_id=1, source_target_pairs={{0,8},{4,12},{8,0},{12,4},{16,24},{20,28},{24,16},{28,20},{1,9},{5... | collective-permute-start | bytes 6152 | tf_op jit(solution)/shard_map/ppermute | solution.py:24
  154.5 1.3 collective-permute-done.26
  155.8 5.9 %collective-permute-done.23 = f16[512,512]{1,0:T(8,128)(2,1)S(1)} collective-permute-done((f16[512,512]{1,0:T(8,128)(2,1)S(1)}, f16[512,512]{1,0:T(8,128)(2,1)S(1)}, u32[]{:S(2)}, u32[]{:S(2)}) %collective-permute-start.23) | collective-permute-done | bytes 524320 | tf_op jit(solution)/shard_map/ppermute | solution.py:44
  161.7 2.5 %collective-permute-start.29 = (f32[1,512]{1,0:T(1,128)S(1)}, f32[1,512]{1,0:T(1,128)S(1)}, u32[]{:S(2)}, u32[]{:S(2)}) collective-permute-start(f32[1,512]{1,0:T(1,128)S(1)} %add.220), channel_id=1, source_target_pairs={{0,4},{4,0},{8,12},{12,8},{16,20},{20,16},{24,28},{28,24},{1,5},{5... | collective-permute-start | bytes 6152 | tf_op jit(solution)/shard_map/ppermute | solution.py:24
  164.4 2.6 %collective-permute-start.27 = (f16[256,512]{1,0:T(8,128)(2,1)S(1)}, f16[256,512]{1,0:T(8,128)(2,1)S(1)}, u32[]{:S(2)}, u32[]{:S(2)}) collective-permute-start(f16[256,512]{1,0:T(8,128)(2,1)S(1)} %slice_convert_fusion.5), channel_id=1, source_target_pairs={{0,8},{1,5},{2,10},{3,7},{4,12},{5,1},{6,14},{7,3},{8,0},{9,13},{1... | collective-permute-start | bytes 786440 | tf_op jit(solution)/shard_map/ppermute | solution.py:44
  167.1 2.1 %collective-permute-start.30 = (f32[1,512]{1,0:T(1,128)S(1)}, f32[1,512]{1,0:T(1,128)S(1)}, u32[]{:S(2)}, u32[]{:S(2)}) collective-permute-start(f32[1,512]{1,0:T(1,128)S(1)} %add.223), channel_id=1, source_target_pairs={{0,2},{1,3},{2,0},{3,1},{4,6},{5,7},{6,4},{7,5},{8,10},{9,11},{10,... | collective-permute-start | bytes 6152 | tf_op jit(solution)/shard_map/ppermute | solution.py:24
  169.2 1.2 collective-permute-start.32
  171.5 1.8 %collective-permute-start.33 = (f16[128,512]{1,0:T(8,128)(2,1)S(1)}, f16[128,512]{1,0:T(8,128)(2,1)S(1)}, u32[]{:S(2)}, u32[]{:S(2)}) collective-permute-start(f16[128,512]{1,0:T(8,128)(2,1)S(1)} %slice_convert_fusion.8), channel_id=1, source_target_pairs={{0,16},{1,17},{2,18},{3,19},{4,20},{5,21},{6,22},{7,23},{8,24},{9,... | collective-permute-start | bytes 393224 | tf_op jit(solution)/shard_map/ppermute | solution.py:44
  173.9 1.4 slice_divide_fusion.1
  175.3 1.8 collective-permute-done.32
  177.1 5.1 %collective-permute-done.33 = f16[128,512]{1,0:T(8,128)(2,1)S(1)} collective-permute-done((f16[128,512]{1,0:T(8,128)(2,1)S(1)}, f16[128,512]{1,0:T(8,128)(2,1)S(1)}, u32[]{:S(2)}, u32[]{:S(2)}) %collective-permute-start.33) | collective-permute-done | bytes 131104 | tf_op jit(solution)/shard_map/ppermute | solution.py:44
  (134 shorter events, 18.4 us)
Async XLA Ops:
  1.7 10.4 %collective-permute-start = (bf16[128,512]{1,0:T(8,128)(2,1)S(1)}, bf16[128,512]{1,0:T(8,128)(2,1)S(1)}, u32[]{:S(2)}, u32[]{:S(2)}) collective-permute-start(bf16[128,512]{1,0:T(8,128)(2,1)S(1)} %get-tuple-element.80), channel_id=1, source_target_pairs={{0,16},{1,17},{2,18},{3,19},{4,20},{5,21},{6,22},{7,23},{8,24},{9,... | collective-permute-start | bytes 393224 | tf_op jit(solution)/shard_map/ppermute | solution.py:44
  12.1 10.4 %collective-permute-start.1 = (bf16[256,512]{1,0:T(8,128)(2,1)S(1)}, bf16[256,512]{1,0:T(8,128)(2,1)S(1)}, u32[]{:S(2)}, u32[]{:S(2)}) collective-permute-start(bf16[256,512]{1,0:T(8,128)(2,1)S(1)} %pad_maximum_fusion.10), channel_id=1, source_target_pairs={{0,8},{1,5},{2,10},{3,7},{4,12},{5,1},{6,14},{7,3},{8,0},{9,13},{1... | collective-permute-start | bytes 786440 | tf_op jit(solution)/shard_map/ppermute | solution.py:44
  12.9 10.2 %collective-permute-start.5 = (bf16[128,512]{1,0:T(8,128)(2,1)S(1)}, bf16[128,512]{1,0:T(8,128)(2,1)S(1)}, u32[]{:S(2)}, u32[]{:S(2)}) collective-permute-start(bf16[128,512]{1,0:T(8,128)(2,1)S(1)} %get-tuple-element.81), channel_id=1, source_target_pairs={{0,16},{1,17},{2,18},{3,19},{4,20},{5,21},{6,22},{7,23},{8,24},{9,... | collective-permute-start | bytes 393224 | tf_op jit(solution)/shard_map/ppermute | solution.py:44
  22.5 8.1 %copy-start.7 = (bf16[256,512]{1,0:T(8,128)(2,1)}, bf16[256,512]{1,0:T(8,128)(2,1)S(1)}, u32[]{:S(2)}) copy-start(bf16[256,512]{1,0:T(8,128)(2,1)S(1)} %collective-permute-done.1) | copy-start | bytes 786436
  22.5 9.2 %collective-permute-start.2 = (bf16[512,512]{1,0:T(8,128)(2,1)S(1)}, bf16[512,512]{1,0:T(8,128)(2,1)S(1)}, u32[]{:S(2)}, u32[]{:S(2)}) collective-permute-start(bf16[512,512]{1,0:T(8,128)(2,1)S(1)} %pad_maximum_fusion.2.refs_3_), channel_id=1, source_target_pairs={{0,4},{1,9},{2,6},{3,11},{4,0},{5,13},{6,2},{7,15},{8,12},{9,1},{1... | collective-permute-start | bytes 1572872 | tf_op jit(solution)/shard_map/ppermute | solution.py:44
  23.2 7.5 %collective-permute-start.6 = (bf16[256,512]{1,0:T(8,128)(2,1)S(1)}, bf16[256,512]{1,0:T(8,128)(2,1)S(1)}, u32[]{:S(2)}, u32[]{:S(2)}) collective-permute-start(bf16[256,512]{1,0:T(8,128)(2,1)S(1)} %pad_maximum_fusion.11), channel_id=1, source_target_pairs={{0,8},{1,5},{2,10},{3,7},{4,12},{5,1},{6,14},{7,3},{8,0},{9,13},{1... | collective-permute-start | bytes 786440 | tf_op jit(solution)/shard_map/ppermute | solution.py:44
  24.1 2.8 %copy-start = (bf16[3072,1024]{1,0:T(8,128)(2,1)S(1)}, bf16[3072,1024]{1,0:T(8,128)(2,1)}, u32[]{:S(2)}) copy-start(bf16[3072,1024]{1,0:T(8,128)(2,1)} %f_ref.1) | copy-start | bytes 18874372
  26.9 2.8 %copy-start.1 = (bf16[3072,1024]{1,0:T(8,128)(2,1)S(1)}, bf16[3072,1024]{1,0:T(8,128)(2,1)}, u32[]{:S(2)}) copy-start(bf16[3072,1024]{1,0:T(8,128)(2,1)} %c_ref.1) | copy-start | bytes 18874372
  29.7 0.9 copy-start.14
  30.6 11.2 %copy-start.2 = (bf16[3072,1024]{1,0:T(8,128)(2,1)}, bf16[3072,1024]{1,0:T(8,128)(2,1)S(1)}, u32[]{:S(2)}) copy-start(bf16[3072,1024]{1,0:T(8,128)(2,1)S(1)} %get-tuple-element.30.refs_1_) | copy-start | bytes 18874372
  30.6 11.2 %copy-start.4 = (bf16[3072,1024]{1,0:T(8,128)(2,1)}, bf16[3072,1024]{1,0:T(8,128)(2,1)S(1)}, u32[]{:S(2)}) copy-start(bf16[3072,1024]{1,0:T(8,128)(2,1)S(1)} %get-tuple-element.31.refs_2_) | copy-start | bytes 18874372
  30.7 11.1 %collective-permute-start.7 = (bf16[512,512]{1,0:T(8,128)(2,1)S(1)}, bf16[512,512]{1,0:T(8,128)(2,1)S(1)}, u32[]{:S(2)}, u32[]{:S(2)}) collective-permute-start(bf16[512,512]{1,0:T(8,128)(2,1)S(1)} %pad_maximum_fusion.3.refs_3_), channel_id=1, source_target_pairs={{0,4},{1,9},{2,6},{3,11},{4,0},{5,13},{6,2},{7,15},{8,12},{9,1},{1... | collective-permute-start | bytes 1572872 | tf_op jit(solution)/shard_map/ppermute | solution.py:44
  40.7 11.1 %collective-permute-start.3 = (f16[528,512]{1,0:T(8,128)(2,1)S(1)}, f16[528,512]{1,0:T(8,128)(2,1)S(1)}, u32[]{:S(2)}, u32[]{:S(2)}) collective-permute-start(f16[528,512]{1,0:T(8,128)(2,1)S(1)} %pad_maximum_fusion), channel_id=1, source_target_pairs={{0,4},{1,9},{2,6},{3,11},{4,0},{5,13},{6,2},{7,15},{8,12},{9,1},{1... | collective-permute-start | bytes 1622024 | tf_op jit(solution)/shard_map/ppermute | solution.py:44
  50.8 11.0 %collective-permute-start.8 = (f16[528,512]{1,0:T(8,128)(2,1)S(1)}, f16[528,512]{1,0:T(8,128)(2,1)S(1)}, u32[]{:S(2)}, u32[]{:S(2)}) collective-permute-start(f16[528,512]{1,0:T(8,128)(2,1)S(1)} %pad_maximum_fusion.1), channel_id=1, source_target_pairs={{0,4},{1,9},{2,6},{3,11},{4,0},{5,13},{6,2},{7,15},{8,12},{9,1},{1... | collective-permute-start | bytes 1622024 | tf_op jit(solution)/shard_map/ppermute | solution.py:44
  52.2 9.6 %collective-permute-start.4 = (f16[272,512]{1,0:T(8,128)(2,1)S(1)}, f16[272,512]{1,0:T(8,128)(2,1)S(1)}, u32[]{:S(2)}, u32[]{:S(2)}) collective-permute-start(f16[272,512]{1,0:T(8,128)(2,1)S(1)} %pad_maximum_fusion.8), channel_id=1, source_target_pairs={{0,8},{1,5},{2,10},{3,7},{4,12},{5,1},{6,14},{7,3},{8,0},{9,13},{1... | collective-permute-start | bytes 835592 | tf_op jit(solution)/shard_map/ppermute | solution.py:44
  62.0 13.0 %copy-start.6 = (f32[128,1024]{1,0:T(8,128)S(1)}, f32[128,1024]{1,0:T(8,128)}, u32[]{:S(2)}) copy-start(f32[128,1024]{1,0:T(8,128)} %param.7) | copy-start | bytes 1572868
  62.3 7.3 %collective-permute-start.10 = (f16[272,512]{1,0:T(8,128)(2,1)S(1)}, f16[272,512]{1,0:T(8,128)(2,1)S(1)}, u32[]{:S(2)}, u32[]{:S(2)}) collective-permute-start(f16[272,512]{1,0:T(8,128)(2,1)S(1)} %pad_maximum_fusion.9), channel_id=1, source_target_pairs={{0,8},{1,5},{2,10},{3,7},{4,12},{5,1},{6,14},{7,3},{8,0},{9,13},{1... | collective-permute-start | bytes 835592 | tf_op jit(solution)/shard_map/ppermute | solution.py:44
  62.8 12.2 %collective-permute-start.9 = (f16[144,512]{1,0:T(8,128)(2,1)S(1)}, f16[144,512]{1,0:T(8,128)(2,1)S(1)}, u32[]{:S(2)}, u32[]{:S(2)}) collective-permute-start(f16[144,512]{1,0:T(8,128)(2,1)S(1)} %pad_maximum_fusion.14), channel_id=1, source_target_pairs={{0,16},{1,17},{2,18},{3,19},{4,20},{5,21},{6,22},{7,23},{8,24},{9,... | collective-permute-start | bytes 442376 | tf_op jit(solution)/shard_map/ppermute | solution.py:44
  67.6 16.9 %copy-start.9 = (f32[1,512]{1,0:T(1,128)}, f32[1,512]{1,0:T(1,128)S(1)}, u32[]{:S(2)}) copy-start(f32[1,512]{1,0:T(1,128)S(1)} %get-tuple-element.98.refs_1_) | copy-start | bytes 6148
  75.0 9.6 %copy-start.10 = (f32[1,512]{1,0:T(1,128)}, f32[1,512]{1,0:T(1,128)S(1)}, u32[]{:S(2)}) copy-start(f32[1,512]{1,0:T(1,128)S(1)} %add_divide_fusion.1.refs_0_) | copy-start | bytes 6148
  75.1 9.1 %collective-permute-start.11 = (f16[128,512]{1,0:T(8,128)(2,1)S(1)}, f16[128,512]{1,0:T(8,128)(2,1)S(1)}, u32[]{:S(2)}, u32[]{:S(2)}) collective-permute-start(f16[128,512]{1,0:T(8,128)(2,1)S(1)} %get-tuple-element.68), channel_id=1, source_target_pairs={{0,16},{1,17},{2,18},{3,19},{4,20},{5,21},{6,22},{7,23},{8,24},{9,... | collective-permute-start | bytes 393224 | tf_op jit(solution)/shard_map/ppermute | solution.py:44
  76.0 8.2 %collective-permute-start.12 = (f16[144,512]{1,0:T(8,128)(2,1)S(1)}, f16[144,512]{1,0:T(8,128)(2,1)S(1)}, u32[]{:S(2)}, u32[]{:S(2)}) collective-permute-start(f16[144,512]{1,0:T(8,128)(2,1)S(1)} %pad_maximum_fusion.15), channel_id=1, source_target_pairs={{0,16},{1,17},{2,18},{3,19},{4,20},{5,21},{6,22},{7,23},{8,24},{9,... | collective-permute-start | bytes 442376 | tf_op jit(solution)/shard_map/ppermute | solution.py:44
  78.4 27.1 %copy-start.11 = (f32[1,512]{1,0:T(1,128)}, f32[1,512]{1,0:T(1,128)S(1)}, u32[]{:S(2)}) copy-start(f32[1,512]{1,0:T(1,128)S(1)} %get-tuple-element.96.refs_3_) | copy-start | bytes 6148
  84.3 21.2 %copy-start.12 = (f32[1,512]{1,0:T(1,128)}, f32[1,512]{1,0:T(1,128)S(1)}, u32[]{:S(2)}) copy-start(f32[1,512]{1,0:T(1,128)S(1)} %add_divide_fusion.refs_2_) | copy-start | bytes 6148
  84.6 5.6 %collective-permute-start.13 = (f32[3,512]{1,0:T(4,128)S(1)}, f32[3,512]{1,0:T(4,128)S(1)}, u32[]{:S(2)}, u32[]{:S(2)}) collective-permute-start(f32[3,512]{1,0:T(4,128)S(1)} %pad_maximum_fusion.16), channel_id=1, source_target_pairs={{0,16},{4,20},{8,24},{12,28},{16,0},{20,4},{24,8},{28,12},{1,17},{... | collective-permute-start | bytes 18440 | tf_op jit(solution)/shard_map/ppermute | solution.py:24
  85.7 21.3 %collective-permute-start.18 = (f16[256,512]{1,0:T(8,128)(2,1)}, f16[256,512]{1,0:T(8,128)(2,1)}, u32[]{:S(2)}, u32[]{:S(2)}) collective-permute-start(f16[256,512]{1,0:T(8,128)(2,1)} %pad_maximum_fusion.12), channel_id=1, source_target_pairs={{0,8},{1,5},{2,10},{3,7},{4,12},{5,1},{6,14},{7,3},{8,0},{9,13},{1... | collective-permute-start | bytes 786440 | tf_op jit(solution)/shard_map/ppermute | solution.py:44
  90.2 4.6 %collective-permute-start.14 = (f32[3,512]{1,0:T(4,128)S(1)}, f32[3,512]{1,0:T(4,128)S(1)}, u32[]{:S(2)}, u32[]{:S(2)}) collective-permute-start(f32[3,512]{1,0:T(4,128)S(1)} %fusion.17), channel_id=1, source_target_pairs={{0,8},{4,12},{8,0},{12,4},{16,24},{20,28},{24,16},{28,20},{1,9},{5... | collective-permute-start | bytes 18440 | tf_op jit(solution)/shard_map/ppermute | solution.py:24
  91.7 15.3 %collective-permute-start.19 = (f16[128,512]{1,0:T(8,128)(2,1)S(1)}, f16[128,512]{1,0:T(8,128)(2,1)S(1)}, u32[]{:S(2)}, u32[]{:S(2)}) collective-permute-start(f16[128,512]{1,0:T(8,128)(2,1)S(1)} %get-tuple-element.66), channel_id=1, source_target_pairs={{0,16},{1,17},{2,18},{3,19},{4,20},{5,21},{6,22},{7,23},{8,24},{9,... | collective-permute-start | bytes 393224 | tf_op jit(solution)/shard_map/ppermute | solution.py:44
  94.8 3.7 %collective-permute-start.15 = (f32[3,512]{1,0:T(4,128)S(1)}, f32[3,512]{1,0:T(4,128)S(1)}, u32[]{:S(2)}, u32[]{:S(2)}) collective-permute-start(f32[3,512]{1,0:T(4,128)S(1)} %fusion.24), channel_id=1, source_target_pairs={{0,4},{4,0},{8,12},{12,8},{16,20},{20,16},{24,28},{28,24},{1,5},{5... | collective-permute-start | bytes 18440 | tf_op jit(solution)/shard_map/ppermute | solution.py:24
  98.6 5.1 %collective-permute-start.16 = (f32[3,512]{1,0:T(4,128)S(1)}, f32[3,512]{1,0:T(4,128)S(1)}, u32[]{:S(2)}, u32[]{:S(2)}) collective-permute-start(f32[3,512]{1,0:T(4,128)S(1)} %add.207), channel_id=1, source_target_pairs={{0,2},{1,3},{2,0},{3,1},{4,6},{5,7},{6,4},{7,5},{8,10},{9,11},{10,... | collective-permute-start | bytes 18440 | tf_op jit(solution)/shard_map/ppermute | solution.py:24
  103.7 1.2 collective-permute-start.17
  107.0 15.4 %copy-start.8 = (bf16[256,512]{1,0:T(8,128)(2,1)S(1)}, bf16[256,512]{1,0:T(8,128)(2,1)}, u32[]{:S(2)}) copy-start(bf16[256,512]{1,0:T(8,128)(2,1)} %copy-done.7) | copy-start | bytes 786436
  108.1 12.1 %collective-permute-start.20 = (f16[512,512]{1,0:T(8,128)(2,1)S(1)}, f16[512,512]{1,0:T(8,128)(2,1)S(1)}, u32[]{:S(2)}, u32[]{:S(2)}) collective-permute-start(f16[512,512]{1,0:T(8,128)(2,1)S(1)} %pad_maximum_fusion.4), channel_id=1, source_target_pairs={{0,4},{1,9},{2,6},{3,11},{4,0},{5,13},{6,2},{7,15},{8,12},{9,1},{1... | collective-permute-start | bytes 1572872 | tf_op jit(solution)/shard_map/ppermute | solution.py:44
  111.2 8.4 %collective-permute-start.21 = (f16[256,512]{1,0:T(8,128)(2,1)S(1)}, f16[256,512]{1,0:T(8,128)(2,1)S(1)}, u32[]{:S(2)}, u32[]{:S(2)}) collective-permute-start(f16[256,512]{1,0:T(8,128)(2,1)S(1)} %pad_maximum_fusion.13), channel_id=1, source_target_pairs={{0,8},{1,5},{2,10},{3,7},{4,12},{5,1},{6,14},{7,3},{8,0},{9,13},{1... | collective-permute-start | bytes 786440 | tf_op jit(solution)/shard_map/ppermute | solution.py:44
  120.3 18.1 %collective-permute-start.22 = (f16[512,512]{1,0:T(8,128)(2,1)S(1)}, f16[512,512]{1,0:T(8,128)(2,1)S(1)}, u32[]{:S(2)}, u32[]{:S(2)}) collective-permute-start(f16[512,512]{1,0:T(8,128)(2,1)S(1)} %pad_maximum_fusion.5), channel_id=1, source_target_pairs={{0,4},{1,9},{2,6},{3,11},{4,0},{5,13},{6,2},{7,15},{8,12},{9,1},{1... | collective-permute-start | bytes 1572872 | tf_op jit(solution)/shard_map/ppermute | solution.py:44
  123.8 2.8 %copy-start.3 = (bf16[3072,1024]{1,0:T(8,128)(2,1)S(1)}, bf16[3072,1024]{1,0:T(8,128)(2,1)}, u32[]{:S(2)}) copy-start(bf16[3072,1024]{1,0:T(8,128)(2,1)} %copy-done.2) | copy-start | bytes 18874372
  126.6 2.8 %copy-start.5 = (bf16[3072,1024]{1,0:T(8,128)(2,1)S(1)}, bf16[3072,1024]{1,0:T(8,128)(2,1)}, u32[]{:S(2)}) copy-start(bf16[3072,1024]{1,0:T(8,128)(2,1)} %copy-done.4) | copy-start | bytes 18874372
  138.3 13.9 %collective-permute-start.24 = (f16[512,512]{1,0:T(8,128)(2,1)S(1)}, f16[512,512]{1,0:T(8,128)(2,1)S(1)}, u32[]{:S(2)}, u32[]{:S(2)}) collective-permute-start(f16[512,512]{1,0:T(8,128)(2,1)S(1)} %slice_convert_fusion), channel_id=1, source_target_pairs={{0,4},{1,9},{2,6},{3,11},{4,0},{5,13},{6,2},{7,15},{8,12},{9,1},{1... | collective-permute-start | bytes 1572872 | tf_op jit(solution)/shard_map/ppermute | solution.py:44
  147.5 4.7 %collective-permute-start.25 = (f32[1,512]{1,0:T(1,128)S(1)}, f32[1,512]{1,0:T(1,128)S(1)}, u32[]{:S(2)}, u32[]{:S(2)}) collective-permute-start(f32[1,512]{1,0:T(1,128)S(1)} %get-tuple-element.93), channel_id=1, source_target_pairs={{0,16},{4,20},{8,24},{12,28},{16,0},{20,4},{24,8},{28,12},{1,17},{... | collective-permute-start | bytes 6152 | tf_op jit(solution)/shard_map/ppermute | solution.py:24
  149.1 12.7 %collective-permute-start.23 = (f16[512,512]{1,0:T(8,128)(2,1)S(1)}, f16[512,512]{1,0:T(8,128)(2,1)S(1)}, u32[]{:S(2)}, u32[]{:S(2)}) collective-permute-start(f16[512,512]{1,0:T(8,128)(2,1)S(1)} %slice_convert_fusion.1), channel_id=1, source_target_pairs={{0,4},{1,9},{2,6},{3,11},{4,0},{5,13},{6,2},{7,15},{8,12},{9,1},{1... | collective-permute-start | bytes 1572872 | tf_op jit(solution)/shard_map/ppermute | solution.py:44
  152.1 3.7 %collective-permute-start.26 = (f32[1,512]{1,0:T(1,128)S(1)}, f32[1,512]{1,0:T(1,128)S(1)}, u32[]{:S(2)}, u32[]{:S(2)}) collective-permute-start(f32[1,512]{1,0:T(1,128)S(1)} %add.219), channel_id=1, source_target_pairs={{0,8},{4,12},{8,0},{12,4},{16,24},{20,28},{24,16},{28,20},{1,9},{5... | collective-permute-start | bytes 6152 | tf_op jit(solution)/shard_map/ppermute | solution.py:24
  154.4 12.6 %collective-permute-start.28 = (f16[256,512]{1,0:T(8,128)(2,1)S(1)}, f16[256,512]{1,0:T(8,128)(2,1)S(1)}, u32[]{:S(2)}, u32[]{:S(2)}) collective-permute-start(f16[256,512]{1,0:T(8,128)(2,1)S(1)} %slice_convert_fusion.4), channel_id=1, source_target_pairs={{0,8},{1,5},{2,10},{3,7},{4,12},{5,1},{6,14},{7,3},{8,0},{9,13},{1... | collective-permute-start | bytes 786440 | tf_op jit(solution)/shard_map/ppermute | solution.py:44
  161.7 5.3 %collective-permute-start.29 = (f32[1,512]{1,0:T(1,128)S(1)}, f32[1,512]{1,0:T(1,128)S(1)}, u32[]{:S(2)}, u32[]{:S(2)}) collective-permute-start(f32[1,512]{1,0:T(1,128)S(1)} %add.220), channel_id=1, source_target_pairs={{0,4},{4,0},{8,12},{12,8},{16,20},{20,16},{24,28},{28,24},{1,5},{5... | collective-permute-start | bytes 6152 | tf_op jit(solution)/shard_map/ppermute | solution.py:24
  164.4 6.9 %collective-permute-start.27 = (f16[256,512]{1,0:T(8,128)(2,1)S(1)}, f16[256,512]{1,0:T(8,128)(2,1)S(1)}, u32[]{:S(2)}, u32[]{:S(2)}) collective-permute-start(f16[256,512]{1,0:T(8,128)(2,1)S(1)} %slice_convert_fusion.5), channel_id=1, source_target_pairs={{0,8},{1,5},{2,10},{3,7},{4,12},{5,1},{6,14},{7,3},{8,0},{9,13},{1... | collective-permute-start | bytes 786440 | tf_op jit(solution)/shard_map/ppermute | solution.py:44
  167.1 3.7 %collective-permute-start.30 = (f32[1,512]{1,0:T(1,128)S(1)}, f32[1,512]{1,0:T(1,128)S(1)}, u32[]{:S(2)}, u32[]{:S(2)}) collective-permute-start(f32[1,512]{1,0:T(1,128)S(1)} %add.223), channel_id=1, source_target_pairs={{0,2},{1,3},{2,0},{3,1},{4,6},{5,7},{6,4},{7,5},{8,10},{9,11},{10,... | collective-permute-start | bytes 6152 | tf_op jit(solution)/shard_map/ppermute | solution.py:24
  169.2 7.9 %collective-permute-start.32 = (f16[128,512]{1,0:T(8,128)(2,1)S(1)}, f16[128,512]{1,0:T(8,128)(2,1)S(1)}, u32[]{:S(2)}, u32[]{:S(2)}) collective-permute-start(f16[128,512]{1,0:T(8,128)(2,1)S(1)} %slice_convert_fusion.9), channel_id=1, source_target_pairs={{0,16},{1,17},{2,18},{3,19},{4,20},{5,21},{6,22},{7,23},{8,24},{9,... | collective-permute-start | bytes 393224 | tf_op jit(solution)/shard_map/ppermute | solution.py:44
  171.4 2.0 %collective-permute-start.31 = (f32[1,512]{1,0:T(1,128)S(1)}, f32[1,512]{1,0:T(1,128)S(1)}, u32[]{:S(2)}, u32[]{:S(2)}) collective-permute-start(f32[1,512]{1,0:T(1,128)S(1)} %add.224), channel_id=1, source_target_pairs={{0,1},{1,0},{2,3},{3,2},{4,5},{5,4},{6,7},{7,6},{8,9},{9,8},{10,11... | collective-permute-start | bytes 6152 | tf_op jit(solution)/shard_map/ppermute | solution.py:24
  171.5 10.7 %collective-permute-start.33 = (f16[128,512]{1,0:T(8,128)(2,1)S(1)}, f16[128,512]{1,0:T(8,128)(2,1)S(1)}, u32[]{:S(2)}, u32[]{:S(2)}) collective-permute-start(f16[128,512]{1,0:T(8,128)(2,1)S(1)} %slice_convert_fusion.8), channel_id=1, source_target_pairs={{0,16},{1,17},{2,18},{3,19},{4,20},{5,21},{6,22},{7,23},{8,24},{9,... | collective-permute-start | bytes 393224 | tf_op jit(solution)/shard_map/ppermute | solution.py:44
  (1 other events, 0.9 us)

commit v4 on v3

--- a/solution.py
+++ b/solution.py
@@ -272,13 +272,17 @@
             sum(colsum(image[k] * image[k]) for k in chunks),
         ]
     )
-    all_hops = [(axis, stride) for axis in ("dp", "mp") for stride in strides_of(axis)]
+    all_hops = [(axis, stride) for axis in ("mp", "dp") for stride in reversed(strides_of(axis))]
     hops = list(all_hops)
     for step in range(1, steps):
         for k in chunks:
             held = join(moving[k])
             moving[k] = (held, trade(held, step))
             moving[k : k + 2] = in_step(moving[k : k + 2])
+    for _ in range(3):
+        hop()
+    arrived, dots = tie((moving[0][-1], dots))
+    moving[0] = (*moving[0][:-1], arrived)
     while hops:
         hop()
     coef = pl.pallas_call(

time: 184 us -> 180 us (0.978)
  starting transfers between devices: 57.1 us -> 50.7 us
  local copies, waits for them, and re-layouts: 13.2 us -> 15.1 us
    ppermute x24, starting transfers between devices: 43.6 us -> 36.8 us  [trade(): return lax.ppermute(values, ('dp', 'mp'), pairs)]
    ppermute x24, waiting for transfers between devices: 54.1 us -> 49.9 us  [trade(): return lax.ppermute(values, ('dp', 'mp'), pairs)]
    ppermute x10, waiting for transfers between devices: 9.81 us -> 13.8 us  [swap(): return lax.ppermute(values, axis, [(i, i ^ stride) for i in range(size)])]
    unnamed x30 -> x36, local copies, waits for them, and re-layouts: 11.2 us -> 13 us
  transfers between devices with their start and end apart: 34 -> 34, of which waited for: 20 -> 17; matrix products, arithmetic and copies ran while one was open for 5% -> 6% of each run, Pallas kernels for 20% -> 21%
where the time goes in v4:
time: 180 us; the launch traced here: 179 us
  waiting for transfers between devices  63.8 us (35%)
  starting transfers between devices  50.7 us (28%)
  Pallas kernels  37.1 us (21%)
  local copies, waits for them, and re-layouts  15.1 us (8%)
  other arithmetic  11.2 us (6%)
    ppermute x24, waiting for transfers between devices, trade(): return lax.ppermute(values, ('dp', 'mp'), pairs)  49.9 us
    ppermute x24, starting transfers between devices, trade(): return lax.ppermute(values, ('dp', 'mp'), pairs)  36.8 us
    pallas_call x4, Pallas kernels, curve(): pl.pallas_call(lambda *refs: curve_kernel(*refs, n_dp=n_dp, token_count=n...  34.7 us
    ppermute x10, starting transfers between devices, swap(): return lax.ppermute(values, axis, [(i, i ^ stride) for i in range(size)])  13.9 us
    ppermute x10, waiting for transfers between devices, swap(): return lax.ppermute(values, axis, [(i, i ^ stride) for i in range(size)])  13.8 us
    unnamed x36, local copies, waits for them, and re-layouts  13 us
  transfers between devices with their start and end apart: 34, of which 17 were waited for; matrix products, arithmetic and copies ran while one was open for 6% of the time, Pallas kernels for 21%

profile of v4, /device:TPU:0, one launch (start us, length us, event | category | flops | bytes accessed | tf_op | source)
XLA Modules:
  0.0 179.0 jit_solution(8928189687539515251)
XLA Ops:
  1.7 4.1 %collective-permute-start = (bf16[128,512]{1,0:T(8,128)(2,1)S(1)}, bf16[128,512]{1,0:T(8,128)(2,1)S(1)}, u32[]{:S(2)}, u32[]{:S(2)}) collective-permute-start(bf16[128,512]{1,0:T(8,128)(2,1)S(1)} %get-tuple-element.84), channel_id=1, source_target_pairs={{0,16},{1,17},{2,18},{3,19},{4,20},{5,21},{6,22},{7,23},{8,24},{9,... | collective-permute-start | bytes 393224 | tf_op jit(solution)/shard_map/ppermute | solution.py:44
  5.8 6.3 %collective-permute-done = bf16[128,512]{1,0:T(8,128)(2,1)S(1)} collective-permute-done((bf16[128,512]{1,0:T(8,128)(2,1)S(1)}, bf16[128,512]{1,0:T(8,128)(2,1)S(1)}, u32[]{:S(2)}, u32[]{:S(2)}) %collective-permute-start) | collective-permute-done | bytes 131104 | tf_op jit(solution)/shard_map/ppermute | solution.py:44
  12.9 3.4 %collective-permute-start.5 = (bf16[128,512]{1,0:T(8,128)(2,1)S(1)}, bf16[128,512]{1,0:T(8,128)(2,1)S(1)}, u32[]{:S(2)}, u32[]{:S(2)}) collective-permute-start(bf16[128,512]{1,0:T(8,128)(2,1)S(1)} %get-tuple-element.83), channel_id=1, source_target_pairs={{0,16},{1,17},{2,18},{3,19},{4,20},{5,21},{6,22},{7,23},{8,24},{9,... | collective-permute-start | bytes 393224 | tf_op jit(solution)/shard_map/ppermute | solution.py:44
  16.3 6.2 %collective-permute-done.1 = bf16[256,512]{1,0:T(8,128)(2,1)S(1)} collective-permute-done((bf16[256,512]{1,0:T(8,128)(2,1)S(1)}, bf16[256,512]{1,0:T(8,128)(2,1)S(1)}, u32[]{:S(2)}, u32[]{:S(2)}) %collective-permute-start.1) | collective-permute-done | bytes 262176 | tf_op jit(solution)/shard_map/ppermute | solution.py:44
  24.1 2.8 %copy-done = bf16[3072,1024]{1,0:T(8,128)(2,1)S(1)} copy-done((bf16[3072,1024]{1,0:T(8,128)(2,1)S(1)}, bf16[3072,1024]{1,0:T(8,128)(2,1)}, u32[]{:S(2)}) %copy-start) | copy-done | bytes 6291480
  26.9 2.8 %copy-done.1 = bf16[3072,1024]{1,0:T(8,128)(2,1)S(1)} copy-done((bf16[3072,1024]{1,0:T(8,128)(2,1)S(1)}, bf16[3072,1024]{1,0:T(8,128)(2,1)}, u32[]{:S(2)}) %copy-start.1) | copy-done | bytes 6291480
  31.8 8.6 %shard_map.69 = (f32[1024,512]{1,0:T(8,128)S(1)}, f32[8,512]{1,0:T(8,128)S(1)}) custom-call(s32[8]{0:T(128)S(1)} %fusion.16.refs_0_, bf16[3072,1024]{1,0:T(8,128)(2,1)S(1)} %get-tuple-element.32.refs_1_, bf16[3072,1024]{1,0:T(8,128)(2,1)S(1)} %get-tuple-element.33.refs_2_, bf16[512,512]{1,0:T(8,128)(2,1)S(1)} %pad_maximum_fusion.2.refs_3_, ...), custom_call_target="tpu_custom_call" | custom-call | flops 6442450944 | bytes 12582912 | tf_op jit(solution)/shard_map/pallas_call | solution.py:181
  40.7 1.1 collective-permute-start.3
  41.8 8.6 %shard_map.70 = (f32[1024,512]{1,0:T(8,128)S(1)}, f32[8,512]{1,0:T(8,128)S(1)}) custom-call(s32[8]{0:T(128)S(1)} %fusion.16.refs_0_, bf16[3072,1024]{1,0:T(8,128)(2,1)S(1)} %get-tuple-element.32.refs_1_, bf16[3072,1024]{1,0:T(8,128)(2,1)S(1)} %get-tuple-element.33.refs_2_, bf16[512,512]{1,0:T(8,128)(2,1)S(1)} %pad_maximum_fusion.3.refs_3_, ...), custom_call_target="tpu_custom_call" | custom-call | flops 6442450944 | bytes 12582912 | tf_op jit(solution)/shard_map/pallas_call | solution.py:181
  50.7 1.1 collective-permute-start.8
  52.1 1.6 collective-permute-start.4
  53.8 7.9 %collective-permute-done.8 = f16[528,512]{1,0:T(8,128)(2,1)S(1)} collective-permute-done((f16[528,512]{1,0:T(8,128)(2,1)S(1)}, f16[528,512]{1,0:T(8,128)(2,1)S(1)}, u32[]{:S(2)}, u32[]{:S(2)}) %collective-permute-start.8) | collective-permute-done | bytes 540704 | tf_op jit(solution)/shard_map/ppermute | solution.py:44
  62.8 4.8 %collective-permute-start.9 = (f16[144,512]{1,0:T(8,128)(2,1)S(1)}, f16[144,512]{1,0:T(8,128)(2,1)S(1)}, u32[]{:S(2)}, u32[]{:S(2)}) collective-permute-start(f16[144,512]{1,0:T(8,128)(2,1)S(1)} %pad_maximum_fusion.14), channel_id=1, source_target_pairs={{0,16},{1,17},{2,18},{3,19},{4,20},{5,21},{6,22},{7,23},{8,24},{9,... | collective-permute-start | bytes 442376 | tf_op jit(solution)/shard_map/ppermute | solution.py:44
  67.6 1.7 collective-permute-done.10
  69.3 5.5 %collective-permute-done.9 = f16[144,512]{1,0:T(8,128)(2,1)S(1)} collective-permute-done((f16[144,512]{1,0:T(8,128)(2,1)S(1)}, f16[144,512]{1,0:T(8,128)(2,1)S(1)}, u32[]{:S(2)}, u32[]{:S(2)}) %collective-permute-start.9) | collective-permute-done | bytes 147488 | tf_op jit(solution)/shard_map/ppermute | solution.py:44
  76.0 2.2 %collective-permute-start.12 = (f16[144,512]{1,0:T(8,128)(2,1)S(1)}, f16[144,512]{1,0:T(8,128)(2,1)S(1)}, u32[]{:S(2)}, u32[]{:S(2)}) collective-permute-start(f16[144,512]{1,0:T(8,128)(2,1)S(1)} %pad_maximum_fusion.15), channel_id=1, source_target_pairs={{0,16},{1,17},{2,18},{3,19},{4,20},{5,21},{6,22},{7,23},{8,24},{9,... | collective-permute-start | bytes 442376 | tf_op jit(solution)/shard_map/ppermute | solution.py:44
  78.2 9.8 %collective-permute-done.12 = f16[144,512]{1,0:T(8,128)(2,1)S(1)} collective-permute-done((f16[144,512]{1,0:T(8,128)(2,1)S(1)}, f16[144,512]{1,0:T(8,128)(2,1)S(1)}, u32[]{:S(2)}, u32[]{:S(2)}) %collective-permute-start.12) | collective-permute-done | bytes 147488 | tf_op jit(solution)/shard_map/ppermute | solution.py:44
  88.5 2.5 %collective-permute-start.14 = (f16[128,512]{1,0:T(8,128)(2,1)S(1)}, f16[128,512]{1,0:T(8,128)(2,1)S(1)}, u32[]{:S(2)}, u32[]{:S(2)}) collective-permute-start(f16[128,512]{1,0:T(8,128)(2,1)S(1)} %multiply_convert_fusion), channel_id=1, source_target_pairs={{0,16},{1,17},{2,18},{3,19},{4,20},{5,21},{6,22},{7,23},{8,24},{9,... | collective-permute-start | bytes 393224 | tf_op jit(solution)/shard_map/ppermute | solution.py:44
  91.1 3.5 %collective-permute-done.14 = f16[128,512]{1,0:T(8,128)(2,1)S(1)} collective-permute-done((f16[128,512]{1,0:T(8,128)(2,1)S(1)}, f16[128,512]{1,0:T(8,128)(2,1)S(1)}, u32[]{:S(2)}, u32[]{:S(2)}) %collective-permute-start.14) | collective-permute-done | bytes 131104 | tf_op jit(solution)/shard_map/ppermute | solution.py:44
  94.6 2.2 %collective-permute-done.13 = f16[256,512]{1,0:T(8,128)(2,1)S(1)} collective-permute-done((f16[256,512]{1,0:T(8,128)(2,1)S(1)}, f16[256,512]{1,0:T(8,128)(2,1)S(1)}, u32[]{:S(2)}, u32[]{:S(2)}) %collective-permute-start.13) | collective-permute-done | bytes 262176 | tf_op jit(solution)/shard_map/ppermute | solution.py:44
  97.8 2.0 %collective-permute-start.16 = (f16[256,512]{1,0:T(8,128)(2,1)S(1)}, f16[256,512]{1,0:T(8,128)(2,1)S(1)}, u32[]{:S(2)}, u32[]{:S(2)}) collective-permute-start(f16[256,512]{1,0:T(8,128)(2,1)S(1)} %pad_maximum_fusion.13), channel_id=1, source_target_pairs={{0,8},{1,5},{2,10},{3,7},{4,12},{5,1},{6,14},{7,3},{8,0},{9,13},{1... | collective-permute-start | bytes 786440 | tf_op jit(solution)/shard_map/ppermute | solution.py:44
  99.8 2.3 %collective-permute-start.18 = (f32[3,512]{1,0:T(4,128)S(1)}, f32[3,512]{1,0:T(4,128)S(1)}, u32[]{:S(2)}, u32[]{:S(2)}) collective-permute-start(f32[3,512]{1,0:T(4,128)S(1)} %fusion.17), channel_id=1, source_target_pairs={{0,2},{1,3},{2,0},{3,1},{4,6},{5,7},{6,4},{7,5},{8,10},{9,11},{10,... | collective-permute-start | bytes 18440 | tf_op jit(solution)/shard_map/ppermute | solution.py:24
  102.1 1.6 collective-permute-done.18
  104.0 3.5 %collective-permute-done.19 = f32[3,512]{1,0:T(4,128)S(1)} collective-permute-done((f32[3,512]{1,0:T(4,128)S(1)}, f32[3,512]{1,0:T(4,128)S(1)}, u32[]{:S(2)}, u32[]{:S(2)}) %collective-permute-start.19) | collective-permute-done | bytes 6176 | tf_op jit(solution)/shard_map/ppermute | solution.py:24
  108.4 2.0 %collective-permute-start.20 = (f32[3,512]{1,0:T(4,128)S(1)}, f32[3,512]{1,0:T(4,128)S(1)}, u32[]{:S(2)}, u32[]{:S(2)}) collective-permute-start(f32[3,512]{1,0:T(4,128)S(1)} %add.209), channel_id=1, source_target_pairs={{0,8},{4,12},{8,0},{12,4},{16,24},{20,28},{24,16},{28,20},{1,9},{5... | collective-permute-start | bytes 18440 | tf_op jit(solution)/shard_map/ppermute | solution.py:24
  110.4 1.8 %collective-permute-done.20 = f32[3,512]{1,0:T(4,128)S(1)} collective-permute-done((f32[3,512]{1,0:T(4,128)S(1)}, f32[3,512]{1,0:T(4,128)S(1)}, u32[]{:S(2)}, u32[]{:S(2)}) %collective-permute-start.20) | collective-permute-done | bytes 6176 | tf_op jit(solution)/shard_map/ppermute | solution.py:24
  112.2 2.0 %collective-permute-start.21 = (f32[3,512]{1,0:T(4,128)S(1)}, f32[3,512]{1,0:T(4,128)S(1)}, u32[]{:S(2)}, u32[]{:S(2)}) collective-permute-start(f32[3,512]{1,0:T(4,128)S(1)} %add.210), channel_id=1, source_target_pairs={{0,16},{4,20},{8,24},{12,28},{16,0},{20,4},{24,8},{28,12},{1,17},{... | collective-permute-start | bytes 18440 | tf_op jit(solution)/shard_map/ppermute | solution.py:24
  115.3 1.4 collective-permute-done.21
  117.3 1.5 shard_map.71
  119.8 1.6 add_convert_fusion
  121.4 2.8 %copy-done.3 = bf16[3072,1024]{1,0:T(8,128)(2,1)S(1)} copy-done((bf16[3072,1024]{1,0:T(8,128)(2,1)S(1)}, bf16[3072,1024]{1,0:T(8,128)(2,1)}, u32[]{:S(2)}) %copy-start.3) | copy-done | bytes 6291480
  124.2 2.8 %copy-done.5 = bf16[3072,1024]{1,0:T(8,128)(2,1)S(1)} copy-done((bf16[3072,1024]{1,0:T(8,128)(2,1)S(1)}, bf16[3072,1024]{1,0:T(8,128)(2,1)}, u32[]{:S(2)}) %copy-start.5) | copy-done | bytes 6291480
  127.0 8.8 %shard_map.73 = (f32[1024,512]{1,0:T(8,128)S(1)}, f32[8,512]{1,0:T(8,128)S(1)}) custom-call(s32[8]{0:T(128)S(1)} %fusion.16.refs_0_, bf16[3072,1024]{1,0:T(8,128)(2,1)S(1)} %copy-done.3, bf16[3072,1024]{1,0:T(8,128)(2,1)S(1)} %copy-done.5, bf16[512,512]{1,0:T(8,128)(2,1)S(1)} %get-tuple-element.103.refs_3_, bf16[512,512]{1,0:T(8,128)(2,1)S(1)} %get-tuple-element.102.refs_4_), custom_call_target="tpu_custom_call" | custom-call | flops 6442450944 | bytes 12582912 | tf_op jit(solution)/shard_map/pallas_call | solution.py:181
  136.8 1.5 add_convert_fusion.2
  138.2 8.6 %shard_map.72 = (f32[1024,512]{1,0:T(8,128)S(1)}, f32[8,512]{1,0:T(8,128)S(1)}) custom-call(s32[8]{0:T(128)S(1)} %fusion.16.refs_0_, bf16[3072,1024]{1,0:T(8,128)(2,1)S(1)} %copy-done.3, bf16[3072,1024]{1,0:T(8,128)(2,1)S(1)} %copy-done.5, bf16[512,512]{1,0:T(8,128)(2,1)S(1)} %get-tuple-element.105.refs_3_, bf16[512,512]{1,0:T(8,128)(2,1)S(1)} %get-tuple-element.104.refs_4_), custom_call_target="tpu_custom_call" | custom-call | flops 6442450944 | bytes 12582912 | tf_op jit(solution)/shard_map/pallas_call | solution.py:181
  147.1 1.5 collective-permute-start.23
  148.6 2.7 %collective-permute-start.26 = (f32[1,512]{1,0:T(1,128)S(1)}, f32[1,512]{1,0:T(1,128)S(1)}, u32[]{:S(2)}, u32[]{:S(2)}) collective-permute-start(f32[1,512]{1,0:T(1,128)S(1)} %add.219), channel_id=1, source_target_pairs={{0,2},{1,3},{2,0},{3,1},{4,6},{5,7},{6,4},{7,5},{8,10},{9,11},{10,... | collective-permute-start | bytes 6152 | tf_op jit(solution)/shard_map/ppermute | solution.py:24
  151.5 1.5 collective-permute-start.28
  153.0 5.5 %collective-permute-done.23 = f16[512,512]{1,0:T(8,128)(2,1)S(1)} collective-permute-done((f16[512,512]{1,0:T(8,128)(2,1)S(1)}, f16[512,512]{1,0:T(8,128)(2,1)S(1)}, u32[]{:S(2)}, u32[]{:S(2)}) %collective-permute-start.23) | collective-permute-done | bytes 524320 | tf_op jit(solution)/shard_map/ppermute | solution.py:44
  158.5 1.4 collective-permute-start.29
  160.2 2.7 %collective-permute-start.27 = (f16[256,512]{1,0:T(8,128)(2,1)S(1)}, f16[256,512]{1,0:T(8,128)(2,1)S(1)}, u32[]{:S(2)}, u32[]{:S(2)}) collective-permute-start(f16[256,512]{1,0:T(8,128)(2,1)S(1)} %slice_convert_fusion.5), channel_id=1, source_target_pairs={{0,8},{1,5},{2,10},{3,7},{4,12},{5,1},{6,14},{7,3},{8,0},{9,13},{1... | collective-permute-start | bytes 786440 | tf_op jit(solution)/shard_map/ppermute | solution.py:44
  163.0 1.9 %collective-permute-start.30 = (f32[1,512]{1,0:T(1,128)S(1)}, f32[1,512]{1,0:T(1,128)S(1)}, u32[]{:S(2)}, u32[]{:S(2)}) collective-permute-start(f32[1,512]{1,0:T(1,128)S(1)} %add.223), channel_id=1, source_target_pairs={{0,8},{4,12},{8,0},{12,4},{16,24},{20,28},{24,16},{28,20},{1,9},{5... | collective-permute-start | bytes 6152 | tf_op jit(solution)/shard_map/ppermute | solution.py:24
  164.9 1.3 collective-permute-start.32
  166.2 2.5 %collective-permute-done.30 = f32[1,512]{1,0:T(1,128)S(1)} collective-permute-done((f32[1,512]{1,0:T(1,128)S(1)}, f32[1,512]{1,0:T(1,128)S(1)}, u32[]{:S(2)}, u32[]{:S(2)}) %collective-permute-start.30) | collective-permute-done | bytes 2080 | tf_op jit(solution)/shard_map/ppermute | solution.py:24
  168.7 1.2 collective-permute-start.31
  169.9 1.9 %collective-permute-start.33 = (f16[128,512]{1,0:T(8,128)(2,1)S(1)}, f16[128,512]{1,0:T(8,128)(2,1)S(1)}, u32[]{:S(2)}, u32[]{:S(2)}) collective-permute-start(f16[128,512]{1,0:T(8,128)(2,1)S(1)} %slice_convert_fusion.8), channel_id=1, source_target_pairs={{0,16},{1,17},{2,18},{3,19},{4,20},{5,21},{6,22},{7,23},{8,24},{9,... | collective-permute-start | bytes 393224 | tf_op jit(solution)/shard_map/ppermute | solution.py:44
  171.8 3.0 %collective-permute-done.31 = f32[1,512]{1,0:T(1,128)S(1)} collective-permute-done((f32[1,512]{1,0:T(1,128)S(1)}, f32[1,512]{1,0:T(1,128)S(1)}, u32[]{:S(2)}, u32[]{:S(2)}) %collective-permute-start.31) | collective-permute-done | bytes 2080 | tf_op jit(solution)/shard_map/ppermute | solution.py:24
  175.4 1.4 slice_divide_fusion.1
  (140 shorter events, 18.4 us)
Async XLA Ops:
  1.7 10.4 %collective-permute-start = (bf16[128,512]{1,0:T(8,128)(2,1)S(1)}, bf16[128,512]{1,0:T(8,128)(2,1)S(1)}, u32[]{:S(2)}, u32[]{:S(2)}) collective-permute-start(bf16[128,512]{1,0:T(8,128)(2,1)S(1)} %get-tuple-element.84), channel_id=1, source_target_pairs={{0,16},{1,17},{2,18},{3,19},{4,20},{5,21},{6,22},{7,23},{8,24},{9,... | collective-permute-start | bytes 393224 | tf_op jit(solution)/shard_map/ppermute | solution.py:44
  12.1 10.4 %collective-permute-start.1 = (bf16[256,512]{1,0:T(8,128)(2,1)S(1)}, bf16[256,512]{1,0:T(8,128)(2,1)S(1)}, u32[]{:S(2)}, u32[]{:S(2)}) collective-permute-start(bf16[256,512]{1,0:T(8,128)(2,1)S(1)} %pad_maximum_fusion.10), channel_id=1, source_target_pairs={{0,8},{1,5},{2,10},{3,7},{4,12},{5,1},{6,14},{7,3},{8,0},{9,13},{1... | collective-permute-start | bytes 786440 | tf_op jit(solution)/shard_map/ppermute | solution.py:44
  12.9 10.2 %collective-permute-start.5 = (bf16[128,512]{1,0:T(8,128)(2,1)S(1)}, bf16[128,512]{1,0:T(8,128)(2,1)S(1)}, u32[]{:S(2)}, u32[]{:S(2)}) collective-permute-start(bf16[128,512]{1,0:T(8,128)(2,1)S(1)} %get-tuple-element.83), channel_id=1, source_target_pairs={{0,16},{1,17},{2,18},{3,19},{4,20},{5,21},{6,22},{7,23},{8,24},{9,... | collective-permute-start | bytes 393224 | tf_op jit(solution)/shard_map/ppermute | solution.py:44
  22.5 9.2 %collective-permute-start.2 = (bf16[512,512]{1,0:T(8,128)(2,1)S(1)}, bf16[512,512]{1,0:T(8,128)(2,1)S(1)}, u32[]{:S(2)}, u32[]{:S(2)}) collective-permute-start(bf16[512,512]{1,0:T(8,128)(2,1)S(1)} %pad_maximum_fusion.2.refs_3_), channel_id=1, source_target_pairs={{0,4},{1,9},{2,6},{3,11},{4,0},{5,13},{6,2},{7,15},{8,12},{9,1},{1... | collective-permute-start | bytes 1572872 | tf_op jit(solution)/shard_map/ppermute | solution.py:44
  23.2 7.4 %collective-permute-start.6 = (bf16[256,512]{1,0:T(8,128)(2,1)S(1)}, bf16[256,512]{1,0:T(8,128)(2,1)S(1)}, u32[]{:S(2)}, u32[]{:S(2)}) collective-permute-start(bf16[256,512]{1,0:T(8,128)(2,1)S(1)} %pad_maximum_fusion.11), channel_id=1, source_target_pairs={{0,8},{1,5},{2,10},{3,7},{4,12},{5,1},{6,14},{7,3},{8,0},{9,13},{1... | collective-permute-start | bytes 786440 | tf_op jit(solution)/shard_map/ppermute | solution.py:44
  24.1 2.8 %copy-start = (bf16[3072,1024]{1,0:T(8,128)(2,1)S(1)}, bf16[3072,1024]{1,0:T(8,128)(2,1)}, u32[]{:S(2)}) copy-start(bf16[3072,1024]{1,0:T(8,128)(2,1)} %f_ref.1) | copy-start | bytes 18874372
  26.9 2.8 %copy-start.1 = (bf16[3072,1024]{1,0:T(8,128)(2,1)S(1)}, bf16[3072,1024]{1,0:T(8,128)(2,1)}, u32[]{:S(2)}) copy-start(bf16[3072,1024]{1,0:T(8,128)(2,1)} %c_ref.1) | copy-start | bytes 18874372
  29.7 0.9 copy-start.17
  30.6 11.2 %copy-start.2 = (bf16[3072,1024]{1,0:T(8,128)(2,1)}, bf16[3072,1024]{1,0:T(8,128)(2,1)S(1)}, u32[]{:S(2)}) copy-start(bf16[3072,1024]{1,0:T(8,128)(2,1)S(1)} %get-tuple-element.32.refs_1_) | copy-start | bytes 18874372
  30.6 11.2 %copy-start.4 = (bf16[3072,1024]{1,0:T(8,128)(2,1)}, bf16[3072,1024]{1,0:T(8,128)(2,1)S(1)}, u32[]{:S(2)}) copy-start(bf16[3072,1024]{1,0:T(8,128)(2,1)S(1)} %get-tuple-element.33.refs_2_) | copy-start | bytes 18874372
  30.7 11.1 %collective-permute-start.7 = (bf16[512,512]{1,0:T(8,128)(2,1)S(1)}, bf16[512,512]{1,0:T(8,128)(2,1)S(1)}, u32[]{:S(2)}, u32[]{:S(2)}) collective-permute-start(bf16[512,512]{1,0:T(8,128)(2,1)S(1)} %pad_maximum_fusion.3.refs_3_), channel_id=1, source_target_pairs={{0,4},{1,9},{2,6},{3,11},{4,0},{5,13},{6,2},{7,15},{8,12},{9,1},{1... | collective-permute-start | bytes 1572872 | tf_op jit(solution)/shard_map/ppermute | solution.py:44
  40.7 11.1 %collective-permute-start.3 = (f16[528,512]{1,0:T(8,128)(2,1)S(1)}, f16[528,512]{1,0:T(8,128)(2,1)S(1)}, u32[]{:S(2)}, u32[]{:S(2)}) collective-permute-start(f16[528,512]{1,0:T(8,128)(2,1)S(1)} %pad_maximum_fusion), channel_id=1, source_target_pairs={{0,4},{1,9},{2,6},{3,11},{4,0},{5,13},{6,2},{7,15},{8,12},{9,1},{1... | collective-permute-start | bytes 1622024 | tf_op jit(solution)/shard_map/ppermute | solution.py:44
  50.7 10.9 %collective-permute-start.8 = (f16[528,512]{1,0:T(8,128)(2,1)S(1)}, f16[528,512]{1,0:T(8,128)(2,1)S(1)}, u32[]{:S(2)}, u32[]{:S(2)}) collective-permute-start(f16[528,512]{1,0:T(8,128)(2,1)S(1)} %pad_maximum_fusion.1), channel_id=1, source_target_pairs={{0,4},{1,9},{2,6},{3,11},{4,0},{5,13},{6,2},{7,15},{8,12},{9,1},{1... | collective-permute-start | bytes 1622024 | tf_op jit(solution)/shard_map/ppermute | solution.py:44
  52.1 9.5 %collective-permute-start.4 = (f16[272,512]{1,0:T(8,128)(2,1)S(1)}, f16[272,512]{1,0:T(8,128)(2,1)S(1)}, u32[]{:S(2)}, u32[]{:S(2)}) collective-permute-start(f16[272,512]{1,0:T(8,128)(2,1)S(1)} %pad_maximum_fusion.8), channel_id=1, source_target_pairs={{0,8},{1,5},{2,10},{3,7},{4,12},{5,1},{6,14},{7,3},{8,0},{9,13},{1... | collective-permute-start | bytes 835592 | tf_op jit(solution)/shard_map/ppermute | solution.py:44
  61.9 13.0 %copy-start.6 = (f32[128,1024]{1,0:T(8,128)S(1)}, f32[128,1024]{1,0:T(8,128)}, u32[]{:S(2)}) copy-start(f32[128,1024]{1,0:T(8,128)} %param.7) | copy-start | bytes 1572868
  62.1 7.2 %collective-permute-start.10 = (f16[272,512]{1,0:T(8,128)(2,1)S(1)}, f16[272,512]{1,0:T(8,128)(2,1)S(1)}, u32[]{:S(2)}, u32[]{:S(2)}) collective-permute-start(f16[272,512]{1,0:T(8,128)(2,1)S(1)} %pad_maximum_fusion.9), channel_id=1, source_target_pairs={{0,8},{1,5},{2,10},{3,7},{4,12},{5,1},{6,14},{7,3},{8,0},{9,13},{1... | collective-permute-start | bytes 835592 | tf_op jit(solution)/shard_map/ppermute | solution.py:44
  62.8 12.1 %collective-permute-start.9 = (f16[144,512]{1,0:T(8,128)(2,1)S(1)}, f16[144,512]{1,0:T(8,128)(2,1)S(1)}, u32[]{:S(2)}, u32[]{:S(2)}) collective-permute-start(f16[144,512]{1,0:T(8,128)(2,1)S(1)} %pad_maximum_fusion.14), channel_id=1, source_target_pairs={{0,16},{1,17},{2,18},{3,19},{4,20},{5,21},{6,22},{7,23},{8,24},{9,... | collective-permute-start | bytes 442376 | tf_op jit(solution)/shard_map/ppermute | solution.py:44
  67.6 20.9 %copy-start.12 = (f32[1,512]{1,0:T(1,128)}, f32[1,512]{1,0:T(1,128)S(1)}, u32[]{:S(2)}) copy-start(f32[1,512]{1,0:T(1,128)S(1)} %get-tuple-element.101.refs_1_) | copy-start | bytes 6148
  74.8 13.6 %copy-start.13 = (f32[1,512]{1,0:T(1,128)}, f32[1,512]{1,0:T(1,128)S(1)}, u32[]{:S(2)}) copy-start(f32[1,512]{1,0:T(1,128)S(1)} %add_divide_fusion.1.refs_0_) | copy-start | bytes 6148
  75.0 13.1 %collective-permute-start.11 = (f16[128,512]{1,0:T(8,128)(2,1)S(1)}, f16[128,512]{1,0:T(8,128)(2,1)S(1)}, u32[]{:S(2)}, u32[]{:S(2)}) collective-permute-start(f16[128,512]{1,0:T(8,128)(2,1)S(1)} %get-tuple-element.71), channel_id=1, source_target_pairs={{0,16},{1,17},{2,18},{3,19},{4,20},{5,21},{6,22},{7,23},{8,24},{9,... | collective-permute-start | bytes 393224 | tf_op jit(solution)/shard_map/ppermute | solution.py:44
  76.0 12.1 %collective-permute-start.12 = (f16[144,512]{1,0:T(8,128)(2,1)S(1)}, f16[144,512]{1,0:T(8,128)(2,1)S(1)}, u32[]{:S(2)}, u32[]{:S(2)}) collective-permute-start(f16[144,512]{1,0:T(8,128)(2,1)S(1)} %pad_maximum_fusion.15), channel_id=1, source_target_pairs={{0,16},{1,17},{2,18},{3,19},{4,20},{5,21},{6,22},{7,23},{8,24},{9,... | collective-permute-start | bytes 442376 | tf_op jit(solution)/shard_map/ppermute | solution.py:44
  78.2 19.6 %copy-start.14 = (f32[1,512]{1,0:T(1,128)}, f32[1,512]{1,0:T(1,128)S(1)}, u32[]{:S(2)}) copy-start(f32[1,512]{1,0:T(1,128)S(1)} %get-tuple-element.98.refs_3_) | copy-start | bytes 6148
  88.2 8.6 %collective-permute-start.13 = (f16[256,512]{1,0:T(8,128)(2,1)S(1)}, f16[256,512]{1,0:T(8,128)(2,1)S(1)}, u32[]{:S(2)}, u32[]{:S(2)}) collective-permute-start(f16[256,512]{1,0:T(8,128)(2,1)S(1)} %pad_maximum_fusion.12), channel_id=1, source_target_pairs={{0,8},{1,5},{2,10},{3,7},{4,12},{5,1},{6,14},{7,3},{8,0},{9,13},{1... | collective-permute-start | bytes 786440 | tf_op jit(solution)/shard_map/ppermute | solution.py:44
  88.3 26.8 %copy-start.15 = (f32[1,512]{1,0:T(1,128)}, f32[1,512]{1,0:T(1,128)S(1)}, u32[]{:S(2)}) copy-start(f32[1,512]{1,0:T(1,128)S(1)} %add_divide_fusion.refs_2_) | copy-start | bytes 6148
  88.5 6.0 %collective-permute-start.14 = (f16[128,512]{1,0:T(8,128)(2,1)S(1)}, f16[128,512]{1,0:T(8,128)(2,1)S(1)}, u32[]{:S(2)}, u32[]{:S(2)}) collective-permute-start(f16[128,512]{1,0:T(8,128)(2,1)S(1)} %multiply_convert_fusion), channel_id=1, source_target_pairs={{0,16},{1,17},{2,18},{3,19},{4,20},{5,21},{6,22},{7,23},{8,24},{9,... | collective-permute-start | bytes 393224 | tf_op jit(solution)/shard_map/ppermute | solution.py:44
  91.0 8.7 %collective-permute-start.17 = (f32[3,512]{1,0:T(4,128)S(1)}, f32[3,512]{1,0:T(4,128)S(1)}, u32[]{:S(2)}, u32[]{:S(2)}) collective-permute-start(f32[3,512]{1,0:T(4,128)S(1)} %pad_maximum_fusion.16), channel_id=1, source_target_pairs={{0,1},{1,0},{2,3},{3,2},{4,5},{5,4},{6,7},{7,6},{8,9},{9,8},{10,11... | collective-permute-start | bytes 18440 | tf_op jit(solution)/shard_map/ppermute | solution.py:24
  97.7 9.8 %collective-permute-start.15 = (f16[512,512]{1,0:T(8,128)(2,1)S(1)}, f16[512,512]{1,0:T(8,128)(2,1)S(1)}, u32[]{:S(2)}, u32[]{:S(2)}) collective-permute-start(f16[512,512]{1,0:T(8,128)(2,1)S(1)} %pad_maximum_fusion.4), channel_id=1, source_target_pairs={{0,4},{1,9},{2,6},{3,11},{4,0},{5,13},{6,2},{7,15},{8,12},{9,1},{1... | collective-permute-start | bytes 1572872 | tf_op jit(solution)/shard_map/ppermute | solution.py:44
  97.8 9.7 %collective-permute-start.16 = (f16[256,512]{1,0:T(8,128)(2,1)S(1)}, f16[256,512]{1,0:T(8,128)(2,1)S(1)}, u32[]{:S(2)}, u32[]{:S(2)}) collective-permute-start(f16[256,512]{1,0:T(8,128)(2,1)S(1)} %pad_maximum_fusion.13), channel_id=1, source_target_pairs={{0,8},{1,5},{2,10},{3,7},{4,12},{5,1},{6,14},{7,3},{8,0},{9,13},{1... | collective-permute-start | bytes 786440 | tf_op jit(solution)/shard_map/ppermute | solution.py:44
  99.8 3.9 %collective-permute-start.18 = (f32[3,512]{1,0:T(4,128)S(1)}, f32[3,512]{1,0:T(4,128)S(1)}, u32[]{:S(2)}, u32[]{:S(2)}) collective-permute-start(f32[3,512]{1,0:T(4,128)S(1)} %fusion.17), channel_id=1, source_target_pairs={{0,2},{1,3},{2,0},{3,1},{4,6},{5,7},{6,4},{7,5},{8,10},{9,11},{10,... | collective-permute-start | bytes 18440 | tf_op jit(solution)/shard_map/ppermute | solution.py:24
  103.8 3.7 %collective-permute-start.19 = (f32[3,512]{1,0:T(4,128)S(1)}, f32[3,512]{1,0:T(4,128)S(1)}, u32[]{:S(2)}, u32[]{:S(2)}) collective-permute-start(f32[3,512]{1,0:T(4,128)S(1)} %fusion.24), channel_id=1, source_target_pairs={{0,4},{4,0},{8,12},{12,8},{16,20},{20,16},{24,28},{28,24},{1,5},{5... | collective-permute-start | bytes 18440 | tf_op jit(solution)/shard_map/ppermute | solution.py:24
  107.5 6.7 %copy-start.9 = (f16[256,512]{1,0:T(8,128)(2,1)}, f16[256,512]{1,0:T(8,128)(2,1)S(1)}, u32[]{:S(2)}) copy-start(f16[256,512]{1,0:T(8,128)(2,1)S(1)} %collective-permute-done.16) | copy-start | bytes 786436
  108.4 3.8 %collective-permute-start.20 = (f32[3,512]{1,0:T(4,128)S(1)}, f32[3,512]{1,0:T(4,128)S(1)}, u32[]{:S(2)}, u32[]{:S(2)}) collective-permute-start(f32[3,512]{1,0:T(4,128)S(1)} %add.209), channel_id=1, source_target_pairs={{0,8},{4,12},{8,0},{12,4},{16,24},{20,28},{24,16},{28,20},{1,9},{5... | collective-permute-start | bytes 18440 | tf_op jit(solution)/shard_map/ppermute | solution.py:24
  112.2 4.5 %collective-permute-start.21 = (f32[3,512]{1,0:T(4,128)S(1)}, f32[3,512]{1,0:T(4,128)S(1)}, u32[]{:S(2)}, u32[]{:S(2)}) collective-permute-start(f32[3,512]{1,0:T(4,128)S(1)} %add.210), channel_id=1, source_target_pairs={{0,16},{4,20},{8,24},{12,28},{16,0},{20,4},{24,8},{28,12},{1,17},{... | collective-permute-start | bytes 18440 | tf_op jit(solution)/shard_map/ppermute | solution.py:24
  115.1 21.4 %collective-permute-start.22 = (f16[512,512]{1,0:T(8,128)(2,1)}, f16[512,512]{1,0:T(8,128)(2,1)}, u32[]{:S(2)}, u32[]{:S(2)}) collective-permute-start(f16[512,512]{1,0:T(8,128)(2,1)} %pad_maximum_fusion.5), channel_id=1, source_target_pairs={{0,4},{1,9},{2,6},{3,11},{4,0},{5,13},{6,2},{7,15},{8,12},{9,1},{1... | collective-permute-start | bytes 1572872 | tf_op jit(solution)/shard_map/ppermute | solution.py:44
  121.4 2.8 %copy-start.3 = (bf16[3072,1024]{1,0:T(8,128)(2,1)S(1)}, bf16[3072,1024]{1,0:T(8,128)(2,1)}, u32[]{:S(2)}) copy-start(bf16[3072,1024]{1,0:T(8,128)(2,1)} %copy-done.2) | copy-start | bytes 18874372
  124.2 2.8 %copy-start.5 = (bf16[3072,1024]{1,0:T(8,128)(2,1)S(1)}, bf16[3072,1024]{1,0:T(8,128)(2,1)}, u32[]{:S(2)}) copy-start(bf16[3072,1024]{1,0:T(8,128)(2,1)} %copy-done.4) | copy-start | bytes 18874372
  135.8 1.0 copy-start.10
  135.9 12.7 %collective-permute-start.24 = (f16[512,512]{1,0:T(8,128)(2,1)S(1)}, f16[512,512]{1,0:T(8,128)(2,1)S(1)}, u32[]{:S(2)}, u32[]{:S(2)}) collective-permute-start(f16[512,512]{1,0:T(8,128)(2,1)S(1)} %slice_convert_fusion), channel_id=1, source_target_pairs={{0,4},{1,9},{2,6},{3,11},{4,0},{5,13},{6,2},{7,15},{8,12},{9,1},{1... | collective-permute-start | bytes 1572872 | tf_op jit(solution)/shard_map/ppermute | solution.py:44
  146.9 1.7 collective-permute-start.25
  147.1 11.4 %collective-permute-start.23 = (f16[512,512]{1,0:T(8,128)(2,1)S(1)}, f16[512,512]{1,0:T(8,128)(2,1)S(1)}, u32[]{:S(2)}, u32[]{:S(2)}) collective-permute-start(f16[512,512]{1,0:T(8,128)(2,1)S(1)} %slice_convert_fusion.1), channel_id=1, source_target_pairs={{0,4},{1,9},{2,6},{3,11},{4,0},{5,13},{6,2},{7,15},{8,12},{9,1},{1... | collective-permute-start | bytes 1572872 | tf_op jit(solution)/shard_map/ppermute | solution.py:44
  148.6 4.4 %collective-permute-start.26 = (f32[1,512]{1,0:T(1,128)S(1)}, f32[1,512]{1,0:T(1,128)S(1)}, u32[]{:S(2)}, u32[]{:S(2)}) collective-permute-start(f32[1,512]{1,0:T(1,128)S(1)} %add.219), channel_id=1, source_target_pairs={{0,2},{1,3},{2,0},{3,1},{4,6},{5,7},{6,4},{7,5},{8,10},{9,11},{10,... | collective-permute-start | bytes 6152 | tf_op jit(solution)/shard_map/ppermute | solution.py:24
  151.5 11.4 %collective-permute-start.28 = (f16[256,512]{1,0:T(8,128)(2,1)S(1)}, f16[256,512]{1,0:T(8,128)(2,1)S(1)}, u32[]{:S(2)}, u32[]{:S(2)}) collective-permute-start(f16[256,512]{1,0:T(8,128)(2,1)S(1)} %slice_convert_fusion.4), channel_id=1, source_target_pairs={{0,8},{1,5},{2,10},{3,7},{4,12},{5,1},{6,14},{7,3},{8,0},{9,13},{1... | collective-permute-start | bytes 786440 | tf_op jit(solution)/shard_map/ppermute | solution.py:44
  158.5 4.3 %collective-permute-start.29 = (f32[1,512]{1,0:T(1,128)S(1)}, f32[1,512]{1,0:T(1,128)S(1)}, u32[]{:S(2)}, u32[]{:S(2)}) collective-permute-start(f32[1,512]{1,0:T(1,128)S(1)} %add.220), channel_id=1, source_target_pairs={{0,4},{4,0},{8,12},{12,8},{16,20},{20,16},{24,28},{28,24},{1,5},{5... | collective-permute-start | bytes 6152 | tf_op jit(solution)/shard_map/ppermute | solution.py:24
  160.2 8.5 %collective-permute-start.27 = (f16[256,512]{1,0:T(8,128)(2,1)S(1)}, f16[256,512]{1,0:T(8,128)(2,1)S(1)}, u32[]{:S(2)}, u32[]{:S(2)}) collective-permute-start(f16[256,512]{1,0:T(8,128)(2,1)S(1)} %slice_convert_fusion.5), channel_id=1, source_target_pairs={{0,8},{1,5},{2,10},{3,7},{4,12},{5,1},{6,14},{7,3},{8,0},{9,13},{1... | collective-permute-start | bytes 786440 | tf_op jit(solution)/shard_map/ppermute | solution.py:44
  163.0 5.7 %collective-permute-start.30 = (f32[1,512]{1,0:T(1,128)S(1)}, f32[1,512]{1,0:T(1,128)S(1)}, u32[]{:S(2)}, u32[]{:S(2)}) collective-permute-start(f32[1,512]{1,0:T(1,128)S(1)} %add.223), channel_id=1, source_target_pairs={{0,8},{4,12},{8,0},{12,4},{16,24},{20,28},{24,16},{28,20},{1,9},{5... | collective-permute-start | bytes 6152 | tf_op jit(solution)/shard_map/ppermute | solution.py:24
  164.9 11.9 %collective-permute-start.32 = (f16[128,512]{1,0:T(8,128)(2,1)S(1)}, f16[128,512]{1,0:T(8,128)(2,1)S(1)}, u32[]{:S(2)}, u32[]{:S(2)}) collective-permute-start(f16[128,512]{1,0:T(8,128)(2,1)S(1)} %slice_convert_fusion.9), channel_id=1, source_target_pairs={{0,16},{1,17},{2,18},{3,19},{4,20},{5,21},{6,22},{7,23},{8,24},{9,... | collective-permute-start | bytes 393224 | tf_op jit(solution)/shard_map/ppermute | solution.py:44
  168.7 6.1 %collective-permute-start.31 = (f32[1,512]{1,0:T(1,128)S(1)}, f32[1,512]{1,0:T(1,128)S(1)}, u32[]{:S(2)}, u32[]{:S(2)}) collective-permute-start(f32[1,512]{1,0:T(1,128)S(1)} %add.224), channel_id=1, source_target_pairs={{0,16},{4,20},{8,24},{12,28},{16,0},{20,4},{24,8},{28,12},{1,17},{... | collective-permute-start | bytes 6152 | tf_op jit(solution)/shard_map/ppermute | solution.py:24
  169.9 7.7 %collective-permute-start.33 = (f16[128,512]{1,0:T(8,128)(2,1)S(1)}, f16[128,512]{1,0:T(8,128)(2,1)S(1)}, u32[]{:S(2)}, u32[]{:S(2)}) collective-permute-start(f16[128,512]{1,0:T(8,128)(2,1)S(1)} %slice_convert_fusion.8), channel_id=1, source_target_pairs={{0,16},{1,17},{2,18},{3,19},{4,20},{5,21},{6,22},{7,23},{8,24},{9,... | collective-permute-start | bytes 393224 | tf_op jit(solution)/shard_map/ppermute | solution.py:44
  (4 other events, 3.1 us)

commit v5 on v3

--- a/solution.py
+++ b/solution.py
@@ -272,7 +272,7 @@
             sum(colsum(image[k] * image[k]) for k in chunks),
         ]
     )
-    all_hops = [(axis, stride) for axis in ("dp", "mp") for stride in strides_of(axis)]
+    all_hops = [(axis, stride) for axis in ("mp", "dp") for stride in reversed(strides_of(axis))]
     hops = list(all_hops)
     for step in range(1, steps):
         for k in chunks:

time: 184 us -> 177 us (0.962)
  starting transfers between devices: 57.1 us -> 49.4 us
    ppermute x24, starting transfers between devices: 43.6 us -> 36.7 us  [trade(): return lax.ppermute(values, ('dp', 'mp'), pairs)]
    ppermute x10, waiting for transfers between devices: 9.81 us -> 15.2 us  [swap(): return lax.ppermute(values, axis, [(i, i ^ stride) for i in range(size)])]
    ppermute x24, waiting for transfers between devices: 54.1 us -> 49.3 us  [trade(): return lax.ppermute(values, ('dp', 'mp'), pairs)]
  transfers between devices with their start and end apart: 34 -> 34, of which waited for: 20 -> 19; matrix products, arithmetic and copies ran while one was open for 5% -> 5% of each run, Pallas kernels for 20% -> 21%
where the time goes in v5:
time: 177 us; the launch traced here: 176 us
  waiting for transfers between devices  64.5 us (36%)
  starting transfers between devices  49.4 us (28%)
  Pallas kernels  37.2 us (21%)
  local copies, waits for them, and re-layouts  13.2 us (7%)
  other arithmetic  10.9 us (6%)
    ppermute x24, waiting for transfers between devices, trade(): return lax.ppermute(values, ('dp', 'mp'), pairs)  49.3 us
    ppermute x24, starting transfers between devices, trade(): return lax.ppermute(values, ('dp', 'mp'), pairs)  36.7 us
    pallas_call x4, Pallas kernels, curve(): pl.pallas_call(lambda *refs: curve_kernel(*refs, n_dp=n_dp, token_count=n...  34.8 us
    ppermute x10, waiting for transfers between devices, swap(): return lax.ppermute(values, axis, [(i, i ^ stride) for i in range(size)])  15.2 us
    ppermute x10, starting transfers between devices, swap(): return lax.ppermute(values, axis, [(i, i ^ stride) for i in range(size)])  12.7 us
    unnamed x30, local copies, waits for them, and re-layouts  11.2 us
  transfers between devices with their start and end apart: 34, of which 19 were waited for; matrix products, arithmetic and copies ran while one was open for 5% of the time, Pallas kernels for 21%

profile of v5, /device:TPU:0, one launch (start us, length us, event | category | flops | bytes accessed | tf_op | source)
XLA Modules:
  0.0 176.4 jit_solution(14651373637153181312)
XLA Ops:
  0.6 1.1 fusion.22
  1.7 4.1 %collective-permute-start = (bf16[128,512]{1,0:T(8,128)(2,1)S(1)}, bf16[128,512]{1,0:T(8,128)(2,1)S(1)}, u32[]{:S(2)}, u32[]{:S(2)}) collective-permute-start(bf16[128,512]{1,0:T(8,128)(2,1)S(1)} %get-tuple-element.80), channel_id=1, source_target_pairs={{0,16},{1,17},{2,18},{3,19},{4,20},{5,21},{6,22},{7,23},{8,24},{9,... | collective-permute-start | bytes 393224 | tf_op jit(solution)/shard_map/ppermute | solution.py:44
  5.8 6.3 %collective-permute-done = bf16[128,512]{1,0:T(8,128)(2,1)S(1)} collective-permute-done((bf16[128,512]{1,0:T(8,128)(2,1)S(1)}, bf16[128,512]{1,0:T(8,128)(2,1)S(1)}, u32[]{:S(2)}, u32[]{:S(2)}) %collective-permute-start) | collective-permute-done | bytes 131104 | tf_op jit(solution)/shard_map/ppermute | solution.py:44
  12.9 3.4 %collective-permute-start.5 = (bf16[128,512]{1,0:T(8,128)(2,1)S(1)}, bf16[128,512]{1,0:T(8,128)(2,1)S(1)}, u32[]{:S(2)}, u32[]{:S(2)}) collective-permute-start(bf16[128,512]{1,0:T(8,128)(2,1)S(1)} %get-tuple-element.81), channel_id=1, source_target_pairs={{0,16},{1,17},{2,18},{3,19},{4,20},{5,21},{6,22},{7,23},{8,24},{9,... | collective-permute-start | bytes 393224 | tf_op jit(solution)/shard_map/ppermute | solution.py:44
  16.3 6.2 %collective-permute-done.1 = bf16[256,512]{1,0:T(8,128)(2,1)S(1)} collective-permute-done((bf16[256,512]{1,0:T(8,128)(2,1)S(1)}, bf16[256,512]{1,0:T(8,128)(2,1)S(1)}, u32[]{:S(2)}, u32[]{:S(2)}) %collective-permute-start.1) | collective-permute-done | bytes 262176 | tf_op jit(solution)/shard_map/ppermute | solution.py:44
  24.1 2.8 %copy-done = bf16[3072,1024]{1,0:T(8,128)(2,1)S(1)} copy-done((bf16[3072,1024]{1,0:T(8,128)(2,1)S(1)}, bf16[3072,1024]{1,0:T(8,128)(2,1)}, u32[]{:S(2)}) %copy-start) | copy-done | bytes 6291480
  26.9 2.8 %copy-done.1 = bf16[3072,1024]{1,0:T(8,128)(2,1)S(1)} copy-done((bf16[3072,1024]{1,0:T(8,128)(2,1)S(1)}, bf16[3072,1024]{1,0:T(8,128)(2,1)}, u32[]{:S(2)}) %copy-start.1) | copy-done | bytes 6291480
  31.8 8.7 %shard_map.69 = (f32[1024,512]{1,0:T(8,128)S(1)}, f32[8,512]{1,0:T(8,128)S(1)}) custom-call(s32[8]{0:T(128)S(1)} %fusion.16.refs_0_, bf16[3072,1024]{1,0:T(8,128)(2,1)S(1)} %get-tuple-element.30.refs_1_, bf16[3072,1024]{1,0:T(8,128)(2,1)S(1)} %get-tuple-element.31.refs_2_, bf16[512,512]{1,0:T(8,128)(2,1)S(1)} %pad_maximum_fusion.2.refs_3_, ...), custom_call_target="tpu_custom_call" | custom-call | flops 6442450944 | bytes 12582912 | tf_op jit(solution)/shard_map/pallas_call | solution.py:181
  40.7 1.1 collective-permute-start.3
  41.8 8.7 %shard_map.70 = (f32[1024,512]{1,0:T(8,128)S(1)}, f32[8,512]{1,0:T(8,128)S(1)}) custom-call(s32[8]{0:T(128)S(1)} %fusion.16.refs_0_, bf16[3072,1024]{1,0:T(8,128)(2,1)S(1)} %get-tuple-element.30.refs_1_, bf16[3072,1024]{1,0:T(8,128)(2,1)S(1)} %get-tuple-element.31.refs_2_, bf16[512,512]{1,0:T(8,128)(2,1)S(1)} %pad_maximum_fusion.3.refs_3_, ...), custom_call_target="tpu_custom_call" | custom-call | flops 6442450944 | bytes 12582912 | tf_op jit(solution)/shard_map/pallas_call | solution.py:181
  50.8 1.1 collective-permute-start.8
  52.2 1.7 collective-permute-start.4
  53.9 7.9 %collective-permute-done.8 = f16[528,512]{1,0:T(8,128)(2,1)S(1)} collective-permute-done((f16[528,512]{1,0:T(8,128)(2,1)S(1)}, f16[528,512]{1,0:T(8,128)(2,1)S(1)}, u32[]{:S(2)}, u32[]{:S(2)}) %collective-permute-start.8) | collective-permute-done | bytes 540704 | tf_op jit(solution)/shard_map/ppermute | solution.py:44
  62.8 4.9 %collective-permute-start.9 = (f16[144,512]{1,0:T(8,128)(2,1)S(1)}, f16[144,512]{1,0:T(8,128)(2,1)S(1)}, u32[]{:S(2)}, u32[]{:S(2)}) collective-permute-start(f16[144,512]{1,0:T(8,128)(2,1)S(1)} %pad_maximum_fusion.14), channel_id=1, source_target_pairs={{0,16},{1,17},{2,18},{3,19},{4,20},{5,21},{6,22},{7,23},{8,24},{9,... | collective-permute-start | bytes 442376 | tf_op jit(solution)/shard_map/ppermute | solution.py:44
  67.6 2.0 %collective-permute-done.10 = f16[272,512]{1,0:T(8,128)(2,1)S(1)} collective-permute-done((f16[272,512]{1,0:T(8,128)(2,1)S(1)}, f16[272,512]{1,0:T(8,128)(2,1)S(1)}, u32[]{:S(2)}, u32[]{:S(2)}) %collective-permute-start.10) | collective-permute-done | bytes 278560 | tf_op jit(solution)/shard_map/ppermute | solution.py:44
  69.6 5.4 %collective-permute-done.9 = f16[144,512]{1,0:T(8,128)(2,1)S(1)} collective-permute-done((f16[144,512]{1,0:T(8,128)(2,1)S(1)}, f16[144,512]{1,0:T(8,128)(2,1)S(1)}, u32[]{:S(2)}, u32[]{:S(2)}) %collective-permute-start.9) | collective-permute-done | bytes 147488 | tf_op jit(solution)/shard_map/ppermute | solution.py:44
  76.0 2.4 %collective-permute-start.12 = (f16[144,512]{1,0:T(8,128)(2,1)S(1)}, f16[144,512]{1,0:T(8,128)(2,1)S(1)}, u32[]{:S(2)}, u32[]{:S(2)}) collective-permute-start(f16[144,512]{1,0:T(8,128)(2,1)S(1)} %pad_maximum_fusion.15), channel_id=1, source_target_pairs={{0,16},{1,17},{2,18},{3,19},{4,20},{5,21},{6,22},{7,23},{8,24},{9,... | collective-permute-start | bytes 442376 | tf_op jit(solution)/shard_map/ppermute | solution.py:44
  78.4 5.6 %collective-permute-done.12 = f16[144,512]{1,0:T(8,128)(2,1)S(1)} collective-permute-done((f16[144,512]{1,0:T(8,128)(2,1)S(1)}, f16[144,512]{1,0:T(8,128)(2,1)S(1)}, u32[]{:S(2)}, u32[]{:S(2)}) %collective-permute-start.12) | collective-permute-done | bytes 147488 | tf_op jit(solution)/shard_map/ppermute | solution.py:44
  85.3 2.6 %collective-permute-start.18 = (f16[256,512]{1,0:T(8,128)(2,1)}, f16[256,512]{1,0:T(8,128)(2,1)}, u32[]{:S(2)}, u32[]{:S(2)}) collective-permute-start(f16[256,512]{1,0:T(8,128)(2,1)} %pad_maximum_fusion.12), channel_id=1, source_target_pairs={{0,8},{1,5},{2,10},{3,7},{4,12},{5,1},{6,14},{7,3},{8,0},{9,13},{1... | collective-permute-start | bytes 786440 | tf_op jit(solution)/shard_map/ppermute | solution.py:44
  87.9 1.6 collective-permute-start.14
  89.4 2.2 %collective-permute-start.19 = (f16[128,512]{1,0:T(8,128)(2,1)S(1)}, f16[128,512]{1,0:T(8,128)(2,1)S(1)}, u32[]{:S(2)}, u32[]{:S(2)}) collective-permute-start(f16[128,512]{1,0:T(8,128)(2,1)S(1)} %get-tuple-element.66), channel_id=1, source_target_pairs={{0,16},{1,17},{2,18},{3,19},{4,20},{5,21},{6,22},{7,23},{8,24},{9,... | collective-permute-start | bytes 393224 | tf_op jit(solution)/shard_map/ppermute | solution.py:44
  91.7 1.4 collective-permute-start.15
  93.0 2.3 %collective-permute-done.15 = f32[3,512]{1,0:T(4,128)S(1)} collective-permute-done((f32[3,512]{1,0:T(4,128)S(1)}, f32[3,512]{1,0:T(4,128)S(1)}, u32[]{:S(2)}, u32[]{:S(2)}) %collective-permute-start.15) | collective-permute-done | bytes 6176 | tf_op jit(solution)/shard_map/ppermute | solution.py:24
  95.8 3.5 %collective-permute-done.16 = f32[3,512]{1,0:T(4,128)S(1)} collective-permute-done((f32[3,512]{1,0:T(4,128)S(1)}, f32[3,512]{1,0:T(4,128)S(1)}, u32[]{:S(2)}, u32[]{:S(2)}) %collective-permute-start.16) | collective-permute-done | bytes 6176 | tf_op jit(solution)/shard_map/ppermute | solution.py:24
  99.3 2.0 %collective-permute-start.17 = (f32[3,512]{1,0:T(4,128)S(1)}, f32[3,512]{1,0:T(4,128)S(1)}, u32[]{:S(2)}, u32[]{:S(2)}) collective-permute-start(f32[3,512]{1,0:T(4,128)S(1)} %add.208), channel_id=1, source_target_pairs={{0,16},{4,20},{8,24},{12,28},{16,0},{20,4},{24,8},{28,12},{1,17},{... | collective-permute-start | bytes 18440 | tf_op jit(solution)/shard_map/ppermute | solution.py:24
  101.2 2.6 %collective-permute-done.17 = f32[3,512]{1,0:T(4,128)S(1)} collective-permute-done((f32[3,512]{1,0:T(4,128)S(1)}, f32[3,512]{1,0:T(4,128)S(1)}, u32[]{:S(2)}, u32[]{:S(2)}) %collective-permute-start.17) | collective-permute-done | bytes 6176 | tf_op jit(solution)/shard_map/ppermute | solution.py:24
  104.4 1.5 shard_map.71
  105.9 1.1 pad_maximum_fusion.4
  107.1 1.2 collective-permute-start.20
  110.4 5.4 %collective-permute-done.21 = f16[256,512]{1,0:T(8,128)(2,1)S(1)} collective-permute-done((f16[256,512]{1,0:T(8,128)(2,1)S(1)}, f16[256,512]{1,0:T(8,128)(2,1)S(1)}, u32[]{:S(2)}, u32[]{:S(2)}) %collective-permute-start.21) | collective-permute-done | bytes 262176 | tf_op jit(solution)/shard_map/ppermute | solution.py:44
  115.8 1.1 collective-permute-done.20
  117.9 1.4 add_convert_fusion
  119.3 2.8 %copy-done.3 = bf16[3072,1024]{1,0:T(8,128)(2,1)S(1)} copy-done((bf16[3072,1024]{1,0:T(8,128)(2,1)S(1)}, bf16[3072,1024]{1,0:T(8,128)(2,1)}, u32[]{:S(2)}) %copy-start.3) | copy-done | bytes 6291480
  122.1 2.8 %copy-done.5 = bf16[3072,1024]{1,0:T(8,128)(2,1)S(1)} copy-done((bf16[3072,1024]{1,0:T(8,128)(2,1)S(1)}, bf16[3072,1024]{1,0:T(8,128)(2,1)}, u32[]{:S(2)}) %copy-start.5) | copy-done | bytes 6291480
  124.9 8.8 %shard_map.73 = (f32[1024,512]{1,0:T(8,128)S(1)}, f32[8,512]{1,0:T(8,128)S(1)}) custom-call(s32[8]{0:T(128)S(1)} %fusion.16.refs_0_, bf16[3072,1024]{1,0:T(8,128)(2,1)S(1)} %copy-done.3, bf16[3072,1024]{1,0:T(8,128)(2,1)S(1)} %copy-done.5, bf16[512,512]{1,0:T(8,128)(2,1)S(1)} %get-tuple-element.100.refs_3_, bf16[512,512]{1,0:T(8,128)(2,1)S(1)} %get-tuple-element.99.refs_4_), custom_call_target="tpu_custom_call" | custom-call | flops 6442450944 | bytes 12582912 | tf_op jit(solution)/shard_map/pallas_call | solution.py:181
  133.8 1.3 collective-permute-start.24
  135.6 8.6 %shard_map.72 = (f32[1024,512]{1,0:T(8,128)S(1)}, f32[8,512]{1,0:T(8,128)S(1)}) custom-call(s32[8]{0:T(128)S(1)} %fusion.16.refs_0_, bf16[3072,1024]{1,0:T(8,128)(2,1)S(1)} %copy-done.3, bf16[3072,1024]{1,0:T(8,128)(2,1)S(1)} %copy-done.5, bf16[512,512]{1,0:T(8,128)(2,1)S(1)} %get-tuple-element.102.refs_3_, bf16[512,512]{1,0:T(8,128)(2,1)S(1)} %get-tuple-element.101.refs_4_), custom_call_target="tpu_custom_call" | custom-call | flops 6442450944 | bytes 12582912 | tf_op jit(solution)/shard_map/pallas_call | solution.py:181
  145.5 1.5 collective-permute-start.26
  147.2 1.8 %collective-permute-start.28 = (f16[256,512]{1,0:T(8,128)(2,1)S(1)}, f16[256,512]{1,0:T(8,128)(2,1)S(1)}, u32[]{:S(2)}, u32[]{:S(2)}) collective-permute-start(f16[256,512]{1,0:T(8,128)(2,1)S(1)} %slice_convert_fusion.4), channel_id=1, source_target_pairs={{0,8},{1,5},{2,10},{3,7},{4,12},{5,1},{6,14},{7,3},{8,0},{9,13},{1... | collective-permute-start | bytes 786440 | tf_op jit(solution)/shard_map/ppermute | solution.py:44
  149.1 7.3 %collective-permute-done.23 = f16[512,512]{1,0:T(8,128)(2,1)S(1)} collective-permute-done((f16[512,512]{1,0:T(8,128)(2,1)S(1)}, f16[512,512]{1,0:T(8,128)(2,1)S(1)}, u32[]{:S(2)}, u32[]{:S(2)}) %collective-permute-start.23) | collective-permute-done | bytes 524320 | tf_op jit(solution)/shard_map/ppermute | solution.py:44
  157.5 1.3 collective-permute-start.27
  158.8 1.3 collective-permute-done.29
  160.2 1.8 %collective-permute-start.30 = (f32[1,512]{1,0:T(1,128)S(1)}, f32[1,512]{1,0:T(1,128)S(1)}, u32[]{:S(2)}, u32[]{:S(2)}) collective-permute-start(f32[1,512]{1,0:T(1,128)S(1)} %add.223), channel_id=1, source_target_pairs={{0,8},{4,12},{8,0},{12,4},{16,24},{20,28},{24,16},{28,20},{1,9},{5... | collective-permute-start | bytes 6152 | tf_op jit(solution)/shard_map/ppermute | solution.py:24
  163.0 1.7 collective-permute-done.30
  164.7 3.1 %collective-permute-start.31 = (f32[1,512]{1,0:T(1,128)S(1)}, f32[1,512]{1,0:T(1,128)S(1)}, u32[]{:S(2)}, u32[]{:S(2)}) collective-permute-start(f32[1,512]{1,0:T(1,128)S(1)} %add.224), channel_id=1, source_target_pairs={{0,16},{4,20},{8,24},{12,28},{16,0},{20,4},{24,8},{28,12},{1,17},{... | collective-permute-start | bytes 6152 | tf_op jit(solution)/shard_map/ppermute | solution.py:24
  168.1 3.4 %collective-permute-done.31 = f32[1,512]{1,0:T(1,128)S(1)} collective-permute-done((f32[1,512]{1,0:T(1,128)S(1)}, f32[1,512]{1,0:T(1,128)S(1)}, u32[]{:S(2)}, u32[]{:S(2)}) %collective-permute-start.31) | collective-permute-done | bytes 2080 | tf_op jit(solution)/shard_map/ppermute | solution.py:24
  172.1 1.4 slice_divide_fusion.1
  173.5 1.6 collective-permute-done.33
  (134 shorter events, 18.8 us)
Async XLA Ops:
  1.7 10.4 %collective-permute-start = (bf16[128,512]{1,0:T(8,128)(2,1)S(1)}, bf16[128,512]{1,0:T(8,128)(2,1)S(1)}, u32[]{:S(2)}, u32[]{:S(2)}) collective-permute-start(bf16[128,512]{1,0:T(8,128)(2,1)S(1)} %get-tuple-element.80), channel_id=1, source_target_pairs={{0,16},{1,17},{2,18},{3,19},{4,20},{5,21},{6,22},{7,23},{8,24},{9,... | collective-permute-start | bytes 393224 | tf_op jit(solution)/shard_map/ppermute | solution.py:44
  12.1 10.4 %collective-permute-start.1 = (bf16[256,512]{1,0:T(8,128)(2,1)S(1)}, bf16[256,512]{1,0:T(8,128)(2,1)S(1)}, u32[]{:S(2)}, u32[]{:S(2)}) collective-permute-start(bf16[256,512]{1,0:T(8,128)(2,1)S(1)} %pad_maximum_fusion.10), channel_id=1, source_target_pairs={{0,8},{1,5},{2,10},{3,7},{4,12},{5,1},{6,14},{7,3},{8,0},{9,13},{1... | collective-permute-start | bytes 786440 | tf_op jit(solution)/shard_map/ppermute | solution.py:44
  12.9 10.2 %collective-permute-start.5 = (bf16[128,512]{1,0:T(8,128)(2,1)S(1)}, bf16[128,512]{1,0:T(8,128)(2,1)S(1)}, u32[]{:S(2)}, u32[]{:S(2)}) collective-permute-start(bf16[128,512]{1,0:T(8,128)(2,1)S(1)} %get-tuple-element.81), channel_id=1, source_target_pairs={{0,16},{1,17},{2,18},{3,19},{4,20},{5,21},{6,22},{7,23},{8,24},{9,... | collective-permute-start | bytes 393224 | tf_op jit(solution)/shard_map/ppermute | solution.py:44
  22.5 8.1 %copy-start.7 = (bf16[256,512]{1,0:T(8,128)(2,1)}, bf16[256,512]{1,0:T(8,128)(2,1)S(1)}, u32[]{:S(2)}) copy-start(bf16[256,512]{1,0:T(8,128)(2,1)S(1)} %collective-permute-done.1) | copy-start | bytes 786436
  22.5 9.2 %collective-permute-start.2 = (bf16[512,512]{1,0:T(8,128)(2,1)S(1)}, bf16[512,512]{1,0:T(8,128)(2,1)S(1)}, u32[]{:S(2)}, u32[]{:S(2)}) collective-permute-start(bf16[512,512]{1,0:T(8,128)(2,1)S(1)} %pad_maximum_fusion.2.refs_3_), channel_id=1, source_target_pairs={{0,4},{1,9},{2,6},{3,11},{4,0},{5,13},{6,2},{7,15},{8,12},{9,1},{1... | collective-permute-start | bytes 1572872 | tf_op jit(solution)/shard_map/ppermute | solution.py:44
  23.2 7.5 %collective-permute-start.6 = (bf16[256,512]{1,0:T(8,128)(2,1)S(1)}, bf16[256,512]{1,0:T(8,128)(2,1)S(1)}, u32[]{:S(2)}, u32[]{:S(2)}) collective-permute-start(bf16[256,512]{1,0:T(8,128)(2,1)S(1)} %pad_maximum_fusion.11), channel_id=1, source_target_pairs={{0,8},{1,5},{2,10},{3,7},{4,12},{5,1},{6,14},{7,3},{8,0},{9,13},{1... | collective-permute-start | bytes 786440 | tf_op jit(solution)/shard_map/ppermute | solution.py:44
  24.1 2.8 %copy-start = (bf16[3072,1024]{1,0:T(8,128)(2,1)S(1)}, bf16[3072,1024]{1,0:T(8,128)(2,1)}, u32[]{:S(2)}) copy-start(bf16[3072,1024]{1,0:T(8,128)(2,1)} %f_ref.1) | copy-start | bytes 18874372
  26.9 2.8 %copy-start.1 = (bf16[3072,1024]{1,0:T(8,128)(2,1)S(1)}, bf16[3072,1024]{1,0:T(8,128)(2,1)}, u32[]{:S(2)}) copy-start(bf16[3072,1024]{1,0:T(8,128)(2,1)} %c_ref.1) | copy-start | bytes 18874372
  29.7 0.9 copy-start.14
  30.6 11.2 %copy-start.2 = (bf16[3072,1024]{1,0:T(8,128)(2,1)}, bf16[3072,1024]{1,0:T(8,128)(2,1)S(1)}, u32[]{:S(2)}) copy-start(bf16[3072,1024]{1,0:T(8,128)(2,1)S(1)} %get-tuple-element.30.refs_1_) | copy-start | bytes 18874372
  30.6 11.2 %copy-start.4 = (bf16[3072,1024]{1,0:T(8,128)(2,1)}, bf16[3072,1024]{1,0:T(8,128)(2,1)S(1)}, u32[]{:S(2)}) copy-start(bf16[3072,1024]{1,0:T(8,128)(2,1)S(1)} %get-tuple-element.31.refs_2_) | copy-start | bytes 18874372
  30.7 11.1 %collective-permute-start.7 = (bf16[512,512]{1,0:T(8,128)(2,1)S(1)}, bf16[512,512]{1,0:T(8,128)(2,1)S(1)}, u32[]{:S(2)}, u32[]{:S(2)}) collective-permute-start(bf16[512,512]{1,0:T(8,128)(2,1)S(1)} %pad_maximum_fusion.3.refs_3_), channel_id=1, source_target_pairs={{0,4},{1,9},{2,6},{3,11},{4,0},{5,13},{6,2},{7,15},{8,12},{9,1},{1... | collective-permute-start | bytes 1572872 | tf_op jit(solution)/shard_map/ppermute | solution.py:44
  40.7 11.1 %collective-permute-start.3 = (f16[528,512]{1,0:T(8,128)(2,1)S(1)}, f16[528,512]{1,0:T(8,128)(2,1)S(1)}, u32[]{:S(2)}, u32[]{:S(2)}) collective-permute-start(f16[528,512]{1,0:T(8,128)(2,1)S(1)} %pad_maximum_fusion), channel_id=1, source_target_pairs={{0,4},{1,9},{2,6},{3,11},{4,0},{5,13},{6,2},{7,15},{8,12},{9,1},{1... | collective-permute-start | bytes 1622024 | tf_op jit(solution)/shard_map/ppermute | solution.py:44
  50.8 11.0 %collective-permute-start.8 = (f16[528,512]{1,0:T(8,128)(2,1)S(1)}, f16[528,512]{1,0:T(8,128)(2,1)S(1)}, u32[]{:S(2)}, u32[]{:S(2)}) collective-permute-start(f16[528,512]{1,0:T(8,128)(2,1)S(1)} %pad_maximum_fusion.1), channel_id=1, source_target_pairs={{0,4},{1,9},{2,6},{3,11},{4,0},{5,13},{6,2},{7,15},{8,12},{9,1},{1... | collective-permute-start | bytes 1622024 | tf_op jit(solution)/shard_map/ppermute | solution.py:44
  52.2 9.6 %collective-permute-start.4 = (f16[272,512]{1,0:T(8,128)(2,1)S(1)}, f16[272,512]{1,0:T(8,128)(2,1)S(1)}, u32[]{:S(2)}, u32[]{:S(2)}) collective-permute-start(f16[272,512]{1,0:T(8,128)(2,1)S(1)} %pad_maximum_fusion.8), channel_id=1, source_target_pairs={{0,8},{1,5},{2,10},{3,7},{4,12},{5,1},{6,14},{7,3},{8,0},{9,13},{1... | collective-permute-start | bytes 835592 | tf_op jit(solution)/shard_map/ppermute | solution.py:44
  62.0 13.0 %copy-start.6 = (f32[128,1024]{1,0:T(8,128)S(1)}, f32[128,1024]{1,0:T(8,128)}, u32[]{:S(2)}) copy-start(f32[128,1024]{1,0:T(8,128)} %param.7) | copy-start | bytes 1572868
  62.3 7.3 %collective-permute-start.10 = (f16[272,512]{1,0:T(8,128)(2,1)S(1)}, f16[272,512]{1,0:T(8,128)(2,1)S(1)}, u32[]{:S(2)}, u32[]{:S(2)}) collective-permute-start(f16[272,512]{1,0:T(8,128)(2,1)S(1)} %pad_maximum_fusion.9), channel_id=1, source_target_pairs={{0,8},{1,5},{2,10},{3,7},{4,12},{5,1},{6,14},{7,3},{8,0},{9,13},{1... | collective-permute-start | bytes 835592 | tf_op jit(solution)/shard_map/ppermute | solution.py:44
  62.8 12.2 %collective-permute-start.9 = (f16[144,512]{1,0:T(8,128)(2,1)S(1)}, f16[144,512]{1,0:T(8,128)(2,1)S(1)}, u32[]{:S(2)}, u32[]{:S(2)}) collective-permute-start(f16[144,512]{1,0:T(8,128)(2,1)S(1)} %pad_maximum_fusion.14), channel_id=1, source_target_pairs={{0,16},{1,17},{2,18},{3,19},{4,20},{5,21},{6,22},{7,23},{8,24},{9,... | collective-permute-start | bytes 442376 | tf_op jit(solution)/shard_map/ppermute | solution.py:44
  67.6 16.7 %copy-start.9 = (f32[1,512]{1,0:T(1,128)}, f32[1,512]{1,0:T(1,128)S(1)}, u32[]{:S(2)}) copy-start(f32[1,512]{1,0:T(1,128)S(1)} %get-tuple-element.98.refs_1_) | copy-start | bytes 6148
  75.0 9.4 %copy-start.10 = (f32[1,512]{1,0:T(1,128)}, f32[1,512]{1,0:T(1,128)S(1)}, u32[]{:S(2)}) copy-start(f32[1,512]{1,0:T(1,128)S(1)} %add_divide_fusion.1.refs_0_) | copy-start | bytes 6148
  75.1 8.9 %collective-permute-start.11 = (f16[128,512]{1,0:T(8,128)(2,1)S(1)}, f16[128,512]{1,0:T(8,128)(2,1)S(1)}, u32[]{:S(2)}, u32[]{:S(2)}) collective-permute-start(f16[128,512]{1,0:T(8,128)(2,1)S(1)} %get-tuple-element.68), channel_id=1, source_target_pairs={{0,16},{1,17},{2,18},{3,19},{4,20},{5,21},{6,22},{7,23},{8,24},{9,... | collective-permute-start | bytes 393224 | tf_op jit(solution)/shard_map/ppermute | solution.py:44
  76.0 8.0 %collective-permute-start.12 = (f16[144,512]{1,0:T(8,128)(2,1)S(1)}, f16[144,512]{1,0:T(8,128)(2,1)S(1)}, u32[]{:S(2)}, u32[]{:S(2)}) collective-permute-start(f16[144,512]{1,0:T(8,128)(2,1)S(1)} %pad_maximum_fusion.15), channel_id=1, source_target_pairs={{0,16},{1,17},{2,18},{3,19},{4,20},{5,21},{6,22},{7,23},{8,24},{9,... | collective-permute-start | bytes 442376 | tf_op jit(solution)/shard_map/ppermute | solution.py:44
  78.4 26.0 %copy-start.11 = (f32[1,512]{1,0:T(1,128)}, f32[1,512]{1,0:T(1,128)S(1)}, u32[]{:S(2)}) copy-start(f32[1,512]{1,0:T(1,128)S(1)} %get-tuple-element.96.refs_3_) | copy-start | bytes 6148
  84.1 20.3 %copy-start.12 = (f32[1,512]{1,0:T(1,128)}, f32[1,512]{1,0:T(1,128)S(1)}, u32[]{:S(2)}) copy-start(f32[1,512]{1,0:T(1,128)S(1)} %add_divide_fusion.refs_2_) | copy-start | bytes 6148
  84.4 3.4 %collective-permute-start.13 = (f32[3,512]{1,0:T(4,128)S(1)}, f32[3,512]{1,0:T(4,128)S(1)}, u32[]{:S(2)}, u32[]{:S(2)}) collective-permute-start(f32[3,512]{1,0:T(4,128)S(1)} %pad_maximum_fusion.16), channel_id=1, source_target_pairs={{0,1},{1,0},{2,3},{3,2},{4,5},{5,4},{6,7},{7,6},{8,9},{9,8},{10,11... | collective-permute-start | bytes 18440 | tf_op jit(solution)/shard_map/ppermute | solution.py:24
  85.3 20.7 %collective-permute-start.18 = (f16[256,512]{1,0:T(8,128)(2,1)}, f16[256,512]{1,0:T(8,128)(2,1)}, u32[]{:S(2)}, u32[]{:S(2)}) collective-permute-start(f16[256,512]{1,0:T(8,128)(2,1)} %pad_maximum_fusion.12), channel_id=1, source_target_pairs={{0,8},{1,5},{2,10},{3,7},{4,12},{5,1},{6,14},{7,3},{8,0},{9,13},{1... | collective-permute-start | bytes 786440 | tf_op jit(solution)/shard_map/ppermute | solution.py:44
  87.9 3.8 %collective-permute-start.14 = (f32[3,512]{1,0:T(4,128)S(1)}, f32[3,512]{1,0:T(4,128)S(1)}, u32[]{:S(2)}, u32[]{:S(2)}) collective-permute-start(f32[3,512]{1,0:T(4,128)S(1)} %fusion.17), channel_id=1, source_target_pairs={{0,2},{1,3},{2,0},{3,1},{4,6},{5,7},{6,4},{7,5},{8,10},{9,11},{10,... | collective-permute-start | bytes 18440 | tf_op jit(solution)/shard_map/ppermute | solution.py:24
  89.4 16.5 %collective-permute-start.19 = (f16[128,512]{1,0:T(8,128)(2,1)S(1)}, f16[128,512]{1,0:T(8,128)(2,1)S(1)}, u32[]{:S(2)}, u32[]{:S(2)}) collective-permute-start(f16[128,512]{1,0:T(8,128)(2,1)S(1)} %get-tuple-element.66), channel_id=1, source_target_pairs={{0,16},{1,17},{2,18},{3,19},{4,20},{5,21},{6,22},{7,23},{8,24},{9,... | collective-permute-start | bytes 393224 | tf_op jit(solution)/shard_map/ppermute | solution.py:44
  91.7 3.7 %collective-permute-start.15 = (f32[3,512]{1,0:T(4,128)S(1)}, f32[3,512]{1,0:T(4,128)S(1)}, u32[]{:S(2)}, u32[]{:S(2)}) collective-permute-start(f32[3,512]{1,0:T(4,128)S(1)} %fusion.24), channel_id=1, source_target_pairs={{0,4},{4,0},{8,12},{12,8},{16,20},{20,16},{24,28},{28,24},{1,5},{5... | collective-permute-start | bytes 18440 | tf_op jit(solution)/shard_map/ppermute | solution.py:24
  95.4 3.9 %collective-permute-start.16 = (f32[3,512]{1,0:T(4,128)S(1)}, f32[3,512]{1,0:T(4,128)S(1)}, u32[]{:S(2)}, u32[]{:S(2)}) collective-permute-start(f32[3,512]{1,0:T(4,128)S(1)} %add.207), channel_id=1, source_target_pairs={{0,8},{4,12},{8,0},{12,4},{16,24},{20,28},{24,16},{28,20},{1,9},{5... | collective-permute-start | bytes 18440 | tf_op jit(solution)/shard_map/ppermute | solution.py:24
  99.3 4.5 %collective-permute-start.17 = (f32[3,512]{1,0:T(4,128)S(1)}, f32[3,512]{1,0:T(4,128)S(1)}, u32[]{:S(2)}, u32[]{:S(2)}) collective-permute-start(f32[3,512]{1,0:T(4,128)S(1)} %add.208), channel_id=1, source_target_pairs={{0,16},{4,20},{8,24},{12,28},{16,0},{20,4},{24,8},{28,12},{1,17},{... | collective-permute-start | bytes 18440 | tf_op jit(solution)/shard_map/ppermute | solution.py:24
  105.9 12.0 %copy-start.8 = (bf16[256,512]{1,0:T(8,128)(2,1)S(1)}, bf16[256,512]{1,0:T(8,128)(2,1)}, u32[]{:S(2)}) copy-start(bf16[256,512]{1,0:T(8,128)(2,1)} %copy-done.7) | copy-start | bytes 786436
  107.1 9.9 %collective-permute-start.20 = (f16[512,512]{1,0:T(8,128)(2,1)S(1)}, f16[512,512]{1,0:T(8,128)(2,1)S(1)}, u32[]{:S(2)}, u32[]{:S(2)}) collective-permute-start(f16[512,512]{1,0:T(8,128)(2,1)S(1)} %pad_maximum_fusion.4), channel_id=1, source_target_pairs={{0,4},{1,9},{2,6},{3,11},{4,0},{5,13},{6,2},{7,15},{8,12},{9,1},{1... | collective-permute-start | bytes 1572872 | tf_op jit(solution)/shard_map/ppermute | solution.py:44
  109.3 6.6 %collective-permute-start.21 = (f16[256,512]{1,0:T(8,128)(2,1)S(1)}, f16[256,512]{1,0:T(8,128)(2,1)S(1)}, u32[]{:S(2)}, u32[]{:S(2)}) collective-permute-start(f16[256,512]{1,0:T(8,128)(2,1)S(1)} %pad_maximum_fusion.13), channel_id=1, source_target_pairs={{0,8},{1,5},{2,10},{3,7},{4,12},{5,1},{6,14},{7,3},{8,0},{9,13},{1... | collective-permute-start | bytes 786440 | tf_op jit(solution)/shard_map/ppermute | solution.py:44
  117.1 18.0 %collective-permute-start.22 = (f16[512,512]{1,0:T(8,128)(2,1)S(1)}, f16[512,512]{1,0:T(8,128)(2,1)S(1)}, u32[]{:S(2)}, u32[]{:S(2)}) collective-permute-start(f16[512,512]{1,0:T(8,128)(2,1)S(1)} %pad_maximum_fusion.5), channel_id=1, source_target_pairs={{0,4},{1,9},{2,6},{3,11},{4,0},{5,13},{6,2},{7,15},{8,12},{9,1},{1... | collective-permute-start | bytes 1572872 | tf_op jit(solution)/shard_map/ppermute | solution.py:44
  119.3 2.8 %copy-start.3 = (bf16[3072,1024]{1,0:T(8,128)(2,1)S(1)}, bf16[3072,1024]{1,0:T(8,128)(2,1)}, u32[]{:S(2)}) copy-start(bf16[3072,1024]{1,0:T(8,128)(2,1)} %copy-done.2) | copy-start | bytes 18874372
  122.1 2.8 %copy-start.5 = (bf16[3072,1024]{1,0:T(8,128)(2,1)S(1)}, bf16[3072,1024]{1,0:T(8,128)(2,1)}, u32[]{:S(2)}) copy-start(bf16[3072,1024]{1,0:T(8,128)(2,1)} %copy-done.4) | copy-start | bytes 18874372
  133.8 11.7 %collective-permute-start.24 = (f16[512,512]{1,0:T(8,128)(2,1)S(1)}, f16[512,512]{1,0:T(8,128)(2,1)S(1)}, u32[]{:S(2)}, u32[]{:S(2)}) collective-permute-start(f16[512,512]{1,0:T(8,128)(2,1)S(1)} %slice_convert_fusion), channel_id=1, source_target_pairs={{0,4},{1,9},{2,6},{3,11},{4,0},{5,13},{6,2},{7,15},{8,12},{9,1},{1... | collective-permute-start | bytes 1572872 | tf_op jit(solution)/shard_map/ppermute | solution.py:44
  144.2 1.2 collective-permute-start.25
  144.4 12.1 %collective-permute-start.23 = (f16[512,512]{1,0:T(8,128)(2,1)S(1)}, f16[512,512]{1,0:T(8,128)(2,1)S(1)}, u32[]{:S(2)}, u32[]{:S(2)}) collective-permute-start(f16[512,512]{1,0:T(8,128)(2,1)S(1)} %slice_convert_fusion.1), channel_id=1, source_target_pairs={{0,4},{1,9},{2,6},{3,11},{4,0},{5,13},{6,2},{7,15},{8,12},{9,1},{1... | collective-permute-start | bytes 1572872 | tf_op jit(solution)/shard_map/ppermute | solution.py:44
  145.5 3.7 %collective-permute-start.26 = (f32[1,512]{1,0:T(1,128)S(1)}, f32[1,512]{1,0:T(1,128)S(1)}, u32[]{:S(2)}, u32[]{:S(2)}) collective-permute-start(f32[1,512]{1,0:T(1,128)S(1)} %add.219), channel_id=1, source_target_pairs={{0,2},{1,3},{2,0},{3,1},{4,6},{5,7},{6,4},{7,5},{8,10},{9,11},{10,... | collective-permute-start | bytes 6152 | tf_op jit(solution)/shard_map/ppermute | solution.py:24
  147.2 12.9 %collective-permute-start.28 = (f16[256,512]{1,0:T(8,128)(2,1)S(1)}, f16[256,512]{1,0:T(8,128)(2,1)S(1)}, u32[]{:S(2)}, u32[]{:S(2)}) collective-permute-start(f16[256,512]{1,0:T(8,128)(2,1)S(1)} %slice_convert_fusion.4), channel_id=1, source_target_pairs={{0,8},{1,5},{2,10},{3,7},{4,12},{5,1},{6,14},{7,3},{8,0},{9,13},{1... | collective-permute-start | bytes 786440 | tf_op jit(solution)/shard_map/ppermute | solution.py:44
  156.5 3.7 %collective-permute-start.29 = (f32[1,512]{1,0:T(1,128)S(1)}, f32[1,512]{1,0:T(1,128)S(1)}, u32[]{:S(2)}, u32[]{:S(2)}) collective-permute-start(f32[1,512]{1,0:T(1,128)S(1)} %add.220), channel_id=1, source_target_pairs={{0,4},{4,0},{8,12},{12,8},{16,20},{20,16},{24,28},{28,24},{1,5},{5... | collective-permute-start | bytes 6152 | tf_op jit(solution)/shard_map/ppermute | solution.py:24
  157.5 7.2 %collective-permute-start.27 = (f16[256,512]{1,0:T(8,128)(2,1)S(1)}, f16[256,512]{1,0:T(8,128)(2,1)S(1)}, u32[]{:S(2)}, u32[]{:S(2)}) collective-permute-start(f16[256,512]{1,0:T(8,128)(2,1)S(1)} %slice_convert_fusion.5), channel_id=1, source_target_pairs={{0,8},{1,5},{2,10},{3,7},{4,12},{5,1},{6,14},{7,3},{8,0},{9,13},{1... | collective-permute-start | bytes 786440 | tf_op jit(solution)/shard_map/ppermute | solution.py:44
  160.2 4.5 %collective-permute-start.30 = (f32[1,512]{1,0:T(1,128)S(1)}, f32[1,512]{1,0:T(1,128)S(1)}, u32[]{:S(2)}, u32[]{:S(2)}) collective-permute-start(f32[1,512]{1,0:T(1,128)S(1)} %add.223), channel_id=1, source_target_pairs={{0,8},{4,12},{8,0},{12,4},{16,24},{20,28},{24,16},{28,20},{1,9},{5... | collective-permute-start | bytes 6152 | tf_op jit(solution)/shard_map/ppermute | solution.py:24
  162.1 11.4 %collective-permute-start.32 = (f16[128,512]{1,0:T(8,128)(2,1)S(1)}, f16[128,512]{1,0:T(8,128)(2,1)S(1)}, u32[]{:S(2)}, u32[]{:S(2)}) collective-permute-start(f16[128,512]{1,0:T(8,128)(2,1)S(1)} %slice_convert_fusion.9), channel_id=1, source_target_pairs={{0,16},{1,17},{2,18},{3,19},{4,20},{5,21},{6,22},{7,23},{8,24},{9,... | collective-permute-start | bytes 393224 | tf_op jit(solution)/shard_map/ppermute | solution.py:44
  164.7 6.7 %collective-permute-start.31 = (f32[1,512]{1,0:T(1,128)S(1)}, f32[1,512]{1,0:T(1,128)S(1)}, u32[]{:S(2)}, u32[]{:S(2)}) collective-permute-start(f32[1,512]{1,0:T(1,128)S(1)} %add.224), channel_id=1, source_target_pairs={{0,16},{4,20},{8,24},{12,28},{16,0},{20,4},{24,8},{28,12},{1,17},{... | collective-permute-start | bytes 6152 | tf_op jit(solution)/shard_map/ppermute | solution.py:24
  168.0 7.1 %collective-permute-start.33 = (f16[128,512]{1,0:T(8,128)(2,1)S(1)}, f16[128,512]{1,0:T(8,128)(2,1)S(1)}, u32[]{:S(2)}, u32[]{:S(2)}) collective-permute-start(f16[128,512]{1,0:T(8,128)(2,1)S(1)} %slice_convert_fusion.8), channel_id=1, source_target_pairs={{0,16},{1,17},{2,18},{3,19},{4,20},{5,21},{6,22},{7,23},{8,24},{9,... | collective-permute-start | bytes 393224 | tf_op jit(solution)/shard_map/ppermute | solution.py:44
  (1 other events, 0.9 us)

commit v6 on v5

--- a/solution.py
+++ b/solution.py
@@ -238,7 +238,7 @@
     features, curvature = load(features, curvature)
     grad = [task_grad[:, k * width : (k + 1) * width] for k in chunks]
 
-    held = [g.astype(jnp.bfloat16) for g in grad]
+    held = list(tie([g.astype(jnp.bfloat16) for g in grad]))
     for step in range(steps):
         grad_rows = [(h, trade(h, step)) for h in held]
         if step + 1 < steps:

time: 177 us -> 182 us (1.028)
  waiting for transfers between devices: 64.5 us -> 74.7 us
  starting transfers between devices: 49.4 us -> 40.6 us
  other arithmetic: 10.9 us -> 14.1 us
    ppermute x24, starting transfers between devices: 36.7 us -> 30 us  [trade(): return lax.ppermute(values, ('dp', 'mp'), pairs)]
    ppermute x24, waiting for transfers between devices: 49.3 us -> 54.6 us  [trade(): return lax.ppermute(values, ('dp', 'mp'), pairs)]
    ppermute x10, waiting for transfers between devices: 15.2 us -> 20 us  [swap(): return lax.ppermute(values, axis, [(i, i ^ stride) for i in range(size)])]
    ppermute x10, starting transfers between devices: 12.7 us -> 10.6 us  [swap(): return lax.ppermute(values, axis, [(i, i ^ stride) for i in range(size)])]
    concatenate x14 -> x12, other arithmetic: 2.69 us -> 4.41 us  [join(): return jnp.concatenate(halves, axis=0)]
    unnamed x30 -> x29, local copies, waits for them, and re-layouts: 11.2 us -> 11.2 us
  transfers between devices with their start and end apart: 34 -> 34, of which waited for: 19 -> 20; matrix products, arithmetic and copies ran while one was open for 5% -> 6% of each run, Pallas kernels for 21% -> 21%
where the time goes in v6:
time: 182 us; the launch traced here: 181 us
  waiting for transfers between devices  74.7 us (41%)
  starting transfers between devices  40.6 us (22%)
  Pallas kernels  37.6 us (21%)
  other arithmetic  14.1 us (8%)
  local copies, waits for them, and re-layouts  13.2 us (7%)
    ppermute x24, waiting for transfers between devices, trade(): return lax.ppermute(values, ('dp', 'mp'), pairs)  54.6 us
    pallas_call x4, Pallas kernels, curve(): pl.pallas_call(lambda *refs: curve_kernel(*refs, n_dp=n_dp, token_count=n...  35.2 us
    ppermute x24, starting transfers between devices, trade(): return lax.ppermute(values, ('dp', 'mp'), pairs)  30 us
    ppermute x10, waiting for transfers between devices, swap(): return lax.ppermute(values, axis, [(i, i ^ stride) for i in range(size)])  20 us
    unnamed x29, local copies, waits for them, and re-layouts  11.2 us
    ppermute x10, starting transfers between devices, swap(): return lax.ppermute(values, axis, [(i, i ^ stride) for i in range(size)])  10.6 us
    concatenate x12, other arithmetic, join(): return jnp.concatenate(halves, axis=0)  4.41 us
  transfers between devices with their start and end apart: 34, of which 20 were waited for; matrix products, arithmetic and copies ran while one was open for 6% of the time, Pallas kernels for 21%

profile of v6, /device:TPU:0, one launch (start us, length us, event | category | flops | bytes accessed | tf_op | source)
XLA Modules:
  0.0 181.4 jit_solution(13247642930594824255)
XLA Ops:
  0.6 1.1 fusion.22
  1.7 4.1 %collective-permute-start = (bf16[128,512]{1,0:T(8,128)(2,1)S(1)}, bf16[128,512]{1,0:T(8,128)(2,1)S(1)}, u32[]{:S(2)}, u32[]{:S(2)}) collective-permute-start(bf16[128,512]{1,0:T(8,128)(2,1)S(1)} %get-tuple-element.34), channel_id=1, source_target_pairs={{0,16},{1,17},{2,18},{3,19},{4,20},{5,21},{6,22},{7,23},{8,24},{9,... | collective-permute-start | bytes 393224 | tf_op jit(solution)/shard_map/ppermute | solution.py:44
  5.8 6.3 %collective-permute-done = bf16[128,512]{1,0:T(8,128)(2,1)S(1)} collective-permute-done((bf16[128,512]{1,0:T(8,128)(2,1)S(1)}, bf16[128,512]{1,0:T(8,128)(2,1)S(1)}, u32[]{:S(2)}, u32[]{:S(2)}) %collective-permute-start) | collective-permute-done | bytes 131104 | tf_op jit(solution)/shard_map/ppermute | solution.py:44
  12.9 3.4 %collective-permute-start.5 = (bf16[128,512]{1,0:T(8,128)(2,1)S(1)}, bf16[128,512]{1,0:T(8,128)(2,1)S(1)}, u32[]{:S(2)}, u32[]{:S(2)}) collective-permute-start(bf16[128,512]{1,0:T(8,128)(2,1)S(1)} %get-tuple-element.37), channel_id=1, source_target_pairs={{0,16},{1,17},{2,18},{3,19},{4,20},{5,21},{6,22},{7,23},{8,24},{9,... | collective-permute-start | bytes 393224 | tf_op jit(solution)/shard_map/ppermute | solution.py:44
  16.3 2.8 %copy-done = bf16[3072,1024]{1,0:T(8,128)(2,1)S(1)} copy-done((bf16[3072,1024]{1,0:T(8,128)(2,1)S(1)}, bf16[3072,1024]{1,0:T(8,128)(2,1)}, u32[]{:S(2)}) %copy-start) | copy-done | bytes 6291480
  19.1 2.8 %copy-done.1 = bf16[3072,1024]{1,0:T(8,128)(2,1)S(1)} copy-done((bf16[3072,1024]{1,0:T(8,128)(2,1)S(1)}, bf16[3072,1024]{1,0:T(8,128)(2,1)}, u32[]{:S(2)}) %copy-start.1) | copy-done | bytes 6291480
  22.8 1.6 collective-permute-start.2
  24.6 8.5 %collective-permute-done.6 = bf16[256,512]{1,0:T(8,128)(2,1)S(1)} collective-permute-done((bf16[256,512]{1,0:T(8,128)(2,1)S(1)}, bf16[256,512]{1,0:T(8,128)(2,1)S(1)}, u32[]{:S(2)}, u32[]{:S(2)}) %collective-permute-start.6) | collective-permute-done | bytes 262176 | tf_op jit(solution)/shard_map/ppermute | solution.py:44
  34.7 8.7 %shard_map.69 = (f32[1024,512]{1,0:T(8,128)S(1)}, f32[8,512]{1,0:T(8,128)S(1)}) custom-call(s32[8]{0:T(128)S(1)} %fusion.16.refs_0_, bf16[3072,1024]{1,0:T(8,128)(2,1)S(1)} %get-tuple-element.32.refs_1_, bf16[3072,1024]{1,0:T(8,128)(2,1)S(1)} %get-tuple-element.33.refs_2_, bf16[512,512]{1,0:T(8,128)(2,1)S(1)} %constant_dynamic-update-slice_fusion.refs_3_, ...), custom_call_target="tpu_custom_call" | custom-call | flops 6442450944 | bytes 12582912 | tf_op jit(solution)/shard_map/pallas_call | solution.py:181
  44.3 8.9 %shard_map.70 = (f32[1024,512]{1,0:T(8,128)S(1)}, f32[8,512]{1,0:T(8,128)S(1)}) custom-call(s32[8]{0:T(128)S(1)} %fusion.16.refs_0_, bf16[3072,1024]{1,0:T(8,128)(2,1)S(1)} %get-tuple-element.32.refs_1_, bf16[3072,1024]{1,0:T(8,128)(2,1)S(1)} %get-tuple-element.33.refs_2_, bf16[512,512]{1,0:T(8,128)(2,1)S(1)} %constant_dynamic-update-slice_fusion.3.refs_3_, ...), custom_call_target="tpu_custom_call" | custom-call | flops 6442450944 | bytes 12582912 | tf_op jit(solution)/shard_map/pallas_call | solution.py:181
  53.5 1.5 collective-permute-start.8
  55.7 9.1 %collective-permute-done.8 = f16[528,512]{1,0:T(8,128)(2,1)S(1)} collective-permute-done((f16[528,512]{1,0:T(8,128)(2,1)S(1)}, f16[528,512]{1,0:T(8,128)(2,1)S(1)}, u32[]{:S(2)}, u32[]{:S(2)}) %collective-permute-start.8) | collective-permute-done | bytes 540704 | tf_op jit(solution)/shard_map/ppermute | solution.py:44
  65.3 1.8 collective-permute-start.10
  67.4 6.6 %collective-permute-done.10 = f16[272,512]{1,0:T(8,128)(2,1)S(1)} collective-permute-done((f16[272,512]{1,0:T(8,128)(2,1)S(1)}, f16[272,512]{1,0:T(8,128)(2,1)S(1)}, u32[]{:S(2)}, u32[]{:S(2)}) %collective-permute-start.10) | collective-permute-done | bytes 278560 | tf_op jit(solution)/shard_map/ppermute | solution.py:44
  74.0 4.4 %collective-permute-done.9 = f16[144,512]{1,0:T(8,128)(2,1)S(1)} collective-permute-done((f16[144,512]{1,0:T(8,128)(2,1)S(1)}, f16[144,512]{1,0:T(8,128)(2,1)S(1)}, u32[]{:S(2)}, u32[]{:S(2)}) %collective-permute-start.9) | collective-permute-done | bytes 147488 | tf_op jit(solution)/shard_map/ppermute | solution.py:44
  78.8 3.0 %collective-permute-start.12 = (f16[144,512]{1,0:T(8,128)(2,1)S(1)}, f16[144,512]{1,0:T(8,128)(2,1)S(1)}, u32[]{:S(2)}, u32[]{:S(2)}) collective-permute-start(f16[144,512]{1,0:T(8,128)(2,1)S(1)} %pad_maximum_fusion.13), channel_id=1, source_target_pairs={{0,16},{1,17},{2,18},{3,19},{4,20},{5,21},{6,22},{7,23},{8,24},{9,... | collective-permute-start | bytes 442376 | tf_op jit(solution)/shard_map/ppermute | solution.py:44
  81.8 5.0 %collective-permute-done.12 = f16[144,512]{1,0:T(8,128)(2,1)S(1)} collective-permute-done((f16[144,512]{1,0:T(8,128)(2,1)S(1)}, f16[144,512]{1,0:T(8,128)(2,1)S(1)}, u32[]{:S(2)}, u32[]{:S(2)}) %collective-permute-start.12) | collective-permute-done | bytes 147488 | tf_op jit(solution)/shard_map/ppermute | solution.py:44
  88.4 1.6 collective-permute-start.14
  90.9 1.2 collective-permute-done.14
  92.1 1.5 collective-permute-start.15
  93.6 2.2 %collective-permute-done.15 = f32[3,512]{1,0:T(4,128)S(1)} collective-permute-done((f32[3,512]{1,0:T(4,128)S(1)}, f32[3,512]{1,0:T(4,128)S(1)}, u32[]{:S(2)}, u32[]{:S(2)}) %collective-permute-start.15) | collective-permute-done | bytes 6176 | tf_op jit(solution)/shard_map/ppermute | solution.py:24
  95.8 1.6 collective-permute-start.16
  97.5 2.0 %collective-permute-done.16 = f32[3,512]{1,0:T(4,128)S(1)} collective-permute-done((f32[3,512]{1,0:T(4,128)S(1)}, f32[3,512]{1,0:T(4,128)S(1)}, u32[]{:S(2)}, u32[]{:S(2)}) %collective-permute-start.16) | collective-permute-done | bytes 6176 | tf_op jit(solution)/shard_map/ppermute | solution.py:24
  100.5 3.5 %collective-permute-done.17 = f32[3,512]{1,0:T(4,128)S(1)} collective-permute-done((f32[3,512]{1,0:T(4,128)S(1)}, f32[3,512]{1,0:T(4,128)S(1)}, u32[]{:S(2)}, u32[]{:S(2)}) %collective-permute-start.17) | collective-permute-done | bytes 6176 | tf_op jit(solution)/shard_map/ppermute | solution.py:24
  104.6 1.5 shard_map.71
  106.1 1.1 pad_maximum_fusion.2
  107.3 1.5 collective-permute-start.20
  110.6 1.7 collective-permute-start.21
  112.5 4.5 %collective-permute-done.21 = f16[256,512]{1,0:T(8,128)(2,1)S(1)} collective-permute-done((f16[256,512]{1,0:T(8,128)(2,1)S(1)}, f16[256,512]{1,0:T(8,128)(2,1)S(1)}, u32[]{:S(2)}, u32[]{:S(2)}) %collective-permute-start.21) | collective-permute-done | bytes 262176 | tf_op jit(solution)/shard_map/ppermute | solution.py:44
  117.0 1.9 %collective-permute-done.20 = f16[512,512]{1,0:T(8,128)(2,1)S(1)} collective-permute-done((f16[512,512]{1,0:T(8,128)(2,1)S(1)}, f16[512,512]{1,0:T(8,128)(2,1)S(1)}, u32[]{:S(2)}, u32[]{:S(2)}) %collective-permute-start.20) | collective-permute-done | bytes 524320 | tf_op jit(solution)/shard_map/ppermute | solution.py:44
  118.9 1.1 pad_maximum_fusion.3
  120.4 1.4 add_convert_fusion
  121.8 2.8 %copy-done.3 = bf16[3072,1024]{1,0:T(8,128)(2,1)S(1)} copy-done((bf16[3072,1024]{1,0:T(8,128)(2,1)S(1)}, bf16[3072,1024]{1,0:T(8,128)(2,1)}, u32[]{:S(2)}) %copy-start.3) | copy-done | bytes 6291480
  124.6 2.8 %copy-done.5 = bf16[3072,1024]{1,0:T(8,128)(2,1)S(1)} copy-done((bf16[3072,1024]{1,0:T(8,128)(2,1)S(1)}, bf16[3072,1024]{1,0:T(8,128)(2,1)}, u32[]{:S(2)}) %copy-start.5) | copy-done | bytes 6291480
  127.3 8.7 %shard_map.73 = (f32[1024,512]{1,0:T(8,128)S(1)}, f32[8,512]{1,0:T(8,128)S(1)}) custom-call(s32[8]{0:T(128)S(1)} %fusion.16.refs_0_, bf16[3072,1024]{1,0:T(8,128)(2,1)S(1)} %copy-done.3, bf16[3072,1024]{1,0:T(8,128)(2,1)S(1)} %copy-done.5, bf16[512,512]{1,0:T(8,128)(2,1)S(1)} %get-tuple-element.104.refs_3_, bf16[512,512]{1,0:T(8,128)(2,1)S(1)} %get-tuple-element.103.refs_4_), custom_call_target="tpu_custom_call" | custom-call | flops 6442450944 | bytes 12582912 | tf_op jit(solution)/shard_map/pallas_call | solution.py:181
  136.1 1.8 collective-permute-start.24
  138.0 1.4 add_convert_fusion.2
  139.3 8.9 %shard_map.72 = (f32[1024,512]{1,0:T(8,128)S(1)}, f32[8,512]{1,0:T(8,128)S(1)}) custom-call(s32[8]{0:T(128)S(1)} %fusion.16.refs_0_, bf16[3072,1024]{1,0:T(8,128)(2,1)S(1)} %copy-done.3, bf16[3072,1024]{1,0:T(8,128)(2,1)S(1)} %copy-done.5, bf16[512,512]{1,0:T(8,128)(2,1)S(1)} %get-tuple-element.106.refs_3_, bf16[512,512]{1,0:T(8,128)(2,1)S(1)} %get-tuple-element.105.refs_4_), custom_call_target="tpu_custom_call" | custom-call | flops 6442450944 | bytes 12582912 | tf_op jit(solution)/shard_map/pallas_call | solution.py:181
  150.6 1.8 collective-permute-start.28
  153.2 7.3 %collective-permute-done.23 = f16[512,512]{1,0:T(8,128)(2,1)S(1)} collective-permute-done((f16[512,512]{1,0:T(8,128)(2,1)S(1)}, f16[512,512]{1,0:T(8,128)(2,1)S(1)}, u32[]{:S(2)}, u32[]{:S(2)}) %collective-permute-start.23) | collective-permute-done | bytes 524320 | tf_op jit(solution)/shard_map/ppermute | solution.py:44
  161.0 1.8 collective-permute-start.27
  162.8 1.3 collective-permute-done.29
  164.2 1.8 collective-permute-start.30
  166.4 1.7 collective-permute-done.30
  168.2 1.8 %collective-permute-start.31 = (f32[1,512]{1,0:T(1,128)S(1)}, f32[1,512]{1,0:T(1,128)S(1)}, u32[]{:S(2)}, u32[]{:S(2)}) collective-permute-start(f32[1,512]{1,0:T(1,128)S(1)} %add.224), channel_id=1, source_target_pairs={{0,16},{4,20},{8,24},{12,28},{16,0},{20,4},{24,8},{28,12},{1,17},{... | collective-permute-start | bytes 6152 | tf_op jit(solution)/shard_map/ppermute | solution.py:24
  170.1 1.2 collective-permute-start.33
  171.3 6.2 %collective-permute-done.31 = f32[1,512]{1,0:T(1,128)S(1)} collective-permute-done((f32[1,512]{1,0:T(1,128)S(1)}, f32[1,512]{1,0:T(1,128)S(1)}, u32[]{:S(2)}, u32[]{:S(2)}) %collective-permute-start.31) | collective-permute-done | bytes 2080 | tf_op jit(solution)/shard_map/ppermute | solution.py:24
  178.1 1.4 slice_divide_fusion.1
  (134 shorter events, 19.7 us)
Async XLA Ops:
  1.7 10.4 %collective-permute-start = (bf16[128,512]{1,0:T(8,128)(2,1)S(1)}, bf16[128,512]{1,0:T(8,128)(2,1)S(1)}, u32[]{:S(2)}, u32[]{:S(2)}) collective-permute-start(bf16[128,512]{1,0:T(8,128)(2,1)S(1)} %get-tuple-element.34), channel_id=1, source_target_pairs={{0,16},{1,17},{2,18},{3,19},{4,20},{5,21},{6,22},{7,23},{8,24},{9,... | collective-permute-start | bytes 393224 | tf_op jit(solution)/shard_map/ppermute | solution.py:44
  12.1 10.7 %collective-permute-start.1 = (bf16[256,512]{1,0:T(8,128)(2,1)S(1)}, bf16[256,512]{1,0:T(8,128)(2,1)S(1)}, u32[]{:S(2)}, u32[]{:S(2)}) collective-permute-start(bf16[256,512]{1,0:T(8,128)(2,1)S(1)} %pad_maximum_fusion.8), channel_id=1, source_target_pairs={{0,8},{1,5},{2,10},{3,7},{4,12},{5,1},{6,14},{7,3},{8,0},{9,13},{1... | collective-permute-start | bytes 786440 | tf_op jit(solution)/shard_map/ppermute | solution.py:44
  12.9 11.5 %collective-permute-start.5 = (bf16[128,512]{1,0:T(8,128)(2,1)S(1)}, bf16[128,512]{1,0:T(8,128)(2,1)S(1)}, u32[]{:S(2)}, u32[]{:S(2)}) collective-permute-start(bf16[128,512]{1,0:T(8,128)(2,1)S(1)} %get-tuple-element.37), channel_id=1, source_target_pairs={{0,16},{1,17},{2,18},{3,19},{4,20},{5,21},{6,22},{7,23},{8,24},{9,... | collective-permute-start | bytes 393224 | tf_op jit(solution)/shard_map/ppermute | solution.py:44
  16.3 2.8 %copy-start = (bf16[3072,1024]{1,0:T(8,128)(2,1)S(1)}, bf16[3072,1024]{1,0:T(8,128)(2,1)}, u32[]{:S(2)}) copy-start(bf16[3072,1024]{1,0:T(8,128)(2,1)} %f_ref.1) | copy-start | bytes 18874372
  19.1 2.8 %copy-start.1 = (bf16[3072,1024]{1,0:T(8,128)(2,1)S(1)}, bf16[3072,1024]{1,0:T(8,128)(2,1)}, u32[]{:S(2)}) copy-start(bf16[3072,1024]{1,0:T(8,128)(2,1)} %c_ref.1) | copy-start | bytes 18874372
  21.9 2.7 %copy-start.11 = (s32[8]{0:T(128)S(1)}, s32[8]{0:T(128)}, u32[]{:S(2)}) copy-start(s32[8]{0:T(128)} %constant.47.clone) | copy-start | bytes 100
  21.9 2.7 %copy-start.12 = (s32[8]{0:T(128)S(1)}, s32[8]{0:T(128)}, u32[]{:S(2)}) copy-start(s32[8]{0:T(128)} %constant.48.clone) | copy-start | bytes 100
  22.7 21.6 %copy-start.2 = (bf16[3072,1024]{1,0:T(8,128)(2,1)}, bf16[3072,1024]{1,0:T(8,128)(2,1)S(1)}, u32[]{:S(2)}) copy-start(bf16[3072,1024]{1,0:T(8,128)(2,1)S(1)} %get-tuple-element.32.refs_1_) | copy-start | bytes 18874372
  22.7 21.6 %copy-start.4 = (bf16[3072,1024]{1,0:T(8,128)(2,1)}, bf16[3072,1024]{1,0:T(8,128)(2,1)S(1)}, u32[]{:S(2)}) copy-start(bf16[3072,1024]{1,0:T(8,128)(2,1)S(1)} %get-tuple-element.33.refs_2_) | copy-start | bytes 18874372
  22.8 11.9 %collective-permute-start.2 = (bf16[512,512]{1,0:T(8,128)(2,1)S(1)}, bf16[512,512]{1,0:T(8,128)(2,1)S(1)}, u32[]{:S(2)}, u32[]{:S(2)}) collective-permute-start(bf16[512,512]{1,0:T(8,128)(2,1)S(1)} %constant_dynamic-update-slice_fusion.refs_3_), channel_id=1, source_target_pairs={{0,4},{1,9},{2,6},{3,11},{4,0},{5,13},{6,2},{7,15},{8,12},{9,1},{1... | collective-permute-start | bytes 1572872 | tf_op jit(solution)/shard_map/ppermute | solution.py:44
  24.4 8.7 %collective-permute-start.6 = (bf16[256,512]{1,0:T(8,128)(2,1)S(1)}, bf16[256,512]{1,0:T(8,128)(2,1)S(1)}, u32[]{:S(2)}, u32[]{:S(2)}) collective-permute-start(bf16[256,512]{1,0:T(8,128)(2,1)S(1)} %pad_maximum_fusion.9), channel_id=1, source_target_pairs={{0,8},{1,5},{2,10},{3,7},{4,12},{5,1},{6,14},{7,3},{8,0},{9,13},{1... | collective-permute-start | bytes 786440 | tf_op jit(solution)/shard_map/ppermute | solution.py:44
  33.2 11.1 %collective-permute-start.7 = (bf16[512,512]{1,0:T(8,128)(2,1)S(1)}, bf16[512,512]{1,0:T(8,128)(2,1)S(1)}, u32[]{:S(2)}, u32[]{:S(2)}) collective-permute-start(bf16[512,512]{1,0:T(8,128)(2,1)S(1)} %constant_dynamic-update-slice_fusion.3.refs_3_), channel_id=1, source_target_pairs={{0,4},{1,9},{2,6},{3,11},{4,0},{5,13},{6,2},{7,15},{8,12},{9,1},{1... | collective-permute-start | bytes 1572872 | tf_op jit(solution)/shard_map/ppermute | solution.py:44
  43.7 11.3 %collective-permute-start.3 = (f16[528,512]{1,0:T(8,128)(2,1)S(1)}, f16[528,512]{1,0:T(8,128)(2,1)S(1)}, u32[]{:S(2)}, u32[]{:S(2)}) collective-permute-start(f16[528,512]{1,0:T(8,128)(2,1)S(1)} %pad_maximum_fusion), channel_id=1, source_target_pairs={{0,4},{1,9},{2,6},{3,11},{4,0},{5,13},{6,2},{7,15},{8,12},{9,1},{1... | collective-permute-start | bytes 1622024 | tf_op jit(solution)/shard_map/ppermute | solution.py:44
  53.5 11.3 %collective-permute-start.8 = (f16[528,512]{1,0:T(8,128)(2,1)S(1)}, f16[528,512]{1,0:T(8,128)(2,1)S(1)}, u32[]{:S(2)}, u32[]{:S(2)}) collective-permute-start(f16[528,512]{1,0:T(8,128)(2,1)S(1)} %pad_maximum_fusion.1), channel_id=1, source_target_pairs={{0,4},{1,9},{2,6},{3,11},{4,0},{5,13},{6,2},{7,15},{8,12},{9,1},{1... | collective-permute-start | bytes 1622024 | tf_op jit(solution)/shard_map/ppermute | solution.py:44
  55.4 9.5 %collective-permute-start.4 = (f16[272,512]{1,0:T(8,128)(2,1)S(1)}, f16[272,512]{1,0:T(8,128)(2,1)S(1)}, u32[]{:S(2)}, u32[]{:S(2)}) collective-permute-start(f16[272,512]{1,0:T(8,128)(2,1)S(1)} %pad_maximum_fusion.6), channel_id=1, source_target_pairs={{0,8},{1,5},{2,10},{3,7},{4,12},{5,1},{6,14},{7,3},{8,0},{9,13},{1... | collective-permute-start | bytes 835592 | tf_op jit(solution)/shard_map/ppermute | solution.py:44
  65.0 13.3 %copy-start.6 = (f32[128,1024]{1,0:T(8,128)S(1)}, f32[128,1024]{1,0:T(8,128)}, u32[]{:S(2)}) copy-start(f32[128,1024]{1,0:T(8,128)} %param.7) | copy-start | bytes 1572868
  65.3 8.7 %collective-permute-start.10 = (f16[272,512]{1,0:T(8,128)(2,1)S(1)}, f16[272,512]{1,0:T(8,128)(2,1)S(1)}, u32[]{:S(2)}, u32[]{:S(2)}) collective-permute-start(f16[272,512]{1,0:T(8,128)(2,1)S(1)} %pad_maximum_fusion.7), channel_id=1, source_target_pairs={{0,8},{1,5},{2,10},{3,7},{4,12},{5,1},{6,14},{7,3},{8,0},{9,13},{1... | collective-permute-start | bytes 835592 | tf_op jit(solution)/shard_map/ppermute | solution.py:44
  67.1 11.2 %collective-permute-start.9 = (f16[144,512]{1,0:T(8,128)(2,1)S(1)}, f16[144,512]{1,0:T(8,128)(2,1)S(1)}, u32[]{:S(2)}, u32[]{:S(2)}) collective-permute-start(f16[144,512]{1,0:T(8,128)(2,1)S(1)} %pad_maximum_fusion.12), channel_id=1, source_target_pairs={{0,16},{1,17},{2,18},{3,19},{4,20},{5,21},{6,22},{7,23},{8,24},{9,... | collective-permute-start | bytes 442376 | tf_op jit(solution)/shard_map/ppermute | solution.py:44
  67.4 19.6 %copy-start.7 = (f32[1,512]{1,0:T(1,128)}, f32[1,512]{1,0:T(1,128)S(1)}, u32[]{:S(2)}) copy-start(f32[1,512]{1,0:T(1,128)S(1)} %get-tuple-element.102.refs_1_) | copy-start | bytes 6148
  78.3 8.7 %copy-start.8 = (f32[1,512]{1,0:T(1,128)}, f32[1,512]{1,0:T(1,128)S(1)}, u32[]{:S(2)}) copy-start(f32[1,512]{1,0:T(1,128)S(1)} %add_divide_fusion.1.refs_0_) | copy-start | bytes 6148
  78.5 8.3 %collective-permute-start.11 = (f16[128,512]{1,0:T(8,128)(2,1)S(1)}, f16[128,512]{1,0:T(8,128)(2,1)S(1)}, u32[]{:S(2)}, u32[]{:S(2)}) collective-permute-start(f16[128,512]{1,0:T(8,128)(2,1)S(1)} %get-tuple-element.72), channel_id=1, source_target_pairs={{0,16},{1,17},{2,18},{3,19},{4,20},{5,21},{6,22},{7,23},{8,24},{9,... | collective-permute-start | bytes 393224 | tf_op jit(solution)/shard_map/ppermute | solution.py:44
  78.8 8.0 %collective-permute-start.12 = (f16[144,512]{1,0:T(8,128)(2,1)S(1)}, f16[144,512]{1,0:T(8,128)(2,1)S(1)}, u32[]{:S(2)}, u32[]{:S(2)}) collective-permute-start(f16[144,512]{1,0:T(8,128)(2,1)S(1)} %pad_maximum_fusion.13), channel_id=1, source_target_pairs={{0,16},{1,17},{2,18},{3,19},{4,20},{5,21},{6,22},{7,23},{8,24},{9,... | collective-permute-start | bytes 442376 | tf_op jit(solution)/shard_map/ppermute | solution.py:44
  81.7 22.9 %copy-start.9 = (f32[1,512]{1,0:T(1,128)}, f32[1,512]{1,0:T(1,128)S(1)}, u32[]{:S(2)}) copy-start(f32[1,512]{1,0:T(1,128)S(1)} %get-tuple-element.100.refs_3_) | copy-start | bytes 6148
  86.8 17.3 %copy-start.10 = (f32[1,512]{1,0:T(1,128)}, f32[1,512]{1,0:T(1,128)S(1)}, u32[]{:S(2)}) copy-start(f32[1,512]{1,0:T(1,128)S(1)} %add_divide_fusion.refs_2_) | copy-start | bytes 6148
  87.1 1.2 collective-permute-start.13
  88.0 18.2 %collective-permute-start.18 = (f16[256,512]{1,0:T(8,128)(2,1)}, f16[256,512]{1,0:T(8,128)(2,1)}, u32[]{:S(2)}, u32[]{:S(2)}) collective-permute-start(f16[256,512]{1,0:T(8,128)(2,1)} %pad_maximum_fusion.10), channel_id=1, source_target_pairs={{0,8},{1,5},{2,10},{3,7},{4,12},{5,1},{6,14},{7,3},{8,0},{9,13},{1... | collective-permute-start | bytes 786440 | tf_op jit(solution)/shard_map/ppermute | solution.py:44
  88.4 3.7 %collective-permute-start.14 = (f32[3,512]{1,0:T(4,128)S(1)}, f32[3,512]{1,0:T(4,128)S(1)}, u32[]{:S(2)}, u32[]{:S(2)}) collective-permute-start(f32[3,512]{1,0:T(4,128)S(1)} %fusion.17), channel_id=1, source_target_pairs={{0,2},{1,3},{2,0},{3,1},{4,6},{5,7},{6,4},{7,5},{8,10},{9,11},{10,... | collective-permute-start | bytes 18440 | tf_op jit(solution)/shard_map/ppermute | solution.py:24
  89.9 16.2 %collective-permute-start.19 = (f16[128,512]{1,0:T(8,128)(2,1)S(1)}, f16[128,512]{1,0:T(8,128)(2,1)}, u32[]{:S(2)}, u32[]{:S(2)}) collective-permute-start(f16[128,512]{1,0:T(8,128)(2,1)S(1)} %get-tuple-element.70), channel_id=1, source_target_pairs={{0,16},{1,17},{2,18},{3,19},{4,20},{5,21},{6,22},{7,23},{8,24},{9,... | collective-permute-start | bytes 393224 | tf_op jit(solution)/shard_map/ppermute | solution.py:44
  92.1 3.7 %collective-permute-start.15 = (f32[3,512]{1,0:T(4,128)S(1)}, f32[3,512]{1,0:T(4,128)S(1)}, u32[]{:S(2)}, u32[]{:S(2)}) collective-permute-start(f32[3,512]{1,0:T(4,128)S(1)} %fusion.24), channel_id=1, source_target_pairs={{0,4},{4,0},{8,12},{12,8},{16,20},{20,16},{24,28},{28,24},{1,5},{5... | collective-permute-start | bytes 18440 | tf_op jit(solution)/shard_map/ppermute | solution.py:24
  95.8 3.7 %collective-permute-start.16 = (f32[3,512]{1,0:T(4,128)S(1)}, f32[3,512]{1,0:T(4,128)S(1)}, u32[]{:S(2)}, u32[]{:S(2)}) collective-permute-start(f32[3,512]{1,0:T(4,128)S(1)} %add.207), channel_id=1, source_target_pairs={{0,8},{4,12},{8,0},{12,4},{16,24},{20,28},{24,16},{28,20},{1,9},{5... | collective-permute-start | bytes 18440 | tf_op jit(solution)/shard_map/ppermute | solution.py:24
  99.5 4.5 %collective-permute-start.17 = (f32[3,512]{1,0:T(4,128)S(1)}, f32[3,512]{1,0:T(4,128)S(1)}, u32[]{:S(2)}, u32[]{:S(2)}) collective-permute-start(f32[3,512]{1,0:T(4,128)S(1)} %add.208), channel_id=1, source_target_pairs={{0,16},{4,20},{8,24},{12,28},{16,0},{20,4},{24,8},{28,12},{1,17},{... | collective-permute-start | bytes 18440 | tf_op jit(solution)/shard_map/ppermute | solution.py:24
  107.3 11.7 %collective-permute-start.20 = (f16[512,512]{1,0:T(8,128)(2,1)S(1)}, f16[512,512]{1,0:T(8,128)(2,1)S(1)}, u32[]{:S(2)}, u32[]{:S(2)}) collective-permute-start(f16[512,512]{1,0:T(8,128)(2,1)S(1)} %pad_maximum_fusion.2), channel_id=1, source_target_pairs={{0,4},{1,9},{2,6},{3,11},{4,0},{5,13},{6,2},{7,15},{8,12},{9,1},{1... | collective-permute-start | bytes 1572872 | tf_op jit(solution)/shard_map/ppermute | solution.py:44
  110.6 6.4 %collective-permute-start.21 = (f16[256,512]{1,0:T(8,128)(2,1)S(1)}, f16[256,512]{1,0:T(8,128)(2,1)S(1)}, u32[]{:S(2)}, u32[]{:S(2)}) collective-permute-start(f16[256,512]{1,0:T(8,128)(2,1)S(1)} %pad_maximum_fusion.11), channel_id=1, source_target_pairs={{0,8},{1,5},{2,10},{3,7},{4,12},{5,1},{6,14},{7,3},{8,0},{9,13},{1... | collective-permute-start | bytes 786440 | tf_op jit(solution)/shard_map/ppermute | solution.py:44
  120.0 18.0 %collective-permute-start.22 = (f16[512,512]{1,0:T(8,128)(2,1)S(1)}, f16[512,512]{1,0:T(8,128)(2,1)S(1)}, u32[]{:S(2)}, u32[]{:S(2)}) collective-permute-start(f16[512,512]{1,0:T(8,128)(2,1)S(1)} %pad_maximum_fusion.3), channel_id=1, source_target_pairs={{0,4},{1,9},{2,6},{3,11},{4,0},{5,13},{6,2},{7,15},{8,12},{9,1},{1... | collective-permute-start | bytes 1572872 | tf_op jit(solution)/shard_map/ppermute | solution.py:44
  121.8 2.8 %copy-start.3 = (bf16[3072,1024]{1,0:T(8,128)(2,1)S(1)}, bf16[3072,1024]{1,0:T(8,128)(2,1)}, u32[]{:S(2)}) copy-start(bf16[3072,1024]{1,0:T(8,128)(2,1)} %copy-done.2) | copy-start | bytes 18874372
  124.6 2.8 %copy-start.5 = (bf16[3072,1024]{1,0:T(8,128)(2,1)S(1)}, bf16[3072,1024]{1,0:T(8,128)(2,1)}, u32[]{:S(2)}) copy-start(bf16[3072,1024]{1,0:T(8,128)(2,1)} %copy-done.4) | copy-start | bytes 18874372
  136.1 13.4 %collective-permute-start.24 = (f16[512,512]{1,0:T(8,128)(2,1)S(1)}, f16[512,512]{1,0:T(8,128)(2,1)S(1)}, u32[]{:S(2)}, u32[]{:S(2)}) collective-permute-start(f16[512,512]{1,0:T(8,128)(2,1)S(1)} %slice_convert_fusion), channel_id=1, source_target_pairs={{0,4},{1,9},{2,6},{3,11},{4,0},{5,13},{6,2},{7,15},{8,12},{9,1},{1... | collective-permute-start | bytes 1572872 | tf_op jit(solution)/shard_map/ppermute | solution.py:44
  148.3 1.2 collective-permute-start.25
  148.5 12.1 %collective-permute-start.23 = (f16[512,512]{1,0:T(8,128)(2,1)S(1)}, f16[512,512]{1,0:T(8,128)(2,1)S(1)}, u32[]{:S(2)}, u32[]{:S(2)}) collective-permute-start(f16[512,512]{1,0:T(8,128)(2,1)S(1)} %slice_convert_fusion.1), channel_id=1, source_target_pairs={{0,4},{1,9},{2,6},{3,11},{4,0},{5,13},{6,2},{7,15},{8,12},{9,1},{1... | collective-permute-start | bytes 1572872 | tf_op jit(solution)/shard_map/ppermute | solution.py:44
  149.5 3.7 %collective-permute-start.26 = (f32[1,512]{1,0:T(1,128)S(1)}, f32[1,512]{1,0:T(1,128)S(1)}, u32[]{:S(2)}, u32[]{:S(2)}) collective-permute-start(f32[1,512]{1,0:T(1,128)S(1)} %add.219), channel_id=1, source_target_pairs={{0,2},{1,3},{2,0},{3,1},{4,6},{5,7},{6,4},{7,5},{8,10},{9,11},{10,... | collective-permute-start | bytes 6152 | tf_op jit(solution)/shard_map/ppermute | solution.py:24
  150.6 13.6 %collective-permute-start.28 = (f16[256,512]{1,0:T(8,128)(2,1)S(1)}, f16[256,512]{1,0:T(8,128)(2,1)S(1)}, u32[]{:S(2)}, u32[]{:S(2)}) collective-permute-start(f16[256,512]{1,0:T(8,128)(2,1)S(1)} %slice_convert_fusion.4), channel_id=1, source_target_pairs={{0,8},{1,5},{2,10},{3,7},{4,12},{5,1},{6,14},{7,3},{8,0},{9,13},{1... | collective-permute-start | bytes 786440 | tf_op jit(solution)/shard_map/ppermute | solution.py:44
  160.5 3.6 %collective-permute-start.29 = (f32[1,512]{1,0:T(1,128)S(1)}, f32[1,512]{1,0:T(1,128)S(1)}, u32[]{:S(2)}, u32[]{:S(2)}) collective-permute-start(f32[1,512]{1,0:T(1,128)S(1)} %add.220), channel_id=1, source_target_pairs={{0,4},{4,0},{8,12},{12,8},{16,20},{20,16},{24,28},{28,24},{1,5},{5... | collective-permute-start | bytes 6152 | tf_op jit(solution)/shard_map/ppermute | solution.py:24
  161.0 7.2 %collective-permute-start.27 = (f16[256,512]{1,0:T(8,128)(2,1)S(1)}, f16[256,512]{1,0:T(8,128)(2,1)S(1)}, u32[]{:S(2)}, u32[]{:S(2)}) collective-permute-start(f16[256,512]{1,0:T(8,128)(2,1)S(1)} %slice_convert_fusion.5), channel_id=1, source_target_pairs={{0,8},{1,5},{2,10},{3,7},{4,12},{5,1},{6,14},{7,3},{8,0},{9,13},{1... | collective-permute-start | bytes 786440 | tf_op jit(solution)/shard_map/ppermute | solution.py:44
  164.2 3.9 %collective-permute-start.30 = (f32[1,512]{1,0:T(1,128)S(1)}, f32[1,512]{1,0:T(1,128)S(1)}, u32[]{:S(2)}, u32[]{:S(2)}) collective-permute-start(f32[1,512]{1,0:T(1,128)S(1)} %add.223), channel_id=1, source_target_pairs={{0,8},{4,12},{8,0},{12,4},{16,24},{20,28},{24,16},{28,20},{1,9},{5... | collective-permute-start | bytes 6152 | tf_op jit(solution)/shard_map/ppermute | solution.py:24
  166.0 13.4 %collective-permute-start.32 = (f16[128,512]{1,0:T(8,128)(2,1)S(1)}, f16[128,512]{1,0:T(8,128)(2,1)S(1)}, u32[]{:S(2)}, u32[]{:S(2)}) collective-permute-start(f16[128,512]{1,0:T(8,128)(2,1)S(1)} %slice_convert_fusion.9), channel_id=1, source_target_pairs={{0,16},{1,17},{2,18},{3,19},{4,20},{5,21},{6,22},{7,23},{8,24},{9,... | collective-permute-start | bytes 393224 | tf_op jit(solution)/shard_map/ppermute | solution.py:44
  168.2 9.3 %collective-permute-start.31 = (f32[1,512]{1,0:T(1,128)S(1)}, f32[1,512]{1,0:T(1,128)S(1)}, u32[]{:S(2)}, u32[]{:S(2)}) collective-permute-start(f32[1,512]{1,0:T(1,128)S(1)} %add.224), channel_id=1, source_target_pairs={{0,16},{4,20},{8,24},{12,28},{16,0},{20,4},{24,8},{28,12},{1,17},{... | collective-permute-start | bytes 6152 | tf_op jit(solution)/shard_map/ppermute | solution.py:24
  170.1 9.3 %collective-permute-start.33 = (f16[128,512]{1,0:T(8,128)(2,1)S(1)}, f16[128,512]{1,0:T(8,128)(2,1)S(1)}, u32[]{:S(2)}, u32[]{:S(2)}) collective-permute-start(f16[128,512]{1,0:T(8,128)(2,1)S(1)} %slice_convert_fusion.8), channel_id=1, source_target_pairs={{0,16},{1,17},{2,18},{3,19},{4,20},{5,21},{6,22},{7,23},{8,24},{9,... | collective-permute-start | bytes 393224 | tf_op jit(solution)/shard_map/ppermute | solution.py:44

commit v7 on v5

--- a/solution.py
+++ b/solution.py
@@ -278,7 +278,8 @@
         for k in chunks:
             held = join(moving[k])
             moving[k] = (held, trade(held, step))
-            moving[k : k + 2] = in_step(moving[k : k + 2])
+            if step + 1 < steps:
+                moving[k : k + 2] = in_step(moving[k : k + 2])
     while hops:
         hop()
     coef = pl.pallas_call(

time: 177 us -> 178 us (level)
  waiting for transfers between devices: 64.5 us -> 69.6 us
  starting transfers between devices: 49.4 us -> 46.1 us
    ppermute x24, waiting for transfers between devices: 49.3 us -> 52.9 us  [trade(): return lax.ppermute(values, ('dp', 'mp'), pairs)]
    ppermute x10, starting transfers between devices: 12.7 us -> 9.14 us  [swap(): return lax.ppermute(values, axis, [(i, i ^ stride) for i in range(size)])]
where the time goes in v7:
time: 178 us
  waiting for transfers between devices  69.6 us (39%)
  starting transfers between devices  46.1 us (26%)
  Pallas kernels  37.1 us (21%)
  local copies, waits for them, and re-layouts  13.2 us (7%)
  other arithmetic  10.7 us (6%)
    ppermute x24, waiting for transfers between devices, trade(): return lax.ppermute(values, ('dp', 'mp'), pairs)  52.9 us
    ppermute x24, starting transfers between devices, trade(): return lax.ppermute(values, ('dp', 'mp'), pairs)  37 us
    pallas_call x4, Pallas kernels, curve(): pl.pallas_call(lambda *refs: curve_kernel(*refs, n_dp=n_dp, token_count=n...  34.7 us
    ppermute x10, waiting for transfers between devices, swap(): return lax.ppermute(values, axis, [(i, i ^ stride) for i in range(size)])  16.7 us
    unnamed x30, local copies, waits for them, and re-layouts  11.2 us
    ppermute x10, starting transfers between devices, swap(): return lax.ppermute(values, axis, [(i, i ^ stride) for i in range(size)])  9.14 us
  transfers between devices with their start and end apart: 34, of which 19 were waited for; matrix products, arithmetic and copies ran while one was open for 5% of the time, Pallas kernels for 21%

profile of v7, /device:TPU:0, one launch (start us, length us, event | category | flops | bytes accessed | tf_op | source)
XLA Modules:
  0.0 178.0 jit_solution(13220586044595299275)
XLA Ops:
  1.7 4.1 %collective-permute-start = (bf16[128,512]{1,0:T(8,128)(2,1)S(1)}, bf16[128,512]{1,0:T(8,128)(2,1)S(1)}, u32[]{:S(2)}, u32[]{:S(2)}) collective-permute-start(bf16[128,512]{1,0:T(8,128)(2,1)S(1)} %get-tuple-element.76), channel_id=1, source_target_pairs={{0,16},{1,17},{2,18},{3,19},{4,20},{5,21},{6,22},{7,23},{8,24},{9,... | collective-permute-start | bytes 393224 | tf_op jit(solution)/shard_map/ppermute | solution.py:44
  5.8 6.3 %collective-permute-done = bf16[128,512]{1,0:T(8,128)(2,1)S(1)} collective-permute-done((bf16[128,512]{1,0:T(8,128)(2,1)S(1)}, bf16[128,512]{1,0:T(8,128)(2,1)S(1)}, u32[]{:S(2)}, u32[]{:S(2)}) %collective-permute-start) | collective-permute-done | bytes 131104 | tf_op jit(solution)/shard_map/ppermute | solution.py:44
  12.9 3.4 %collective-permute-start.5 = (bf16[128,512]{1,0:T(8,128)(2,1)S(1)}, bf16[128,512]{1,0:T(8,128)(2,1)S(1)}, u32[]{:S(2)}, u32[]{:S(2)}) collective-permute-start(bf16[128,512]{1,0:T(8,128)(2,1)S(1)} %get-tuple-element.77), channel_id=1, source_target_pairs={{0,16},{1,17},{2,18},{3,19},{4,20},{5,21},{6,22},{7,23},{8,24},{9,... | collective-permute-start | bytes 393224 | tf_op jit(solution)/shard_map/ppermute | solution.py:44
  16.3 6.2 %collective-permute-done.1 = bf16[256,512]{1,0:T(8,128)(2,1)S(1)} collective-permute-done((bf16[256,512]{1,0:T(8,128)(2,1)S(1)}, bf16[256,512]{1,0:T(8,128)(2,1)S(1)}, u32[]{:S(2)}, u32[]{:S(2)}) %collective-permute-start.1) | collective-permute-done | bytes 262176 | tf_op jit(solution)/shard_map/ppermute | solution.py:44
  24.1 2.8 %copy-done = bf16[3072,1024]{1,0:T(8,128)(2,1)S(1)} copy-done((bf16[3072,1024]{1,0:T(8,128)(2,1)S(1)}, bf16[3072,1024]{1,0:T(8,128)(2,1)}, u32[]{:S(2)}) %copy-start) | copy-done | bytes 6291480
  26.9 2.8 %copy-done.1 = bf16[3072,1024]{1,0:T(8,128)(2,1)S(1)} copy-done((bf16[3072,1024]{1,0:T(8,128)(2,1)S(1)}, bf16[3072,1024]{1,0:T(8,128)(2,1)}, u32[]{:S(2)}) %copy-start.1) | copy-done | bytes 6291480
  31.8 8.6 %shard_map.69 = (f32[1024,512]{1,0:T(8,128)S(1)}, f32[8,512]{1,0:T(8,128)S(1)}) custom-call(s32[8]{0:T(128)S(1)} %fusion.16.refs_0_, bf16[3072,1024]{1,0:T(8,128)(2,1)S(1)} %get-tuple-element.28.refs_1_, bf16[3072,1024]{1,0:T(8,128)(2,1)S(1)} %get-tuple-element.29.refs_2_, bf16[512,512]{1,0:T(8,128)(2,1)S(1)} %pad_maximum_fusion.2.refs_3_, ...), custom_call_target="tpu_custom_call" | custom-call | flops 6442450944 | bytes 12582912 | tf_op jit(solution)/shard_map/pallas_call | solution.py:181
  40.7 1.1 collective-permute-start.3
  41.8 8.6 %shard_map.70 = (f32[1024,512]{1,0:T(8,128)S(1)}, f32[8,512]{1,0:T(8,128)S(1)}) custom-call(s32[8]{0:T(128)S(1)} %fusion.16.refs_0_, bf16[3072,1024]{1,0:T(8,128)(2,1)S(1)} %get-tuple-element.28.refs_1_, bf16[3072,1024]{1,0:T(8,128)(2,1)S(1)} %get-tuple-element.29.refs_2_, bf16[512,512]{1,0:T(8,128)(2,1)S(1)} %pad_maximum_fusion.3.refs_3_, ...), custom_call_target="tpu_custom_call" | custom-call | flops 6442450944 | bytes 12582912 | tf_op jit(solution)/shard_map/pallas_call | solution.py:181
  50.7 1.1 collective-permute-start.8
  52.1 1.7 collective-permute-start.4
  53.7 7.9 %collective-permute-done.8 = f16[528,512]{1,0:T(8,128)(2,1)S(1)} collective-permute-done((f16[528,512]{1,0:T(8,128)(2,1)S(1)}, f16[528,512]{1,0:T(8,128)(2,1)S(1)}, u32[]{:S(2)}, u32[]{:S(2)}) %collective-permute-start.8) | collective-permute-done | bytes 540704 | tf_op jit(solution)/shard_map/ppermute | solution.py:44
  62.7 4.8 %collective-permute-start.9 = (f16[144,512]{1,0:T(8,128)(2,1)S(1)}, f16[144,512]{1,0:T(8,128)(2,1)S(1)}, u32[]{:S(2)}, u32[]{:S(2)}) collective-permute-start(f16[144,512]{1,0:T(8,128)(2,1)S(1)} %pad_maximum_fusion.14), channel_id=1, source_target_pairs={{0,16},{1,17},{2,18},{3,19},{4,20},{5,21},{6,22},{7,23},{8,24},{9,... | collective-permute-start | bytes 442376 | tf_op jit(solution)/shard_map/ppermute | solution.py:44
  67.5 1.9 %collective-permute-done.10 = f16[272,512]{1,0:T(8,128)(2,1)S(1)} collective-permute-done((f16[272,512]{1,0:T(8,128)(2,1)S(1)}, f16[272,512]{1,0:T(8,128)(2,1)S(1)}, u32[]{:S(2)}, u32[]{:S(2)}) %collective-permute-start.10) | collective-permute-done | bytes 278560 | tf_op jit(solution)/shard_map/ppermute | solution.py:44
  69.4 5.4 %collective-permute-done.9 = f16[144,512]{1,0:T(8,128)(2,1)S(1)} collective-permute-done((f16[144,512]{1,0:T(8,128)(2,1)S(1)}, f16[144,512]{1,0:T(8,128)(2,1)S(1)}, u32[]{:S(2)}, u32[]{:S(2)}) %collective-permute-start.9) | collective-permute-done | bytes 147488 | tf_op jit(solution)/shard_map/ppermute | solution.py:44
  75.9 2.3 %collective-permute-start.12 = (f16[144,512]{1,0:T(8,128)(2,1)S(1)}, f16[144,512]{1,0:T(8,128)(2,1)S(1)}, u32[]{:S(2)}, u32[]{:S(2)}) collective-permute-start(f16[144,512]{1,0:T(8,128)(2,1)S(1)} %pad_maximum_fusion.15), channel_id=1, source_target_pairs={{0,16},{1,17},{2,18},{3,19},{4,20},{5,21},{6,22},{7,23},{8,24},{9,... | collective-permute-start | bytes 442376 | tf_op jit(solution)/shard_map/ppermute | solution.py:44
  78.3 5.6 %collective-permute-done.12 = f16[144,512]{1,0:T(8,128)(2,1)S(1)} collective-permute-done((f16[144,512]{1,0:T(8,128)(2,1)S(1)}, f16[144,512]{1,0:T(8,128)(2,1)S(1)}, u32[]{:S(2)}, u32[]{:S(2)}) %collective-permute-start.12) | collective-permute-done | bytes 147488 | tf_op jit(solution)/shard_map/ppermute | solution.py:44
  84.4 1.2 collective-permute-done.13
  85.5 1.6 collective-permute-start.14
  87.9 2.6 %collective-permute-start.18 = (f16[256,512]{1,0:T(8,128)(2,1)}, f16[256,512]{1,0:T(8,128)(2,1)}, u32[]{:S(2)}, u32[]{:S(2)}) collective-permute-start(f16[256,512]{1,0:T(8,128)(2,1)} %pad_maximum_fusion.12), channel_id=1, source_target_pairs={{0,8},{1,5},{2,10},{3,7},{4,12},{5,1},{6,14},{7,3},{8,0},{9,13},{1... | collective-permute-start | bytes 786440 | tf_op jit(solution)/shard_map/ppermute | solution.py:44
  90.5 1.7 collective-permute-start.15
  92.2 2.2 %collective-permute-done.15 = f32[3,512]{1,0:T(4,128)S(1)} collective-permute-done((f32[3,512]{1,0:T(4,128)S(1)}, f32[3,512]{1,0:T(4,128)S(1)}, u32[]{:S(2)}, u32[]{:S(2)}) %collective-permute-start.15) | collective-permute-done | bytes 6176 | tf_op jit(solution)/shard_map/ppermute | solution.py:24
  94.4 1.4 collective-permute-start.16
  95.8 2.3 %collective-permute-done.16 = f32[3,512]{1,0:T(4,128)S(1)} collective-permute-done((f32[3,512]{1,0:T(4,128)S(1)}, f32[3,512]{1,0:T(4,128)S(1)}, u32[]{:S(2)}, u32[]{:S(2)}) %collective-permute-start.16) | collective-permute-done | bytes 6176 | tf_op jit(solution)/shard_map/ppermute | solution.py:24
  98.0 2.1 %collective-permute-start.17 = (f32[3,512]{1,0:T(4,128)S(1)}, f32[3,512]{1,0:T(4,128)S(1)}, u32[]{:S(2)}, u32[]{:S(2)}) collective-permute-start(f32[3,512]{1,0:T(4,128)S(1)} %add.208), channel_id=1, source_target_pairs={{0,16},{4,20},{8,24},{12,28},{16,0},{20,4},{24,8},{28,12},{1,17},{... | collective-permute-start | bytes 18440 | tf_op jit(solution)/shard_map/ppermute | solution.py:24
  101.0 1.6 collective-permute-done.17
  103.2 1.5 shard_map.71
  105.7 2.6 %collective-permute-done.19 = f16[128,512]{1,0:T(8,128)(2,1)S(1)} collective-permute-done((f16[128,512]{1,0:T(8,128)(2,1)S(1)}, f16[128,512]{1,0:T(8,128)(2,1)S(1)}, u32[]{:S(2)}, u32[]{:S(2)}) %collective-permute-start.19) | collective-permute-done | bytes 131104 | tf_op jit(solution)/shard_map/ppermute | solution.py:44
  108.3 1.1 pad_maximum_fusion.5
  109.4 1.4 collective-permute-start.23
  111.1 8.3 %collective-permute-done.20 = f16[256,512]{1,0:T(8,128)(2,1)S(1)} collective-permute-done((f16[256,512]{1,0:T(8,128)(2,1)S(1)}, f16[256,512]{1,0:T(8,128)(2,1)S(1)}, u32[]{:S(2)}, u32[]{:S(2)}) %collective-permute-start.20) | collective-permute-done | bytes 262176 | tf_op jit(solution)/shard_map/ppermute | solution.py:44
  119.6 1.4 collective-permute-start.21
  121.0 1.4 add_convert_fusion
  122.4 2.8 %copy-done.3 = bf16[3072,1024]{1,0:T(8,128)(2,1)S(1)} copy-done((bf16[3072,1024]{1,0:T(8,128)(2,1)S(1)}, bf16[3072,1024]{1,0:T(8,128)(2,1)}, u32[]{:S(2)}) %copy-start.3) | copy-done | bytes 6291480
  125.1 2.8 %copy-done.5 = bf16[3072,1024]{1,0:T(8,128)(2,1)S(1)} copy-done((bf16[3072,1024]{1,0:T(8,128)(2,1)S(1)}, bf16[3072,1024]{1,0:T(8,128)(2,1)}, u32[]{:S(2)}) %copy-start.5) | copy-done | bytes 6291480
  127.9 8.8 %shard_map.73 = (f32[1024,512]{1,0:T(8,128)S(1)}, f32[8,512]{1,0:T(8,128)S(1)}) custom-call(s32[8]{0:T(128)S(1)} %fusion.16.refs_0_, bf16[3072,1024]{1,0:T(8,128)(2,1)S(1)} %copy-done.3, bf16[3072,1024]{1,0:T(8,128)(2,1)S(1)} %copy-done.5, bf16[512,512]{1,0:T(8,128)(2,1)S(1)} %get-tuple-element.96.refs_3_, bf16[512,512]{1,0:T(8,128)(2,1)S(1)} %get-tuple-element.95.refs_4_), custom_call_target="tpu_custom_call" | custom-call | flops 6442450944 | bytes 12582912 | tf_op jit(solution)/shard_map/pallas_call | solution.py:181
  138.1 8.6 %shard_map.72 = (f32[1024,512]{1,0:T(8,128)S(1)}, f32[8,512]{1,0:T(8,128)S(1)}) custom-call(s32[8]{0:T(128)S(1)} %fusion.16.refs_0_, bf16[3072,1024]{1,0:T(8,128)(2,1)S(1)} %copy-done.3, bf16[3072,1024]{1,0:T(8,128)(2,1)S(1)} %copy-done.5, bf16[512,512]{1,0:T(8,128)(2,1)S(1)} %get-tuple-element.98.refs_3_, bf16[512,512]{1,0:T(8,128)(2,1)S(1)} %get-tuple-element.97.refs_4_), custom_call_target="tpu_custom_call" | custom-call | flops 6442450944 | bytes 12582912 | tf_op jit(solution)/shard_map/pallas_call | solution.py:181
  146.9 1.4 collective-permute-start.22
  149.2 2.8 %collective-permute-done.26 = f32[1,512]{1,0:T(1,128)S(1)} collective-permute-done((f32[1,512]{1,0:T(1,128)S(1)}, f32[1,512]{1,0:T(1,128)S(1)}, u32[]{:S(2)}, u32[]{:S(2)}) %collective-permute-start.26) | collective-permute-done | bytes 2080 | tf_op jit(solution)/shard_map/ppermute | solution.py:24
  152.0 7.0 %collective-permute-done.22 = f16[512,512]{1,0:T(8,128)(2,1)S(1)} collective-permute-done((f16[512,512]{1,0:T(8,128)(2,1)S(1)}, f16[512,512]{1,0:T(8,128)(2,1)S(1)}, u32[]{:S(2)}, u32[]{:S(2)}) %collective-permute-start.22) | collective-permute-done | bytes 524320 | tf_op jit(solution)/shard_map/ppermute | solution.py:44
  159.0 1.3 collective-permute-start.29
  160.7 1.9 %collective-permute-done.29 = f32[1,512]{1,0:T(1,128)S(1)} collective-permute-done((f32[1,512]{1,0:T(1,128)S(1)}, f32[1,512]{1,0:T(1,128)S(1)}, u32[]{:S(2)}, u32[]{:S(2)}) %collective-permute-start.29) | collective-permute-done | bytes 2080 | tf_op jit(solution)/shard_map/ppermute | solution.py:24
  163.1 2.6 %collective-permute-start.32 = (f16[128,512]{1,0:T(8,128)(2,1)S(1)}, f16[128,512]{1,0:T(8,128)(2,1)S(1)}, u32[]{:S(2)}, u32[]{:S(2)}) collective-permute-start(f16[128,512]{1,0:T(8,128)(2,1)S(1)} %slice_convert_fusion.9), channel_id=1, source_target_pairs={{0,16},{1,17},{2,18},{3,19},{4,20},{5,21},{6,22},{7,23},{8,24},{9,... | collective-permute-start | bytes 393224 | tf_op jit(solution)/shard_map/ppermute | solution.py:44
  165.6 3.3 %collective-permute-done.30 = f32[1,512]{1,0:T(1,128)S(1)} collective-permute-done((f32[1,512]{1,0:T(1,128)S(1)}, f32[1,512]{1,0:T(1,128)S(1)}, u32[]{:S(2)}, u32[]{:S(2)}) %collective-permute-start.30) | collective-permute-done | bytes 2080 | tf_op jit(solution)/shard_map/ppermute | solution.py:24
  169.1 3.0 %collective-permute-start.33 = (f16[128,512]{1,0:T(8,128)(2,1)S(1)}, f16[128,512]{1,0:T(8,128)(2,1)S(1)}, u32[]{:S(2)}, u32[]{:S(2)}) collective-permute-start(f16[128,512]{1,0:T(8,128)(2,1)S(1)} %slice_convert_fusion.8), channel_id=1, source_target_pairs={{0,16},{1,17},{2,18},{3,19},{4,20},{5,21},{6,22},{7,23},{8,24},{9,... | collective-permute-start | bytes 393224 | tf_op jit(solution)/shard_map/ppermute | solution.py:44
  172.1 1.5 collective-permute-done.31
  174.2 1.4 slice_divide_fusion.1
  175.6 1.1 collective-permute-done.33
  (134 shorter events, 17.7 us)
Async XLA Ops:
  1.7 10.4 %collective-permute-start = (bf16[128,512]{1,0:T(8,128)(2,1)S(1)}, bf16[128,512]{1,0:T(8,128)(2,1)S(1)}, u32[]{:S(2)}, u32[]{:S(2)}) collective-permute-start(bf16[128,512]{1,0:T(8,128)(2,1)S(1)} %get-tuple-element.76), channel_id=1, source_target_pairs={{0,16},{1,17},{2,18},{3,19},{4,20},{5,21},{6,22},{7,23},{8,24},{9,... | collective-permute-start | bytes 393224 | tf_op jit(solution)/shard_map/ppermute | solution.py:44
  12.1 10.4 %collective-permute-start.1 = (bf16[256,512]{1,0:T(8,128)(2,1)S(1)}, bf16[256,512]{1,0:T(8,128)(2,1)S(1)}, u32[]{:S(2)}, u32[]{:S(2)}) collective-permute-start(bf16[256,512]{1,0:T(8,128)(2,1)S(1)} %pad_maximum_fusion.10), channel_id=1, source_target_pairs={{0,8},{1,5},{2,10},{3,7},{4,12},{5,1},{6,14},{7,3},{8,0},{9,13},{1... | collective-permute-start | bytes 786440 | tf_op jit(solution)/shard_map/ppermute | solution.py:44
  12.9 10.2 %collective-permute-start.5 = (bf16[128,512]{1,0:T(8,128)(2,1)S(1)}, bf16[128,512]{1,0:T(8,128)(2,1)S(1)}, u32[]{:S(2)}, u32[]{:S(2)}) collective-permute-start(bf16[128,512]{1,0:T(8,128)(2,1)S(1)} %get-tuple-element.77), channel_id=1, source_target_pairs={{0,16},{1,17},{2,18},{3,19},{4,20},{5,21},{6,22},{7,23},{8,24},{9,... | collective-permute-start | bytes 393224 | tf_op jit(solution)/shard_map/ppermute | solution.py:44
  22.5 8.1 %copy-start.7 = (bf16[256,512]{1,0:T(8,128)(2,1)}, bf16[256,512]{1,0:T(8,128)(2,1)S(1)}, u32[]{:S(2)}) copy-start(bf16[256,512]{1,0:T(8,128)(2,1)S(1)} %collective-permute-done.1) | copy-start | bytes 786436
  22.5 9.2 %collective-permute-start.2 = (bf16[512,512]{1,0:T(8,128)(2,1)S(1)}, bf16[512,512]{1,0:T(8,128)(2,1)S(1)}, u32[]{:S(2)}, u32[]{:S(2)}) collective-permute-start(bf16[512,512]{1,0:T(8,128)(2,1)S(1)} %pad_maximum_fusion.2.refs_3_), channel_id=1, source_target_pairs={{0,4},{1,9},{2,6},{3,11},{4,0},{5,13},{6,2},{7,15},{8,12},{9,1},{1... | collective-permute-start | bytes 1572872 | tf_op jit(solution)/shard_map/ppermute | solution.py:44
  23.2 7.5 %collective-permute-start.6 = (bf16[256,512]{1,0:T(8,128)(2,1)S(1)}, bf16[256,512]{1,0:T(8,128)(2,1)S(1)}, u32[]{:S(2)}, u32[]{:S(2)}) collective-permute-start(bf16[256,512]{1,0:T(8,128)(2,1)S(1)} %pad_maximum_fusion.11), channel_id=1, source_target_pairs={{0,8},{1,5},{2,10},{3,7},{4,12},{5,1},{6,14},{7,3},{8,0},{9,13},{1... | collective-permute-start | bytes 786440 | tf_op jit(solution)/shard_map/ppermute | solution.py:44
  24.1 2.8 %copy-start = (bf16[3072,1024]{1,0:T(8,128)(2,1)S(1)}, bf16[3072,1024]{1,0:T(8,128)(2,1)}, u32[]{:S(2)}) copy-start(bf16[3072,1024]{1,0:T(8,128)(2,1)} %f_ref.1) | copy-start | bytes 18874372
  26.9 2.8 %copy-start.1 = (bf16[3072,1024]{1,0:T(8,128)(2,1)S(1)}, bf16[3072,1024]{1,0:T(8,128)(2,1)}, u32[]{:S(2)}) copy-start(bf16[3072,1024]{1,0:T(8,128)(2,1)} %c_ref.1) | copy-start | bytes 18874372
  29.7 0.9 copy-start.14
  30.6 11.2 %copy-start.2 = (bf16[3072,1024]{1,0:T(8,128)(2,1)}, bf16[3072,1024]{1,0:T(8,128)(2,1)S(1)}, u32[]{:S(2)}) copy-start(bf16[3072,1024]{1,0:T(8,128)(2,1)S(1)} %get-tuple-element.28.refs_1_) | copy-start | bytes 18874372
  30.6 11.2 %copy-start.4 = (bf16[3072,1024]{1,0:T(8,128)(2,1)}, bf16[3072,1024]{1,0:T(8,128)(2,1)S(1)}, u32[]{:S(2)}) copy-start(bf16[3072,1024]{1,0:T(8,128)(2,1)S(1)} %get-tuple-element.29.refs_2_) | copy-start | bytes 18874372
  30.7 11.1 %collective-permute-start.7 = (bf16[512,512]{1,0:T(8,128)(2,1)S(1)}, bf16[512,512]{1,0:T(8,128)(2,1)S(1)}, u32[]{:S(2)}, u32[]{:S(2)}) collective-permute-start(bf16[512,512]{1,0:T(8,128)(2,1)S(1)} %pad_maximum_fusion.3.refs_3_), channel_id=1, source_target_pairs={{0,4},{1,9},{2,6},{3,11},{4,0},{5,13},{6,2},{7,15},{8,12},{9,1},{1... | collective-permute-start | bytes 1572872 | tf_op jit(solution)/shard_map/ppermute | solution.py:44
  40.7 11.1 %collective-permute-start.3 = (f16[528,512]{1,0:T(8,128)(2,1)S(1)}, f16[528,512]{1,0:T(8,128)(2,1)S(1)}, u32[]{:S(2)}, u32[]{:S(2)}) collective-permute-start(f16[528,512]{1,0:T(8,128)(2,1)S(1)} %pad_maximum_fusion), channel_id=1, source_target_pairs={{0,4},{1,9},{2,6},{3,11},{4,0},{5,13},{6,2},{7,15},{8,12},{9,1},{1... | collective-permute-start | bytes 1622024 | tf_op jit(solution)/shard_map/ppermute | solution.py:44
  50.7 11.0 %collective-permute-start.8 = (f16[528,512]{1,0:T(8,128)(2,1)S(1)}, f16[528,512]{1,0:T(8,128)(2,1)S(1)}, u32[]{:S(2)}, u32[]{:S(2)}) collective-permute-start(f16[528,512]{1,0:T(8,128)(2,1)S(1)} %pad_maximum_fusion.1), channel_id=1, source_target_pairs={{0,4},{1,9},{2,6},{3,11},{4,0},{5,13},{6,2},{7,15},{8,12},{9,1},{1... | collective-permute-start | bytes 1622024 | tf_op jit(solution)/shard_map/ppermute | solution.py:44
  52.1 9.6 %collective-permute-start.4 = (f16[272,512]{1,0:T(8,128)(2,1)S(1)}, f16[272,512]{1,0:T(8,128)(2,1)S(1)}, u32[]{:S(2)}, u32[]{:S(2)}) collective-permute-start(f16[272,512]{1,0:T(8,128)(2,1)S(1)} %pad_maximum_fusion.8), channel_id=1, source_target_pairs={{0,8},{1,5},{2,10},{3,7},{4,12},{5,1},{6,14},{7,3},{8,0},{9,13},{1... | collective-permute-start | bytes 835592 | tf_op jit(solution)/shard_map/ppermute | solution.py:44
  61.8 13.0 %copy-start.6 = (f32[128,1024]{1,0:T(8,128)S(1)}, f32[128,1024]{1,0:T(8,128)}, u32[]{:S(2)}) copy-start(f32[128,1024]{1,0:T(8,128)} %param.7) | copy-start | bytes 1572868
  62.1 7.3 %collective-permute-start.10 = (f16[272,512]{1,0:T(8,128)(2,1)S(1)}, f16[272,512]{1,0:T(8,128)(2,1)S(1)}, u32[]{:S(2)}, u32[]{:S(2)}) collective-permute-start(f16[272,512]{1,0:T(8,128)(2,1)S(1)} %pad_maximum_fusion.9), channel_id=1, source_target_pairs={{0,8},{1,5},{2,10},{3,7},{4,12},{5,1},{6,14},{7,3},{8,0},{9,13},{1... | collective-permute-start | bytes 835592 | tf_op jit(solution)/shard_map/ppermute | solution.py:44
  62.7 12.2 %collective-permute-start.9 = (f16[144,512]{1,0:T(8,128)(2,1)S(1)}, f16[144,512]{1,0:T(8,128)(2,1)S(1)}, u32[]{:S(2)}, u32[]{:S(2)}) collective-permute-start(f16[144,512]{1,0:T(8,128)(2,1)S(1)} %pad_maximum_fusion.14), channel_id=1, source_target_pairs={{0,16},{1,17},{2,18},{3,19},{4,20},{5,21},{6,22},{7,23},{8,24},{9,... | collective-permute-start | bytes 442376 | tf_op jit(solution)/shard_map/ppermute | solution.py:44
  67.5 16.7 %copy-start.9 = (f32[1,512]{1,0:T(1,128)}, f32[1,512]{1,0:T(1,128)S(1)}, u32[]{:S(2)}) copy-start(f32[1,512]{1,0:T(1,128)S(1)} %get-tuple-element.94.refs_1_) | copy-start | bytes 6148
  74.9 9.4 %copy-start.10 = (f32[1,512]{1,0:T(1,128)}, f32[1,512]{1,0:T(1,128)S(1)}, u32[]{:S(2)}) copy-start(f32[1,512]{1,0:T(1,128)S(1)} %add_divide_fusion.1.refs_0_) | copy-start | bytes 6148
  75.0 8.9 %collective-permute-start.11 = (f16[128,512]{1,0:T(8,128)(2,1)S(1)}, f16[128,512]{1,0:T(8,128)(2,1)S(1)}, u32[]{:S(2)}, u32[]{:S(2)}) collective-permute-start(f16[128,512]{1,0:T(8,128)(2,1)S(1)} %get-tuple-element.64), channel_id=1, source_target_pairs={{0,16},{1,17},{2,18},{3,19},{4,20},{5,21},{6,22},{7,23},{8,24},{9,... | collective-permute-start | bytes 393224 | tf_op jit(solution)/shard_map/ppermute | solution.py:44
  75.9 8.0 %collective-permute-start.12 = (f16[144,512]{1,0:T(8,128)(2,1)S(1)}, f16[144,512]{1,0:T(8,128)(2,1)S(1)}, u32[]{:S(2)}, u32[]{:S(2)}) collective-permute-start(f16[144,512]{1,0:T(8,128)(2,1)S(1)} %pad_maximum_fusion.15), channel_id=1, source_target_pairs={{0,16},{1,17},{2,18},{3,19},{4,20},{5,21},{6,22},{7,23},{8,24},{9,... | collective-permute-start | bytes 442376 | tf_op jit(solution)/shard_map/ppermute | solution.py:44
  78.3 24.9 %copy-start.11 = (f32[1,512]{1,0:T(1,128)}, f32[1,512]{1,0:T(1,128)S(1)}, u32[]{:S(2)}) copy-start(f32[1,512]{1,0:T(1,128)S(1)} %get-tuple-element.92.refs_3_) | copy-start | bytes 6148
  83.9 19.2 %copy-start.12 = (f32[1,512]{1,0:T(1,128)}, f32[1,512]{1,0:T(1,128)S(1)}, u32[]{:S(2)}) copy-start(f32[1,512]{1,0:T(1,128)S(1)} %add_divide_fusion.refs_2_) | copy-start | bytes 6148
  84.3 1.2 collective-permute-start.13
  85.5 4.9 %collective-permute-start.14 = (f32[3,512]{1,0:T(4,128)S(1)}, f32[3,512]{1,0:T(4,128)S(1)}, u32[]{:S(2)}, u32[]{:S(2)}) collective-permute-start(f32[3,512]{1,0:T(4,128)S(1)} %fusion.17), channel_id=1, source_target_pairs={{0,2},{1,3},{2,0},{3,1},{4,6},{5,7},{6,4},{7,5},{8,10},{9,11},{10,... | collective-permute-start | bytes 18440 | tf_op jit(solution)/shard_map/ppermute | solution.py:24
  87.9 20.4 %collective-permute-start.18 = (f16[256,512]{1,0:T(8,128)(2,1)}, f16[256,512]{1,0:T(8,128)(2,1)}, u32[]{:S(2)}, u32[]{:S(2)}) collective-permute-start(f16[256,512]{1,0:T(8,128)(2,1)} %pad_maximum_fusion.12), channel_id=1, source_target_pairs={{0,8},{1,5},{2,10},{3,7},{4,12},{5,1},{6,14},{7,3},{8,0},{9,13},{1... | collective-permute-start | bytes 786440 | tf_op jit(solution)/shard_map/ppermute | solution.py:44
  90.5 3.9 %collective-permute-start.15 = (f32[3,512]{1,0:T(4,128)S(1)}, f32[3,512]{1,0:T(4,128)S(1)}, u32[]{:S(2)}, u32[]{:S(2)}) collective-permute-start(f32[3,512]{1,0:T(4,128)S(1)} %fusion.24), channel_id=1, source_target_pairs={{0,4},{4,0},{8,12},{12,8},{16,20},{20,16},{24,28},{28,24},{1,5},{5... | collective-permute-start | bytes 18440 | tf_op jit(solution)/shard_map/ppermute | solution.py:24
  94.4 3.7 %collective-permute-start.16 = (f32[3,512]{1,0:T(4,128)S(1)}, f32[3,512]{1,0:T(4,128)S(1)}, u32[]{:S(2)}, u32[]{:S(2)}) collective-permute-start(f32[3,512]{1,0:T(4,128)S(1)} %add.207), channel_id=1, source_target_pairs={{0,8},{4,12},{8,0},{12,4},{16,24},{20,28},{24,16},{28,20},{1,9},{5... | collective-permute-start | bytes 18440 | tf_op jit(solution)/shard_map/ppermute | solution.py:24
  98.0 4.5 %collective-permute-start.17 = (f32[3,512]{1,0:T(4,128)S(1)}, f32[3,512]{1,0:T(4,128)S(1)}, u32[]{:S(2)}, u32[]{:S(2)}) collective-permute-start(f32[3,512]{1,0:T(4,128)S(1)} %add.208), channel_id=1, source_target_pairs={{0,16},{4,20},{8,24},{12,28},{16,0},{20,4},{24,8},{28,12},{1,17},{... | collective-permute-start | bytes 18440 | tf_op jit(solution)/shard_map/ppermute | solution.py:24
  100.1 8.2 %collective-permute-start.19 = (f16[128,512]{1,0:T(8,128)(2,1)S(1)}, f16[128,512]{1,0:T(8,128)(2,1)S(1)}, u32[]{:S(2)}, u32[]{:S(2)}) collective-permute-start(f16[128,512]{1,0:T(8,128)(2,1)S(1)} %get-tuple-element.62), channel_id=1, source_target_pairs={{0,16},{1,17},{2,18},{3,19},{4,20},{5,21},{6,22},{7,23},{8,24},{9,... | collective-permute-start | bytes 393224 | tf_op jit(solution)/shard_map/ppermute | solution.py:44
  104.7 16.2 %copy-start.8 = (bf16[256,512]{1,0:T(8,128)(2,1)S(1)}, bf16[256,512]{1,0:T(8,128)(2,1)}, u32[]{:S(2)}) copy-start(bf16[256,512]{1,0:T(8,128)(2,1)} %copy-done.7) | copy-start | bytes 786436
  109.4 11.6 %collective-permute-start.23 = (f16[512,512]{1,0:T(8,128)(2,1)S(1)}, f16[512,512]{1,0:T(8,128)(2,1)S(1)}, u32[]{:S(2)}, u32[]{:S(2)}) collective-permute-start(f16[512,512]{1,0:T(8,128)(2,1)S(1)} %pad_maximum_fusion.5), channel_id=1, source_target_pairs={{0,4},{1,9},{2,6},{3,11},{4,0},{5,13},{6,2},{7,15},{8,12},{9,1},{1... | collective-permute-start | bytes 1572872 | tf_op jit(solution)/shard_map/ppermute | solution.py:44
  110.9 8.6 %collective-permute-start.20 = (f16[256,512]{1,0:T(8,128)(2,1)S(1)}, f16[256,512]{1,0:T(8,128)(2,1)S(1)}, u32[]{:S(2)}, u32[]{:S(2)}) collective-permute-start(f16[256,512]{1,0:T(8,128)(2,1)S(1)} %pad_maximum_fusion.13), channel_id=1, source_target_pairs={{0,8},{1,5},{2,10},{3,7},{4,12},{5,1},{6,14},{7,3},{8,0},{9,13},{1... | collective-permute-start | bytes 786440 | tf_op jit(solution)/shard_map/ppermute | solution.py:44
  119.6 18.1 %collective-permute-start.21 = (f16[512,512]{1,0:T(8,128)(2,1)S(1)}, f16[512,512]{1,0:T(8,128)(2,1)S(1)}, u32[]{:S(2)}, u32[]{:S(2)}) collective-permute-start(f16[512,512]{1,0:T(8,128)(2,1)S(1)} %pad_maximum_fusion.4), channel_id=1, source_target_pairs={{0,4},{1,9},{2,6},{3,11},{4,0},{5,13},{6,2},{7,15},{8,12},{9,1},{1... | collective-permute-start | bytes 1572872 | tf_op jit(solution)/shard_map/ppermute | solution.py:44
  122.4 2.8 %copy-start.3 = (bf16[3072,1024]{1,0:T(8,128)(2,1)S(1)}, bf16[3072,1024]{1,0:T(8,128)(2,1)}, u32[]{:S(2)}) copy-start(bf16[3072,1024]{1,0:T(8,128)(2,1)} %copy-done.2) | copy-start | bytes 18874372
  125.1 2.8 %copy-start.5 = (bf16[3072,1024]{1,0:T(8,128)(2,1)S(1)}, bf16[3072,1024]{1,0:T(8,128)(2,1)}, u32[]{:S(2)}) copy-start(bf16[3072,1024]{1,0:T(8,128)(2,1)} %copy-done.4) | copy-start | bytes 18874372
  136.8 11.5 %collective-permute-start.24 = (f16[512,512]{1,0:T(8,128)(2,1)S(1)}, f16[512,512]{1,0:T(8,128)(2,1)S(1)}, u32[]{:S(2)}, u32[]{:S(2)}) collective-permute-start(f16[512,512]{1,0:T(8,128)(2,1)S(1)} %slice_convert_fusion), channel_id=1, source_target_pairs={{0,4},{1,9},{2,6},{3,11},{4,0},{5,13},{6,2},{7,15},{8,12},{9,1},{1... | collective-permute-start | bytes 1572872 | tf_op jit(solution)/shard_map/ppermute | solution.py:44
  146.7 1.5 collective-permute-start.25
  146.9 12.1 %collective-permute-start.22 = (f16[512,512]{1,0:T(8,128)(2,1)S(1)}, f16[512,512]{1,0:T(8,128)(2,1)S(1)}, u32[]{:S(2)}, u32[]{:S(2)}) collective-permute-start(f16[512,512]{1,0:T(8,128)(2,1)S(1)} %slice_convert_fusion.1), channel_id=1, source_target_pairs={{0,4},{1,9},{2,6},{3,11},{4,0},{5,13},{6,2},{7,15},{8,12},{9,1},{1... | collective-permute-start | bytes 1572872 | tf_op jit(solution)/shard_map/ppermute | solution.py:44
  148.3 3.7 %collective-permute-start.26 = (f32[1,512]{1,0:T(1,128)S(1)}, f32[1,512]{1,0:T(1,128)S(1)}, u32[]{:S(2)}, u32[]{:S(2)}) collective-permute-start(f32[1,512]{1,0:T(1,128)S(1)} %add.219), channel_id=1, source_target_pairs={{0,2},{1,3},{2,0},{3,1},{4,6},{5,7},{6,4},{7,5},{8,10},{9,11},{10,... | collective-permute-start | bytes 6152 | tf_op jit(solution)/shard_map/ppermute | solution.py:24
  149.1 13.5 %collective-permute-start.28 = (f16[256,512]{1,0:T(8,128)(2,1)S(1)}, f16[256,512]{1,0:T(8,128)(2,1)S(1)}, u32[]{:S(2)}, u32[]{:S(2)}) collective-permute-start(f16[256,512]{1,0:T(8,128)(2,1)S(1)} %slice_convert_fusion.4), channel_id=1, source_target_pairs={{0,8},{1,5},{2,10},{3,7},{4,12},{5,1},{6,14},{7,3},{8,0},{9,13},{1... | collective-permute-start | bytes 786440 | tf_op jit(solution)/shard_map/ppermute | solution.py:44
  159.0 3.6 %collective-permute-start.29 = (f32[1,512]{1,0:T(1,128)S(1)}, f32[1,512]{1,0:T(1,128)S(1)}, u32[]{:S(2)}, u32[]{:S(2)}) collective-permute-start(f32[1,512]{1,0:T(1,128)S(1)} %add.220), channel_id=1, source_target_pairs={{0,4},{4,0},{8,12},{12,8},{16,20},{20,16},{24,28},{28,24},{1,5},{5... | collective-permute-start | bytes 6152 | tf_op jit(solution)/shard_map/ppermute | solution.py:24
  160.5 8.4 %collective-permute-start.27 = (f16[256,512]{1,0:T(8,128)(2,1)S(1)}, f16[256,512]{1,0:T(8,128)(2,1)S(1)}, u32[]{:S(2)}, u32[]{:S(2)}) collective-permute-start(f16[256,512]{1,0:T(8,128)(2,1)S(1)} %slice_convert_fusion.5), channel_id=1, source_target_pairs={{0,8},{1,5},{2,10},{3,7},{4,12},{5,1},{6,14},{7,3},{8,0},{9,13},{1... | collective-permute-start | bytes 786440 | tf_op jit(solution)/shard_map/ppermute | solution.py:44
  162.7 6.2 %collective-permute-start.30 = (f32[1,512]{1,0:T(1,128)S(1)}, f32[1,512]{1,0:T(1,128)S(1)}, u32[]{:S(2)}, u32[]{:S(2)}) collective-permute-start(f32[1,512]{1,0:T(1,128)S(1)} %add.223), channel_id=1, source_target_pairs={{0,8},{4,12},{8,0},{12,4},{16,24},{20,28},{24,16},{28,20},{1,9},{5... | collective-permute-start | bytes 6152 | tf_op jit(solution)/shard_map/ppermute | solution.py:24
  163.1 12.5 %collective-permute-start.32 = (f16[128,512]{1,0:T(8,128)(2,1)S(1)}, f16[128,512]{1,0:T(8,128)(2,1)S(1)}, u32[]{:S(2)}, u32[]{:S(2)}) collective-permute-start(f16[128,512]{1,0:T(8,128)(2,1)S(1)} %slice_convert_fusion.9), channel_id=1, source_target_pairs={{0,16},{1,17},{2,18},{3,19},{4,20},{5,21},{6,22},{7,23},{8,24},{9,... | collective-permute-start | bytes 393224 | tf_op jit(solution)/shard_map/ppermute | solution.py:44
  168.9 4.6 %collective-permute-start.31 = (f32[1,512]{1,0:T(1,128)S(1)}, f32[1,512]{1,0:T(1,128)S(1)}, u32[]{:S(2)}, u32[]{:S(2)}) collective-permute-start(f32[1,512]{1,0:T(1,128)S(1)} %add.224), channel_id=1, source_target_pairs={{0,16},{4,20},{8,24},{12,28},{16,0},{20,4},{24,8},{28,12},{1,17},{... | collective-permute-start | bytes 6152 | tf_op jit(solution)/shard_map/ppermute | solution.py:24
  169.1 7.6 %collective-permute-start.33 = (f16[128,512]{1,0:T(8,128)(2,1)S(1)}, f16[128,512]{1,0:T(8,128)(2,1)S(1)}, u32[]{:S(2)}, u32[]{:S(2)}) collective-permute-start(f16[128,512]{1,0:T(8,128)(2,1)S(1)} %slice_convert_fusion.8), channel_id=1, source_target_pairs={{0,16},{1,17},{2,18},{3,19},{4,20},{5,21},{6,22},{7,23},{8,24},{9,... | collective-permute-start | bytes 393224 | tf_op jit(solution)/shard_map/ppermute | solution.py:44
  (1 other events, 0.9 us)
